TPU v7x, 128 devices: a whole 4x4x4 slice. The times are simulated.
128 devices in a mesh: patch: 16 (over y, x), head: 8 (over z, core).
Axes of the slice: x: 4, y: 4, z: 4, core: 2. Of those that a mesh axis runs over, the one named last changes fastest.
Arguments:
- hidden: bfloat16 [16384, 3072], P('patch', 'head'), may hold values from -6 to 6
- key_cache: bfloat16 [16384, 3072], P('patch', 'head'), may hold values from -600 to 600
- value_cache: bfloat16 [16384, 3072], P('patch', 'head'), may hold values from -6 to 6
- block_order: int32 [16, 8], P('patch'), may hold values from 0 to 7, each once within a row
- refresh_counts: int32 [16], P('patch'), may hold values from 1 to 4, 32 in all
- modulation: float32 [3, 3072], replicated, may hold values from -4 to 4
- query_gain: float32 [128], replicated, may hold values from 0.25 to 1.75
- key_gain: float32 [128], replicated, may hold values from 2 to 4
- w_qkv: bfloat16 [3072, 3, 3072], P(None, None, 'head'), may hold values from -0.109375 to 0.109375
- w_mlp: bfloat16 [3072, 6144], P(None, 'head'), may hold values from -0.109375 to 0.109375
- w_out_attn: bfloat16 [3072, 3072], P('head'), may hold values from -0.0625 to 0.0625
- w_out_mlp: bfloat16 [6144, 3072], P('head'), may hold values from -0.0625 to 0.0625
Outputs:
- refreshed_out: bfloat16 [8192, 3072], P('patch', 'head')
Inputs may be any that keep to these rules, and one draw needn't show every extreme that they name: `block_order`: each row holds every block number of a shard once. `refresh_counts`: the counts of all shards sum to exactly 2 times the number of patch shards, and some shard has 4.
All inputs are finite; a program needn't handle non-finite values.
Results may differ from a plain program's by a relative error of at most 0.025.
Values may be sent and summed in bfloat16 or wider, within the bound.
No kernel may reach another device: no remote copies, remote signals or barrier semaphores. Data moves between devices by JAX's collectives and lax.ppermute only.
A program may use at most 192 MiB of HBM per device.

v0:
```python
import jax
import jax.numpy as jnp
from jax import lax
from jax.sharding import PartitionSpec as P

HD = 128
BLOCK = 128
RMAX = 4


neg_large = -1e30


def layer_norm_mod(token_rows, modulation):
    values = token_rows.astype(jnp.float32)
    center = values - jnp.mean(values, axis=-1, keepdims=True)
    spread = jnp.mean(center * center, axis=-1, keepdims=True)
    normed = center * lax.rsqrt(spread + 1e-06)
    return (normed * (1.0 + modulation[1]) + modulation[0]).astype(jnp.bfloat16)


def rms_scale(values, gain):
    scaled = values * lax.rsqrt(jnp.mean(values * values, axis=-1, keepdims=True) + 1e-06) * gain
    return scaled.astype(jnp.bfloat16)


def attend_block(queries, key_heads, value_heads, running):
    acc_num, acc_top, acc_total = running
    scores = jnp.einsum(
        "hqd,khd->hqk", queries, key_heads, preferred_element_type=jnp.float32
    ) * queries.shape[-1] ** (-0.5)
    new_top = jnp.maximum(acc_top, jnp.max(scores, axis=-1))
    weights = jnp.exp(scores - new_top[..., None])
    factor = jnp.exp(acc_top - new_top)
    acc_total = acc_total * factor + jnp.sum(weights, axis=-1)
    acc_num = acc_num * factor[..., None] + jnp.einsum(
        "hqk,khd->hqd",
        weights.astype(jnp.bfloat16),
        value_heads,
        preferred_element_type=jnp.float32,
    )
    return (acc_num, new_top, acc_total)


def attend_keys(queries, key_rows, value_rows, running):
    head_count, head_width = (queries.shape[0], queries.shape[2])
    length = key_rows.shape[0]
    key_heads = key_rows.reshape(length, head_count, head_width)
    value_heads = value_rows.reshape(length, head_count, head_width)
    sub_blocks = length // 2048

    def advance(state_now, paired):
        return (attend_block(queries, paired[0], paired[1], state_now), None)

    running, _ = lax.scan(
        advance,
        running,
        (
            key_heads.reshape(sub_blocks, 2048, head_count, head_width),
            value_heads.reshape(sub_blocks, 2048, head_count, head_width),
        ),
    )
    return running


def empty_state(head_count, query_count, head_width):
    return (
        jnp.zeros((head_count, query_count, head_width), jnp.float32),
        jnp.full((head_count, query_count), neg_large, jnp.float32),
        jnp.zeros((head_count, query_count), jnp.float32),
    )


def body(
    hidden,
    key_cache,
    value_cache,
    block_order,
    refresh_counts,
    modulation,
    query_gain,
    key_gain,
    w_qkv,
    w_mlp,
    w_out_attn,
    w_out_mlp,
):
    local_cols = hidden.shape[1]
    head_cols = key_cache.shape[1]
    heads_here = head_cols // HD
    num_blocks = hidden.shape[0] // BLOCK
    chosen = block_order[0, :RMAX]
    count_here = refresh_counts[0]
    slot_live = jnp.arange(RMAX) < count_here
    row_live = jnp.repeat(slot_live, BLOCK)
    work_rows = hidden.reshape(num_blocks, BLOCK, local_cols)[chosen].reshape(
        RMAX * BLOCK, local_cols
    )
    full_rows = lax.all_gather(work_rows, "head", axis=1, tiled=True)
    modded = layer_norm_mod(full_rows, modulation)
    projected = jnp.dot(
        modded, w_qkv.reshape(w_qkv.shape[0], 3 * head_cols), preferred_element_type=jnp.float32
    )
    query_new = rms_scale(projected[:, :head_cols].reshape(-1, heads_here, HD), query_gain)
    key_new = rms_scale(
        projected[:, head_cols : 2 * head_cols].reshape(-1, heads_here, HD), key_gain
    )
    value_new = projected[:, 2 * head_cols :].astype(jnp.bfloat16)
    hidden_mlp = jax.nn.gelu(
        jnp.dot(modded, w_mlp, preferred_element_type=jnp.float32), approximate=True
    ).astype(jnp.bfloat16)
    key_slots = key_new.reshape(RMAX, BLOCK, head_cols)
    value_slots = value_new.reshape(RMAX, BLOCK, head_cols)
    key_blocks = key_cache.reshape(num_blocks, BLOCK, head_cols)
    value_blocks = value_cache.reshape(num_blocks, BLOCK, head_cols)
    keep_key = jnp.where(slot_live[:, None, None], key_slots, key_blocks[chosen])
    keep_value = jnp.where(slot_live[:, None, None], value_slots, value_blocks[chosen])
    key_patched = key_blocks.at[chosen].set(keep_key).reshape(-1, head_cols)
    value_patched = value_blocks.at[chosen].set(keep_value).reshape(-1, head_cols)
    work_count = work_rows.shape[0]
    query_heads = jnp.transpose(query_new, (1, 0, 2))
    acc_num, acc_top, acc_total = attend_keys(
        query_heads,
        lax.all_gather(key_patched, "patch", axis=0, tiled=True),
        lax.all_gather(value_patched, "patch", axis=0, tiled=True),
        empty_state(heads_here, work_count, HD),
    )
    attn_out = acc_num / acc_total[..., None]
    attn_rows = jnp.transpose(attn_out, (1, 0, 2)).reshape(-1, head_cols).astype(jnp.bfloat16)
    branch_sum = jnp.dot(attn_rows, w_out_attn, preferred_element_type=jnp.float32) + jnp.dot(
        hidden_mlp, w_out_mlp, preferred_element_type=jnp.float32
    )
    summed = lax.psum_scatter(
        branch_sum.astype(jnp.bfloat16), "head", scatter_dimension=1, tiled=True
    ).astype(jnp.float32)
    gate_cols = lax.dynamic_slice_in_dim(
        modulation[2], lax.axis_index("head") * local_cols, local_cols
    )
    result = (work_rows.astype(jnp.float32) + gate_cols * summed).astype(jnp.bfloat16)
    return jnp.where(row_live[:, None], result, jnp.zeros((), jnp.bfloat16))


def solution(mesh):
    in_specs = (
        P("patch", "head"),
        P("patch", "head"),
        P("patch", "head"),
        P("patch", None),
        P("patch"),
        P(),
        P(),
        P(),
        P(None, None, "head"),
        P(None, "head"),
        P("head", None),
        P("head", None),
    )
    out_specs = P("patch", "head")
    return jax.shard_map(body, mesh=mesh, in_specs=in_specs, out_specs=out_specs, check_vma=False)
```

profile of v0, /device:TPU:0, one launch (start us, length us, event | category | flops | bytes accessed | tf_op | source)
XLA Modules:
  0.0 516.2 jit_solution(12558271862673758257)
XLA Ops:
  6.5 1.3 copy.72
  7.8 2.1 copy.73
  10.6 2.5 gather_fusion
  13.2 10.3 %copy.40 = bf16[3072,3,384]{0,2,1:T(8,128)(2,1)} copy(bf16[3072,3,384]{2,0,1:T(8,128)(2,1)} %param.22) | data formatting | bytes 14155776 | tf_op args[8]
  24.1 2.5 gather_fusion.2
  27.8 1.6 fusion.58
  29.4 14.3 %all-gather.4.cloned.1.call-done = bf16[512,3072]{1,0:T(8,128)(2,1)} async-done(((bf16[512,384]{1,0:T(8,128)(2,1)}), bf16[512,3072]{1,0:T(8,128)(2,1)}) %all-gather.4.cloned.1.call-update) | async-done | bytes 3145744 | tf_op jit(solution)/shard_map/all_gather | solution.py:99
  43.7 2.5 convert_reduce_fusion
  46.2 2.8 fusion.23
  49.1 7.6 %fusion.51 = f32[512,1152]{1,0:T(8,128)S(1)} fusion(bf16[3072,1152]{0,1:T(8,128)(2,1)} %bitcast.88, bf16[512,3072]{1,0:T(8,128)(2,1)S(1)} %copy-done.1, f32[3072]{0:T(1024)S(1)} %bitcast.104, f32[3072]{0:T(1024)S(1)} %bitcast.107, f32[512]{0:T(512)S(1)} %add_rsqrt_fusion.2, f32[512]{0:T(512)S(1)} %broadcast_multiply_fusion), kind=kOutput, calls=%fused_computation.78 | convolution fusion | flops 3633315840 | bytes 12611584 | tf_op jit(solution)/shard_map/dot_general | solution.py:101
  56.7 1.5 fusion.57
  59.1 2.3 copy.41
  61.4 1.2 reduce_sum.47
  62.6 1.0 mul.132
  63.6 2.3 mul.133
  65.9 2.3 copy.42
  68.1 2.9 broadcast_select_fusion
  71.0 2.5 scatter_fusion.1
  73.5 2.3 copy.45
  75.9 1.6 scatter_fusion
  77.6 1.2 copy.43
  79.0 2.3 copy.44
  81.4 1.2 multiply_reduce_fusion
  82.6 2.0 fusion.42
  84.6 1.2 copy.47
  85.9 14.3 %fusion.35 = f32[512,3072]{1,0:T(8,128)} fusion(bf16[768,3072]{1,0:T(8,128)(2,1)} %param.25, bf16[3072,768]{1,0:T(8,128)(2,1)} %param.23, bf16[512,3072]{1,0:T(8,128)(2,1)} %all-gather.4.cloned.1.call-done, f32[3072]{0:T(1024)} %bitcast.105, f32[3072]{0:T(1024)} %bitcast.106, f32[512]{0:T(512)S(1)} %copy-done.12, f32[512]{0:T(512)S(1)} %copy-done.8), kind=kOutput, calls=%fused_computation.45 | convolution fusion | flops 4844814336 | bytes 18903040 | tf_op jit(solution)/shard_map/dot_general | solution.py:130
  100.2 65.6 %all-gather.8.cloned.1.call-done = bf16[16384,384]{0,1:T(8,128)(2,1)} async-done(((bf16[1024,384]{0,1:T(8,128)(2,1)}), bf16[16384,384]{0,1:T(8,128)(2,1)}) %all-gather.8.cloned.1.call-update) | async-done | bytes 12582928 | tf_op jit(solution)/shard_map/all_gather | solution.py:125
  165.8 14.7 %copy.54 = bf16[48,8,8,2048]{3,2,1,0:T(8,128)(2,1)} copy(bf16[48,8,8,2048]{3,1,2,0:T(8,128)(2,1)} %bitcast.85) | data formatting | bytes 25165824
  180.4 17.0 %copy.48 = bf16[8,2048,3,128]{3,1,2,0:T(8,128)(2,1)} copy(bf16[8,2048,3,128]{1,0,3,2:T(8,128)(2,1)} %bitcast.83) | data formatting | bytes 25165824
  197.4 60.1 %all-gather.6.cloned.1.call-done = bf16[16384,384]{0,1:T(8,128)(2,1)} async-done(((bf16[1024,384]{0,1:T(8,128)(2,1)}), bf16[16384,384]{0,1:T(8,128)(2,1)}) %all-gather.6.cloned.1.call-update) | async-done | bytes 12582928 | tf_op jit(solution)/shard_map/all_gather | solution.py:124
  257.6 14.6 %copy.53 = bf16[48,8,8,2048]{3,2,1,0:T(8,128)(2,1)} copy(bf16[48,8,8,2048]{3,1,2,0:T(8,128)(2,1)} %bitcast.86) | data formatting | bytes 25165824
  272.1 17.5 %copy.46 = bf16[8,2048,3,128]{3,1,2,0:T(8,128)(2,1)} copy(bf16[8,2048,3,128]{1,0,3,2:T(8,128)(2,1)} %bitcast.84) | data formatting | bytes 25165824
  289.6 168.6 %while.15 = (s32[]{:T(128)}, f32[3,512,128]{2,1,0:T(8,128)S(1)}, f32[3,512]{1,0:T(4,128)S(1)}, f32[3,512]{1,0:T(4,128)}, bf16[8,2048,3,128]{3,1,2,0:T(8,128)(2,1...) while((s32[]{:T(128)}, f32[3,512,128]{2,1,0:T(8,128)S(1)}, ...), condition=%wide.region_9.10_spmd.clone, body=%wide.region_6.9_spmd.clone.sunk | while | flops 1636376064 | bytes 43009184 | solution.py:55
  289.6 7.8 %bitcast_reduce_fusion.2 = (f32[3,512]{1,0:T(4,128)S(1)}, f32[3,2048,512]{2,1,0:T(8,128)}) fusion(bf16[3,512,128]{2,1,0:T(8,128)(2,1)S(1)} %get-tuple-element.190, bf16[8,2048,3,128]{3,1,2,0:T(8,128)(2,1)} %get-tuple-element.189, s32[]{:T(128)} %get-tuple-element.176), kind=kOutput, calls=%fused_computation.6.clone.1 | convolution fusion | flops 811596288 | bytes 14555648 | tf_op jit(solution)/shard_map/while/body/eval_jaxpr/hqd,khd->hqk/dot_general | solution.py:29
  297.5 6.6 %fusion.74 = f32[3,512]{1,0:T(4,128)S(1)} fusion(f32[3,2048,512]{2,1,0:T(8,128)} %get-tuple-element.163, f32[3,512]{1,0:T(4,128)S(1)} %select_maximum_fusion.2), kind=kLoop, calls=%fused_computation.8.clone.1 | loop fusion | flops 9435648 | bytes 12595200 | tf_op jit(solution)/shard_map/while/body/eval_jaxpr/reduce_sum | solution.py:35
  304.1 6.6 %fusion.76 = f32[3,512,128]{2,1,0:T(8,128)S(1)} fusion(bf16[8,2048,3,128]{3,1,2,0:T(8,128)(2,1)} %get-tuple-element.191, s32[]{:T(128)} %get-tuple-element.176, f32[3,2048,512]{2,1,0:T(8,128)} %get-tuple-element.163, f32[3,512]{1,0:T(4,128)S(1)} %select_maximum_fusion.2, f32[3,512,128]{2,1,0:T(8,128)S(1)} %get-tuple-element.177, ...), kind=kOutput, calls=%fused_computation.18.clone.1 | convolution fusion | flops 815333376 | bytes 15741441 | tf_op jit(solution)/shard_map/while/body/eval_jaxpr/hqk,khd->hqd/dot_general | solution.py:36
  310.7 7.8 %bitcast_reduce_fusion.2 = (f32[3,512]{1,0:T(4,128)S(1)}, f32[3,2048,512]{2,1,0:T(8,128)}) fusion(bf16[3,512,128]{2,1,0:T(8,128)(2,1)S(1)} %get-tuple-element.190, bf16[8,2048,3,128]{3,1,2,0:T(8,128)(2,1)} %get-tuple-element.189, s32[]{:T(128)} %get-tuple-element.176), kind=kOutput, calls=%fused_computation.6.clone.1 | convolution fusion | flops 811596288 | bytes 14555648 | tf_op jit(solution)/shard_map/while/body/eval_jaxpr/hqd,khd->hqk/dot_general | solution.py:29
  318.5 6.6 %fusion.74 = f32[3,512]{1,0:T(4,128)S(1)} fusion(f32[3,2048,512]{2,1,0:T(8,128)} %get-tuple-element.163, f32[3,512]{1,0:T(4,128)S(1)} %select_maximum_fusion.2), kind=kLoop, calls=%fused_computation.8.clone.1 | loop fusion | flops 9435648 | bytes 12595200 | tf_op jit(solution)/shard_map/while/body/eval_jaxpr/reduce_sum | solution.py:35
  325.2 6.6 %fusion.76 = f32[3,512,128]{2,1,0:T(8,128)S(1)} fusion(bf16[8,2048,3,128]{3,1,2,0:T(8,128)(2,1)} %get-tuple-element.191, s32[]{:T(128)} %get-tuple-element.176, f32[3,2048,512]{2,1,0:T(8,128)} %get-tuple-element.163, f32[3,512]{1,0:T(4,128)S(1)} %select_maximum_fusion.2, f32[3,512,128]{2,1,0:T(8,128)S(1)} %get-tuple-element.177, ...), kind=kOutput, calls=%fused_computation.18.clone.1 | convolution fusion | flops 815333376 | bytes 15741441 | tf_op jit(solution)/shard_map/while/body/eval_jaxpr/hqk,khd->hqd/dot_general | solution.py:36
  331.8 7.8 %bitcast_reduce_fusion.2 = (f32[3,512]{1,0:T(4,128)S(1)}, f32[3,2048,512]{2,1,0:T(8,128)}) fusion(bf16[3,512,128]{2,1,0:T(8,128)(2,1)S(1)} %get-tuple-element.190, bf16[8,2048,3,128]{3,1,2,0:T(8,128)(2,1)} %get-tuple-element.189, s32[]{:T(128)} %get-tuple-element.176), kind=kOutput, calls=%fused_computation.6.clone.1 | convolution fusion | flops 811596288 | bytes 14555648 | tf_op jit(solution)/shard_map/while/body/eval_jaxpr/hqd,khd->hqk/dot_general | solution.py:29
  339.6 6.6 %fusion.74 = f32[3,512]{1,0:T(4,128)S(1)} fusion(f32[3,2048,512]{2,1,0:T(8,128)} %get-tuple-element.163, f32[3,512]{1,0:T(4,128)S(1)} %select_maximum_fusion.2), kind=kLoop, calls=%fused_computation.8.clone.1 | loop fusion | flops 9435648 | bytes 12595200 | tf_op jit(solution)/shard_map/while/body/eval_jaxpr/reduce_sum | solution.py:35
  346.3 6.6 %fusion.76 = f32[3,512,128]{2,1,0:T(8,128)S(1)} fusion(bf16[8,2048,3,128]{3,1,2,0:T(8,128)(2,1)} %get-tuple-element.191, s32[]{:T(128)} %get-tuple-element.176, f32[3,2048,512]{2,1,0:T(8,128)} %get-tuple-element.163, f32[3,512]{1,0:T(4,128)S(1)} %select_maximum_fusion.2, f32[3,512,128]{2,1,0:T(8,128)S(1)} %get-tuple-element.177, ...), kind=kOutput, calls=%fused_computation.18.clone.1 | convolution fusion | flops 815333376 | bytes 15741441 | tf_op jit(solution)/shard_map/while/body/eval_jaxpr/hqk,khd->hqd/dot_general | solution.py:36
  352.9 7.8 %bitcast_reduce_fusion.2 = (f32[3,512]{1,0:T(4,128)S(1)}, f32[3,2048,512]{2,1,0:T(8,128)}) fusion(bf16[3,512,128]{2,1,0:T(8,128)(2,1)S(1)} %get-tuple-element.190, bf16[8,2048,3,128]{3,1,2,0:T(8,128)(2,1)} %get-tuple-element.189, s32[]{:T(128)} %get-tuple-element.176), kind=kOutput, calls=%fused_computation.6.clone.1 | convolution fusion | flops 811596288 | bytes 14555648 | tf_op jit(solution)/shard_map/while/body/eval_jaxpr/hqd,khd->hqk/dot_general | solution.py:29
  360.7 6.6 %fusion.74 = f32[3,512]{1,0:T(4,128)S(1)} fusion(f32[3,2048,512]{2,1,0:T(8,128)} %get-tuple-element.163, f32[3,512]{1,0:T(4,128)S(1)} %select_maximum_fusion.2), kind=kLoop, calls=%fused_computation.8.clone.1 | loop fusion | flops 9435648 | bytes 12595200 | tf_op jit(solution)/shard_map/while/body/eval_jaxpr/reduce_sum | solution.py:35
  367.3 6.6 %fusion.76 = f32[3,512,128]{2,1,0:T(8,128)S(1)} fusion(bf16[8,2048,3,128]{3,1,2,0:T(8,128)(2,1)} %get-tuple-element.191, s32[]{:T(128)} %get-tuple-element.176, f32[3,2048,512]{2,1,0:T(8,128)} %get-tuple-element.163, f32[3,512]{1,0:T(4,128)S(1)} %select_maximum_fusion.2, f32[3,512,128]{2,1,0:T(8,128)S(1)} %get-tuple-element.177, ...), kind=kOutput, calls=%fused_computation.18.clone.1 | convolution fusion | flops 815333376 | bytes 15741441 | tf_op jit(solution)/shard_map/while/body/eval_jaxpr/hqk,khd->hqd/dot_general | solution.py:36
  373.9 7.8 %bitcast_reduce_fusion.2 = (f32[3,512]{1,0:T(4,128)S(1)}, f32[3,2048,512]{2,1,0:T(8,128)}) fusion(bf16[3,512,128]{2,1,0:T(8,128)(2,1)S(1)} %get-tuple-element.190, bf16[8,2048,3,128]{3,1,2,0:T(8,128)(2,1)} %get-tuple-element.189, s32[]{:T(128)} %get-tuple-element.176), kind=kOutput, calls=%fused_computation.6.clone.1 | convolution fusion | flops 811596288 | bytes 14555648 | tf_op jit(solution)/shard_map/while/body/eval_jaxpr/hqd,khd->hqk/dot_general | solution.py:29
  381.7 6.6 %fusion.74 = f32[3,512]{1,0:T(4,128)S(1)} fusion(f32[3,2048,512]{2,1,0:T(8,128)} %get-tuple-element.163, f32[3,512]{1,0:T(4,128)S(1)} %select_maximum_fusion.2), kind=kLoop, calls=%fused_computation.8.clone.1 | loop fusion | flops 9435648 | bytes 12595200 | tf_op jit(solution)/shard_map/while/body/eval_jaxpr/reduce_sum | solution.py:35
  388.4 6.6 %fusion.76 = f32[3,512,128]{2,1,0:T(8,128)S(1)} fusion(bf16[8,2048,3,128]{3,1,2,0:T(8,128)(2,1)} %get-tuple-element.191, s32[]{:T(128)} %get-tuple-element.176, f32[3,2048,512]{2,1,0:T(8,128)} %get-tuple-element.163, f32[3,512]{1,0:T(4,128)S(1)} %select_maximum_fusion.2, f32[3,512,128]{2,1,0:T(8,128)S(1)} %get-tuple-element.177, ...), kind=kOutput, calls=%fused_computation.18.clone.1 | convolution fusion | flops 815333376 | bytes 15741441 | tf_op jit(solution)/shard_map/while/body/eval_jaxpr/hqk,khd->hqd/dot_general | solution.py:36
  395.0 7.8 %bitcast_reduce_fusion.2 = (f32[3,512]{1,0:T(4,128)S(1)}, f32[3,2048,512]{2,1,0:T(8,128)}) fusion(bf16[3,512,128]{2,1,0:T(8,128)(2,1)S(1)} %get-tuple-element.190, bf16[8,2048,3,128]{3,1,2,0:T(8,128)(2,1)} %get-tuple-element.189, s32[]{:T(128)} %get-tuple-element.176), kind=kOutput, calls=%fused_computation.6.clone.1 | convolution fusion | flops 811596288 | bytes 14555648 | tf_op jit(solution)/shard_map/while/body/eval_jaxpr/hqd,khd->hqk/dot_general | solution.py:29
  402.8 6.6 %fusion.74 = f32[3,512]{1,0:T(4,128)S(1)} fusion(f32[3,2048,512]{2,1,0:T(8,128)} %get-tuple-element.163, f32[3,512]{1,0:T(4,128)S(1)} %select_maximum_fusion.2), kind=kLoop, calls=%fused_computation.8.clone.1 | loop fusion | flops 9435648 | bytes 12595200 | tf_op jit(solution)/shard_map/while/body/eval_jaxpr/reduce_sum | solution.py:35
  409.5 6.6 %fusion.76 = f32[3,512,128]{2,1,0:T(8,128)S(1)} fusion(bf16[8,2048,3,128]{3,1,2,0:T(8,128)(2,1)} %get-tuple-element.191, s32[]{:T(128)} %get-tuple-element.176, f32[3,2048,512]{2,1,0:T(8,128)} %get-tuple-element.163, f32[3,512]{1,0:T(4,128)S(1)} %select_maximum_fusion.2, f32[3,512,128]{2,1,0:T(8,128)S(1)} %get-tuple-element.177, ...), kind=kOutput, calls=%fused_computation.18.clone.1 | convolution fusion | flops 815333376 | bytes 15741441 | tf_op jit(solution)/shard_map/while/body/eval_jaxpr/hqk,khd->hqd/dot_general | solution.py:36
  416.1 7.8 %bitcast_reduce_fusion.2 = (f32[3,512]{1,0:T(4,128)S(1)}, f32[3,2048,512]{2,1,0:T(8,128)}) fusion(bf16[3,512,128]{2,1,0:T(8,128)(2,1)S(1)} %get-tuple-element.190, bf16[8,2048,3,128]{3,1,2,0:T(8,128)(2,1)} %get-tuple-element.189, s32[]{:T(128)} %get-tuple-element.176), kind=kOutput, calls=%fused_computation.6.clone.1 | convolution fusion | flops 811596288 | bytes 14555648 | tf_op jit(solution)/shard_map/while/body/eval_jaxpr/hqd,khd->hqk/dot_general | solution.py:29
  423.9 6.6 %fusion.74 = f32[3,512]{1,0:T(4,128)S(1)} fusion(f32[3,2048,512]{2,1,0:T(8,128)} %get-tuple-element.163, f32[3,512]{1,0:T(4,128)S(1)} %select_maximum_fusion.2), kind=kLoop, calls=%fused_computation.8.clone.1 | loop fusion | flops 9435648 | bytes 12595200 | tf_op jit(solution)/shard_map/while/body/eval_jaxpr/reduce_sum | solution.py:35
  430.5 6.6 %fusion.76 = f32[3,512,128]{2,1,0:T(8,128)S(1)} fusion(bf16[8,2048,3,128]{3,1,2,0:T(8,128)(2,1)} %get-tuple-element.191, s32[]{:T(128)} %get-tuple-element.176, f32[3,2048,512]{2,1,0:T(8,128)} %get-tuple-element.163, f32[3,512]{1,0:T(4,128)S(1)} %select_maximum_fusion.2, f32[3,512,128]{2,1,0:T(8,128)S(1)} %get-tuple-element.177, ...), kind=kOutput, calls=%fused_computation.18.clone.1 | convolution fusion | flops 815333376 | bytes 15741441 | tf_op jit(solution)/shard_map/while/body/eval_jaxpr/hqk,khd->hqd/dot_general | solution.py:36
  437.1 7.8 %bitcast_reduce_fusion.2 = (f32[3,512]{1,0:T(4,128)S(1)}, f32[3,2048,512]{2,1,0:T(8,128)}) fusion(bf16[3,512,128]{2,1,0:T(8,128)(2,1)S(1)} %get-tuple-element.190, bf16[8,2048,3,128]{3,1,2,0:T(8,128)(2,1)} %get-tuple-element.189, s32[]{:T(128)} %get-tuple-element.176), kind=kOutput, calls=%fused_computation.6.clone.1 | convolution fusion | flops 811596288 | bytes 14555648 | tf_op jit(solution)/shard_map/while/body/eval_jaxpr/hqd,khd->hqk/dot_general | solution.py:29
  444.9 6.6 %fusion.74 = f32[3,512]{1,0:T(4,128)S(1)} fusion(f32[3,2048,512]{2,1,0:T(8,128)} %get-tuple-element.163, f32[3,512]{1,0:T(4,128)S(1)} %select_maximum_fusion.2), kind=kLoop, calls=%fused_computation.8.clone.1 | loop fusion | flops 9435648 | bytes 12595200 | tf_op jit(solution)/shard_map/while/body/eval_jaxpr/reduce_sum | solution.py:35
  451.6 6.6 %fusion.76 = f32[3,512,128]{2,1,0:T(8,128)S(1)} fusion(bf16[8,2048,3,128]{3,1,2,0:T(8,128)(2,1)} %get-tuple-element.191, s32[]{:T(128)} %get-tuple-element.176, f32[3,2048,512]{2,1,0:T(8,128)} %get-tuple-element.163, f32[3,512]{1,0:T(4,128)S(1)} %select_maximum_fusion.2, f32[3,512,128]{2,1,0:T(8,128)S(1)} %get-tuple-element.177, ...), kind=kOutput, calls=%fused_computation.18.clone.1 | convolution fusion | flops 815333376 | bytes 15741441 | tf_op jit(solution)/shard_map/while/body/eval_jaxpr/hqk,khd->hqd/dot_general | solution.py:36
  458.2 1.2 copy.49
  459.4 1.2 divide_convert_fusion
  460.6 6.3 %add_convert_fusion = bf16[512,3072]{1,0:T(8,128)(2,1)} fusion(f32[512,3072]{1,0:T(8,128)} %fusion.35, bf16[512,384]{0,1:T(8,128)(2,1)S(1)} %bitcast.100, bf16[384,3072]{1,0:T(8,128)(2,1)S(1)} %copy-done), kind=kOutput, calls=%fused_computation.35 | convolution fusion | flops 1211105280 | bytes 12189696 | tf_op jit(solution)/shard_map/dot_general | solution.py:130
  466.9 4.7 copy.51
  472.4 35.1 %reduce-scatter.4.cloned.1.call-done = bf16[384,512]{1,0:T(8,128)(2,1)} async-done(((bf16[3072,512]{1,0:T(8,128)(2,1)}), bf16[384,512]{1,0:T(8,128)(2,1)}) %reduce-scatter.4.cloned.1.call-update) | async-done | bytes 393232
  507.5 1.2 copy.52
  508.7 0.9 fusion.43
  (107 shorter events, 4.2 us)
Async XLA Ops:
  6.5 454.1 %copy-start = (bf16[384,3072]{1,0:T(8,128)(2,1)S(1)}, bf16[384,3072]{1,0:T(8,128)(2,1)}, u32[]{:S(2)}) copy-start(bf16[384,3072]{1,0:T(8,128)(2,1)} %param.24) | copy-start | bytes 7077892
  6.5 37.1 %all-gather.4.cloned.1.call-start = ((), (), s32[]{:S(2)}) async-start(), calls=%async_computation.1 | async-start | bytes 3538944 | tf_op jit(solution)/shard_map/all_gather | solution.py:99
  10.6 12.9 %copy-start.9 = (s32[4]{0:T(128)}, s32[4]{0:T(128)S(1)}, u32[]{:S(2)}) copy-start(s32[4]{0:T(128)S(1)} %fusion.44) | copy-start | bytes 52
  13.1 14.7 %copy-start.15 = (f32[128]{0:T(128)S(1)}, f32[128]{0:T(128)}, u32[]{:S(2)}) copy-start(f32[128]{0:T(128)} %param.21) | copy-start | bytes 1540
  13.1 152.7 %all-gather.8.cloned.1.call-start = ((), (), s32[]{:S(2)}) async-start(), calls=%async_computation.3 | async-start | bytes 13369344 | tf_op jit(solution)/shard_map/all_gather | solution.py:125
  29.4 27.3 %copy-start.5 = (f32[1,3072]{1,0:T(1,128)}, f32[1,3072]{1,0:T(1,128)S(1)}, u32[]{:S(2)}) copy-start(f32[1,3072]{1,0:T(1,128)S(1)} %get-tuple-element.112) | copy-start | bytes 36868
  43.7 5.4 %copy-start.1 = (bf16[512,3072]{1,0:T(8,128)(2,1)S(1)}, bf16[512,3072]{1,0:T(8,128)(2,1)}, u32[]{:S(2)}) copy-start(bf16[512,3072]{1,0:T(8,128)(2,1)} %all-gather.4.cloned.1.call-done) | copy-start | bytes 9437188
  43.7 5.4 %copy-start.6 = (f32[1,3072]{1,0:T(1,128)S(1)}, f32[1,3072]{1,0:T(1,128)}, u32[]{:S(2)}) copy-start(f32[1,3072]{1,0:T(1,128)} %get-tuple-element.113) | copy-start | bytes 36868
  46.2 10.5 %copy-start.7 = (f32[512]{0:T(512)}, f32[512]{0:T(512)S(1)}, u32[]{:S(2)}) copy-start(f32[512]{0:T(512)S(1)} %broadcast_multiply_fusion) | copy-start | bytes 6148
  49.1 7.7 %copy-start.11 = (f32[512]{0:T(512)}, f32[512]{0:T(512)S(1)}, u32[]{:S(2)}) copy-start(f32[512]{0:T(512)S(1)} %add_rsqrt_fusion.2) | copy-start | bytes 6148
  58.3 12.7 %copy-start.10 = (s32[4]{0:T(128)S(1)}, s32[4]{0:T(128)}, u32[]{:S(2)}) copy-start(s32[4]{0:T(128)} %copy-done.9) | copy-start | bytes 52
  71.0 11.6 %copy-start.13 = (f32[128]{0:T(128)S(1)}, f32[128]{0:T(128)}, u32[]{:S(2)}) copy-start(f32[128]{0:T(128)} %param.20) | copy-start | bytes 1540
  71.0 14.8 %copy-start.8 = (f32[512]{0:T(512)S(1)}, f32[512]{0:T(512)}, u32[]{:S(2)}) copy-start(f32[512]{0:T(512)} %copy-done.7) | copy-start | bytes 6148
  71.0 14.8 %copy-start.12 = (f32[512]{0:T(512)S(1)}, f32[512]{0:T(512)}, u32[]{:S(2)}) copy-start(f32[512]{0:T(512)} %copy-done.11) | copy-start | bytes 6148
  75.9 181.7 %all-gather.6.cloned.1.call-start = ((), (), s32[]{:S(2)}) async-start(), calls=%async_computation.2 | async-start | bytes 13369344 | tf_op jit(solution)/shard_map/all_gather | solution.py:124
  78.8 428.7 %reduce-scatter.4.cloned.1.call-start = ((), (), s32[]{:S(2)}) async-start(), calls=%async_computation.4 | async-start | bytes 3538944
  297.4 6.6 %copy-start.3 = (f32[3,512]{1,0:T(4,128)S(1)}, f32[3,512]{1,0:T(4,128)}, u32[]{:S(2)}) copy-start(f32[3,512]{1,0:T(4,128)} %get-tuple-element.179) | copy-start | bytes 18436 | tf_op jit(solution)/shard_map/while
  304.1 6.6 %copy-start.4 = (f32[3,512]{1,0:T(4,128)}, f32[3,512]{1,0:T(4,128)S(1)}, u32[]{:S(2)}) copy-start(f32[3,512]{1,0:T(4,128)S(1)} %get-tuple-element.188) | copy-start | bytes 18436 | tf_op jit(solution)/shard_map/while
  318.5 6.6 %copy-start.3 = (f32[3,512]{1,0:T(4,128)S(1)}, f32[3,512]{1,0:T(4,128)}, u32[]{:S(2)}) copy-start(f32[3,512]{1,0:T(4,128)} %get-tuple-element.179) | copy-start | bytes 18436 | tf_op jit(solution)/shard_map/while
  325.2 6.6 %copy-start.4 = (f32[3,512]{1,0:T(4,128)}, f32[3,512]{1,0:T(4,128)S(1)}, u32[]{:S(2)}) copy-start(f32[3,512]{1,0:T(4,128)S(1)} %get-tuple-element.188) | copy-start | bytes 18436 | tf_op jit(solution)/shard_map/while
  339.6 6.6 %copy-start.3 = (f32[3,512]{1,0:T(4,128)S(1)}, f32[3,512]{1,0:T(4,128)}, u32[]{:S(2)}) copy-start(f32[3,512]{1,0:T(4,128)} %get-tuple-element.179) | copy-start | bytes 18436 | tf_op jit(solution)/shard_map/while
  346.3 6.6 %copy-start.4 = (f32[3,512]{1,0:T(4,128)}, f32[3,512]{1,0:T(4,128)S(1)}, u32[]{:S(2)}) copy-start(f32[3,512]{1,0:T(4,128)S(1)} %get-tuple-element.188) | copy-start | bytes 18436 | tf_op jit(solution)/shard_map/while
  360.6 6.6 %copy-start.3 = (f32[3,512]{1,0:T(4,128)S(1)}, f32[3,512]{1,0:T(4,128)}, u32[]{:S(2)}) copy-start(f32[3,512]{1,0:T(4,128)} %get-tuple-element.179) | copy-start | bytes 18436 | tf_op jit(solution)/shard_map/while
  367.3 6.6 %copy-start.4 = (f32[3,512]{1,0:T(4,128)}, f32[3,512]{1,0:T(4,128)S(1)}, u32[]{:S(2)}) copy-start(f32[3,512]{1,0:T(4,128)S(1)} %get-tuple-element.188) | copy-start | bytes 18436 | tf_op jit(solution)/shard_map/while
  381.7 6.6 %copy-start.3 = (f32[3,512]{1,0:T(4,128)S(1)}, f32[3,512]{1,0:T(4,128)}, u32[]{:S(2)}) copy-start(f32[3,512]{1,0:T(4,128)} %get-tuple-element.179) | copy-start | bytes 18436 | tf_op jit(solution)/shard_map/while
  388.4 6.6 %copy-start.4 = (f32[3,512]{1,0:T(4,128)}, f32[3,512]{1,0:T(4,128)S(1)}, u32[]{:S(2)}) copy-start(f32[3,512]{1,0:T(4,128)S(1)} %get-tuple-element.188) | copy-start | bytes 18436 | tf_op jit(solution)/shard_map/while
  402.8 6.6 %copy-start.3 = (f32[3,512]{1,0:T(4,128)S(1)}, f32[3,512]{1,0:T(4,128)}, u32[]{:S(2)}) copy-start(f32[3,512]{1,0:T(4,128)} %get-tuple-element.179) | copy-start | bytes 18436 | tf_op jit(solution)/shard_map/while
  409.5 6.6 %copy-start.4 = (f32[3,512]{1,0:T(4,128)}, f32[3,512]{1,0:T(4,128)S(1)}, u32[]{:S(2)}) copy-start(f32[3,512]{1,0:T(4,128)S(1)} %get-tuple-element.188) | copy-start | bytes 18436 | tf_op jit(solution)/shard_map/while
  423.9 6.6 %copy-start.3 = (f32[3,512]{1,0:T(4,128)S(1)}, f32[3,512]{1,0:T(4,128)}, u32[]{:S(2)}) copy-start(f32[3,512]{1,0:T(4,128)} %get-tuple-element.179) | copy-start | bytes 18436 | tf_op jit(solution)/shard_map/while
  430.5 6.6 %copy-start.4 = (f32[3,512]{1,0:T(4,128)}, f32[3,512]{1,0:T(4,128)S(1)}, u32[]{:S(2)}) copy-start(f32[3,512]{1,0:T(4,128)S(1)} %get-tuple-element.188) | copy-start | bytes 18436 | tf_op jit(solution)/shard_map/while
  444.9 6.6 %copy-start.3 = (f32[3,512]{1,0:T(4,128)S(1)}, f32[3,512]{1,0:T(4,128)}, u32[]{:S(2)}) copy-start(f32[3,512]{1,0:T(4,128)} %get-tuple-element.179) | copy-start | bytes 18436 | tf_op jit(solution)/shard_map/while
  451.6 6.6 %copy-start.4 = (f32[3,512]{1,0:T(4,128)}, f32[3,512]{1,0:T(4,128)S(1)}, u32[]{:S(2)}) copy-start(f32[3,512]{1,0:T(4,128)S(1)} %get-tuple-element.188) | copy-start | bytes 18436 | tf_op jit(solution)/shard_map/while
  466.9 5.4 %copy-start.14 = (pred[4]{0:T(512)(128)(4,1)S(1)}, pred[4]{0:T(512)(128)(4,1)}, u32[]{:S(2)}) copy-start(pred[4]{0:T(512)(128)(4,1)} %iota_compare_fusion) | copy-start | bytes 16
  466.9 41.8 %copy-start.2 = (bf16[4,128,384]{2,1,0:T(8,128)(2,1)S(1)}, bf16[4,128,384]{2,1,0:T(8,128)(2,1)}, u32[]{:S(2)}) copy-start(bf16[4,128,384]{2,1,0:T(8,128)(2,1)} %gather_fusion) | copy-start | bytes 1179652
Sparse Core Ops, SparseCore 0:
  13.2 30.3 all-gather.3
  76.0 89.7 all-gather.7
  167.9 89.5 all-gather.5
  471.8 35.6 reduce-scatter.3
where the time goes:
time: 519 us; the launch traced here: 516 us
  waiting for transfers between devices  175 us (34%)
  matrix products  143 us (28%)
  local copies, waits for them, and re-layouts  111 us (21%)
  other arithmetic  72.4 us (14%)
  between operations  14 us (3%)
    unnamed x38, local copies, waits for them, and re-layouts  84.6 us
    all_gather x1, waiting for transfers between devices, body(): lax.all_gather(value_patched, 'patch', axis=0, tiled=True)  65.6 us
    dot_general x8, matrix products, attend_block(): jnp.einsum('hqd,khd->hqk', queries, key_heads, preferred_element_type=jnp...  62.3 us
    all_gather x1, waiting for transfers between devices, body(): lax.all_gather(key_patched, 'patch', axis=0, tiled=True)  60.1 us
    reduce_sum x8, other arithmetic, attend_block(): acc_total = acc_total * factor + jnp.sum(weights, axis=-1)  53 us
    dot_general x8, matrix products, attend_block(): jnp.einsum('hqk,khd->hqd', weights.astype(jnp.bfloat16), value_heads, pre...  52.4 us
    unnamed x5, waiting for transfers between devices  35.1 us
    dot_general x1, matrix products, body(): jnp.dot(hidden_mlp, w_out_mlp, preferred_element_type=jnp.float32)  14.3 us
  transfers between devices with their start and end apart: 4, of which 4 were waited for; matrix products, arithmetic and copies ran while one was open for 14% of the time, Pallas kernels for 0%

commit v1 on v0

v1 whole, which is shorter than its diff:
```python
import functools
import math

import jax
import jax.numpy as jnp
from jax import lax
from jax.experimental import pallas as pl
from jax.experimental.pallas import tpu as pltpu
from jax.sharding import PartitionSpec as P

HD = 128
BLOCK = 128
RMAX = 4
NZ = 4
SIDE = 4
LSE_ROWS = 16
BF16 = jnp.bfloat16
F32 = jnp.float32
EXP2_SCALE = HD ** (-0.5) * math.log2(math.e)
VMEM = pltpu.VMEM


def whole(shape):
    return pl.BlockSpec(shape, lambda *_: (0,) * len(shape), memory_space=VMEM)


def params(mib):
    return pltpu.CompilerParams(vmem_limit_bytes=mib * 2**20)


def pick_rows_kernel(order, hidden_ref, rows_ref):
    rows_ref[...] = hidden_ref[...]


def pick_rows(order, hidden):
    width = hidden.shape[1]
    return pl.pallas_call(
        pick_rows_kernel,
        grid_spec=pltpu.PrefetchScalarGridSpec(
            num_scalar_prefetch=1,
            grid=(RMAX,),
            in_specs=[pl.BlockSpec((BLOCK, width), lambda i, order: (order[i], 0))],
            out_specs=pl.BlockSpec((BLOCK, width), lambda i, order: (i, 0)),
        ),
        out_shape=jax.ShapeDtypeStruct((RMAX * BLOCK, width), BF16),
        compiler_params=params(16),
        name="pick_rows",
    )(order, hidden)


def pick_cache_kernel(order, key_slot, value_slot, key_rest, value_rest, slots_ref, rest_ref):
    width = key_slot.shape[1]
    slots_ref[:, :width] = key_slot[...]
    slots_ref[:, width:] = value_slot[...]
    rest_ref[:, :width] = key_rest[...]
    rest_ref[:, width:] = value_rest[...]


def pick_cache(order, key_cache, value_cache):
    width = key_cache.shape[1]
    slot = pl.BlockSpec((BLOCK, width), lambda i, order: (order[i], 0))
    rest = pl.BlockSpec((BLOCK, width), lambda i, order: (order[RMAX + i], 0))
    out = pl.BlockSpec((BLOCK, 2 * width), lambda i, order: (i, 0))
    shape = jax.ShapeDtypeStruct((RMAX * BLOCK, 2 * width), BF16)
    return pl.pallas_call(
        pick_cache_kernel,
        grid_spec=pltpu.PrefetchScalarGridSpec(
            num_scalar_prefetch=1,
            grid=(RMAX,),
            in_specs=[slot, slot, rest, rest],
            out_specs=[out, out],
        ),
        out_shape=[shape, shape],
        compiler_params=params(16),
        name="pick_cache",
    )(order, key_cache, value_cache, key_cache, value_cache)


def project_kernel(
    place, r0, r1, r2, r3, s0, s1, s2, s3, mod_ref, qg_ref, kg_ref, w_ref, old_ref,
    q_ref, kv_ref, modded_ref,
):
    step = pl.program_id(0)
    z, core, count = place[0], place[1], place[2]
    pieces = []
    for k in range(NZ):
        zs = lax.rem(z - k + NZ, NZ)
        pieces.append(((r0, r1, r2, r3)[k], zs * 2 + core))
        pieces.append(((s0, s1, s2, s3)[k], zs * 2 + 1 - core))
    rows, width = r0.shape
    features = width * len(pieces)
    tall = 64

    @pl.when(step == 0)
    def _():
        def norm(i, carry):
            here = pl.ds(pl.multiple_of(i * tall, tall), tall)
            total = jnp.zeros((tall, width), F32)
            for ref, _h in pieces:
                total = total + ref[here, :].astype(F32)
            mean = jnp.sum(total, axis=-1, keepdims=True) * (1.0 / features)
            square = jnp.zeros((tall, width), F32)
            for ref, _h in pieces:
                center = ref[here, :].astype(F32) - mean
                square = square + center * center
            spread = jnp.sum(square, axis=-1, keepdims=True) * (1.0 / features)
            inv = lax.rsqrt(spread + 1e-06)
            for ref, h in pieces:
                cols = pl.ds(pl.multiple_of(h * width, 128), width)
                normed = (ref[here, :].astype(F32) - mean) * inv
                out = normed * (1.0 + mod_ref[1:2, cols]) + mod_ref[0:1, cols]
                modded_ref[here, cols] = out.astype(BF16)
            return carry

        lax.fori_loop(0, rows // tall, norm, 0)

    def half(i, carry):
        here = pl.ds(pl.multiple_of(i * 256, 256), 256)
        acc = jnp.dot(modded_ref[here, :], w_ref[...], preferred_element_type=F32)

        def rms(gain):
            out = []
            for j in range(width // HD):
                v = acc[:, j * HD : (j + 1) * HD]
                scale = lax.rsqrt(jnp.mean(v * v, axis=-1, keepdims=True) + 1e-06)
                out.append((v * scale * gain).astype(BF16))
            return jnp.concatenate(out, axis=1)

        first = i * 256
        fresh = first + lax.broadcasted_iota(jnp.int32, (256, width), 0) < count * BLOCK

        @pl.when(step == 0)
        def _():
            q_ref[here, :] = rms(qg_ref[...])

        @pl.when(step == 1)
        def _():
            old = old_ref[here, :width]
            kv_ref[here, :width] = jnp.where(fresh, rms(kg_ref[...]).astype(F32), old.astype(F32)).astype(BF16)

        @pl.when(step == 2)
        def _():
            old = old_ref[here, width:]
            kv_ref[here, width:] = jnp.where(fresh, acc, old.astype(F32)).astype(BF16)

        return carry

    lax.fori_loop(0, rows // 256, half, 0)


def project(place, own, swapped, modulation, query_gain, key_gain, w_qkv, old):
    rows, width = own[0].shape
    features = w_qkv.shape[0]
    return pl.pallas_call(
        project_kernel,
        grid_spec=pltpu.PrefetchScalarGridSpec(
            num_scalar_prefetch=1,
            grid=(3,),
            in_specs=[whole((rows, width))] * 8
            + [whole(modulation.shape), whole((1, HD)), whole((1, HD))]
            + [pl.BlockSpec((features, width), lambda i, *_: (0, i)), whole(old.shape)],
            out_specs=[whole((rows, width)), whole((rows, 2 * width)), whole((rows, features))],
        ),
        out_shape=[
            jax.ShapeDtypeStruct((rows, width), BF16),
            jax.ShapeDtypeStruct((rows, 2 * width), BF16),
            jax.ShapeDtypeStruct((rows, features), BF16),
        ],
        compiler_params=params(48),
        cost_estimate=pl.CostEstimate(
            flops=2 * rows * features * 3 * width, bytes_accessed=14_000_000, transcendentals=0
        ),
        name="project",
    )(place, *own, *swapped, modulation, query_gain.reshape(1, HD), key_gain.reshape(1, HD), w_qkv, old)


def mlp_kernel(modded_ref, w_ref, out_ref):
    def half(i, carry):
        here = pl.ds(pl.multiple_of(i * 256, 256), 256)
        acc = jnp.dot(modded_ref[here, :], w_ref[...], preferred_element_type=F32)
        out_ref[here, :] = jax.nn.gelu(acc, approximate=True).astype(BF16)
        return carry

    lax.fori_loop(0, modded_ref.shape[0] // 256, half, 0)


def mlp_in(modded, w_mlp):
    rows, features = modded.shape
    hidden = w_mlp.shape[1]
    tile = 256
    return pl.pallas_call(
        mlp_kernel,
        grid=(hidden // tile,),
        in_specs=[whole(modded.shape), pl.BlockSpec((features, tile), lambda i: (0, i))],
        out_specs=pl.BlockSpec((rows, tile), lambda i: (0, i)),
        out_shape=jax.ShapeDtypeStruct((rows, hidden), BF16),
        compiler_params=params(40),
        cost_estimate=pl.CostEstimate(
            flops=2 * rows * features * hidden, bytes_accessed=9_000_000, transcendentals=0
        ),
        name="mlp_in",
    )(modded, w_mlp)


def attend_kernel(counts, *refs):
    q_refs, k_refs, v_refs = refs[:4], refs[4:12], refs[12:20]
    o_refs, (qs, os_, ls) = refs[20:24], refs[24:]
    rows = q_refs[0].shape[0]
    slots = rows // BLOCK
    starts, total = [], 0
    for s in range(SIDE):
        starts.append(total)
        total = total + counts[s]

    for s in range(SIDE):
        for i in range(slots):
            @pl.when(i < counts[s])
            def _(s=s, i=i):
                to = pl.ds(pl.multiple_of((starts[s] + i) * BLOCK, BLOCK), BLOCK)
                qs[to, :] = q_refs[s][i * BLOCK : (i + 1) * BLOCK, :]

    def tile(t, carry):
        here = pl.ds(pl.multiple_of(t * 2 * BLOCK, 2 * BLOCK), 2 * BLOCK)
        q = qs[here, :]
        scores = [
            lax.dot_general(q, k[...], (((1,), (1,)), ((), ())), preferred_element_type=F32)
            for k in k_refs
        ]
        top = functools.reduce(jnp.maximum, scores)
        top = jnp.max(top, axis=-1, keepdims=True)
        acc = jnp.zeros((2 * BLOCK, 2 * HD), F32)
        ones = jnp.ones((rows, HD), BF16)
        for score, v in zip(scores, v_refs):
            weights = jnp.exp2((score - top) * EXP2_SCALE).astype(BF16)
            acc = acc + jnp.dot(
                weights, jnp.concatenate([v[...], ones], axis=1), preferred_element_type=F32
            )
        os_[here, :] = (acc[:, :HD] / acc[:, HD:]).astype(BF16)
        ls[here, :] = top * EXP2_SCALE + jnp.log2(acc[:, HD:])
        return carry

    lax.fori_loop(0, lax.div(total + 1, 2), tile, 0)

    line = lax.broadcasted_iota(jnp.int32, (LSE_ROWS, BLOCK), 0)
    for s in range(SIDE):
        packed = jnp.zeros((LSE_ROWS, BLOCK), F32)
        for i in range(slots):
            at = jnp.where(i < counts[s], starts[s] + i, 0)
            here = pl.ds(pl.multiple_of(at * BLOCK, BLOCK), BLOCK)
            o_refs[s][i * BLOCK : (i + 1) * BLOCK, :] = os_[here, :]
            lse = jnp.transpose(ls[here, :])[:LSE_ROWS, :]
            high = lse.astype(BF16).astype(F32)
            mid = (lse - high).astype(BF16).astype(F32)
            low = lse - high - mid
            part = line - 4 * i
            packed = jnp.where(part == 0, high, packed)
            packed = jnp.where(part == 1, mid, packed)
            packed = jnp.where(part == 2, low, packed)
        o_refs[s][rows : rows + LSE_ROWS, :] = packed.astype(BF16)


def attend(counts, queries, caches):
    rows, width = queries[0].shape
    heads = width // HD
    key_block = pl.BlockSpec((rows, HD), lambda j, *_: (0, j))
    value_block = pl.BlockSpec((rows, HD), lambda j, *_: (0, heads + j))
    tall = rows + LSE_ROWS
    return pl.pallas_call(
        attend_kernel,
        grid_spec=pltpu.PrefetchScalarGridSpec(
            num_scalar_prefetch=1,
            grid=(heads,),
            in_specs=[key_block] * 4 + [key_block] * 8 + [value_block] * 8,
            out_specs=[pl.BlockSpec((tall, HD), lambda j, *_: (0, j))] * 4,
            scratch_shapes=[
                VMEM((SIDE * rows, HD), BF16),
                VMEM((SIDE * rows, HD), BF16),
                VMEM((SIDE * rows, HD), F32),
            ],
        ),
        out_shape=[jax.ShapeDtypeStruct((tall, width), BF16)] * 4,
        compiler_params=params(48),
        cost_estimate=pl.CostEstimate(
            flops=12_000_000_000, bytes_accessed=10_000_000, transcendentals=12_000_000
        ),
        name="attend",
    )(counts, *queries, *caches, *caches)


def branch_send_kernel(cols, p0, p1, p2, p3, mlp_ref, wa_ref, wm_ref, send_ref, attn_ref):
    parts = (p0, p1, p2, p3)
    rows = mlp_ref.shape[0]
    heads = attn_ref.shape[1] // HD

    @pl.when(pl.program_id(0) == 0)
    def _():
        for j in range(heads):
            lanes = slice(j * HD, (j + 1) * HD)
            lses = [p[rows : rows + LSE_ROWS, lanes].astype(F32) for p in parts]
            for i in range(rows // BLOCK):
                each = []
                for lse in lses:
                    total = lse[4 * i : 4 * i + 1] + lse[4 * i + 1 : 4 * i + 2] + lse[4 * i + 2 : 4 * i + 3]
                    each.append(jnp.broadcast_to(total, (BLOCK, BLOCK)))
                top = functools.reduce(jnp.maximum, each)
                shares = [jnp.exp2(e - top) for e in each]
                scale = 1.0 / functools.reduce(jnp.add, shares)
                here = slice(i * BLOCK, (i + 1) * BLOCK)
                mixed = jnp.zeros((BLOCK, HD), F32)
                for share, p in zip(shares, parts):
                    mixed = mixed + jnp.transpose(share * scale) * p[here, lanes].astype(F32)
                attn_ref[here, lanes] = mixed.astype(BF16)

    acc = jnp.dot(attn_ref[...], wa_ref[...], preferred_element_type=F32)
    acc = acc + jnp.dot(mlp_ref[...], wm_ref[...], preferred_element_type=F32)
    send_ref[0] = acc.astype(BF16)


def branch_keep_kernel(cols, attn_ref, mlp_ref, wa_ref, wm_ref, keep_ref):
    acc = jnp.dot(attn_ref[...], wa_ref[...], preferred_element_type=F32)
    acc = acc + jnp.dot(mlp_ref[...], wm_ref[...], preferred_element_type=F32)
    keep_ref[0] = acc.astype(BF16)


def branch(cols, inputs, mlp_hidden, w_attn, w_mlp, first):
    rows = mlp_hidden.shape[0]
    width = w_attn.shape[0]
    specs = [whole(a.shape) for a in inputs] + [
        whole(mlp_hidden.shape),
        pl.BlockSpec((w_attn.shape[0], width), lambda i, cols: (0, cols[i])),
        pl.BlockSpec((w_mlp.shape[0], width), lambda i, cols: (0, cols[i])),
    ]
    out_specs = [pl.BlockSpec((1, rows, width), lambda i, cols: (i, 0, 0))]
    out_shape = [jax.ShapeDtypeStruct((NZ, rows, width), BF16)]
    if first:
        out_specs.append(whole((rows, width)))
        out_shape.append(jax.ShapeDtypeStruct((rows, width), BF16))
    return pl.pallas_call(
        branch_send_kernel if first else branch_keep_kernel,
        grid_spec=pltpu.PrefetchScalarGridSpec(
            num_scalar_prefetch=1, grid=(NZ,), in_specs=specs, out_specs=out_specs
        ),
        out_shape=out_shape,
        compiler_params=params(40),
        cost_estimate=pl.CostEstimate(
            flops=2 * rows * (width + w_mlp.shape[0]) * NZ * width,
            bytes_accessed=7_000_000,
            transcendentals=0,
        ),
        name="branch_send" if first else "branch_keep",
    )(cols, *inputs, mlp_hidden, w_attn, w_mlp)


def along_x(a, k):
    return lax.ppermute(a, "patch", [(y * 4 + x, y * 4 + (x + k) % 4) for y in range(4) for x in range(4)])


def along_y(a, k):
    return lax.ppermute(a, "patch", [(y * 4 + x, (y + k) % 4 * 4 + x) for y in range(4) for x in range(4)])


def along_z(a, k):
    return lax.ppermute(a, "head", [(z * 2 + c, (z + k) % 4 * 2 + c) for z in range(4) for c in range(2)])


def other_core(a):
    return lax.ppermute(a, "head", [(i, i ^ 1) for i in range(8)])


def body(
    hidden, key_cache, value_cache, block_order, refresh_counts, modulation,
    query_gain, key_gain, w_qkv, w_mlp, w_out_attn, w_out_mlp,
):
    width = hidden.shape[1]
    order = block_order[0]
    count = refresh_counts[0]
    head = lax.axis_index("head")
    z, core = head // 2, head % 2

    rows = pick_rows(order, hidden)
    far = {k: along_z(rows, k) for k in (1, 3, 2)}
    own = [rows, far[1], far[2], far[3]]
    swapped = [other_core(a) for a in own]

    old_slots, rest = pick_cache(order, key_cache, value_cache)
    rest_far = {k: along_y(rest, k) for k in (1, 3, 2)}
    counts_far = {k: along_x(refresh_counts, k) for k in (1, 3, 2)}
    counts = jnp.concatenate([refresh_counts, counts_far[1], counts_far[2], counts_far[3]])

    place = jnp.stack([z, core, count]).astype(jnp.int32)
    queries, fresh, modded = project(
        place, own, swapped, modulation, query_gain, key_gain,
        w_qkv.reshape(w_qkv.shape[0], 3 * width), old_slots,
    )
    query_far = {k: along_x(queries, k) for k in (1, 3, 2)}
    fresh_far = {k: along_y(fresh, k) for k in (1, 3, 2)}
    mlp_hidden = mlp_in(modded, w_mlp)

    parts = attend(
        counts,
        [queries, query_far[1], query_far[2], query_far[3]],
        [rest, rest_far[1], rest_far[2], rest_far[3], fresh, fresh_far[1], fresh_far[2], fresh_far[3]],
    )
    back = {k: along_x(parts[k], -k) for k in (1, 3, 2)}

    ahead = (z + jnp.arange(NZ)) % NZ * 2
    send, attn = branch(
        (ahead + 1 - core).astype(jnp.int32),
        [parts[0], back[1], back[2], back[3]], mlp_hidden, w_out_attn, w_out_mlp, True,
    )
    (keep,) = branch((ahead + core).astype(jnp.int32), [attn], mlp_hidden, w_out_attn, w_out_mlp, False)
    got = other_core(send)
    chip = keep.astype(F32) + got.astype(F32)
    summed = chip[0]
    for k in (2, 1, 3):
        summed = summed + along_z(chip[k].astype(BF16), k).astype(F32)

    gate = lax.dynamic_slice_in_dim(modulation[2], head * width, width)
    result = (rows.astype(F32) + gate * summed).astype(BF16)
    live = jnp.arange(rows.shape[0]) < count * BLOCK
    return jnp.where(live[:, None], result, jnp.zeros((), BF16))


def solution(mesh):
    in_specs = (
        P("patch", "head"), P("patch", "head"), P("patch", "head"), P("patch", None), P("patch"),
        P(), P(), P(),
        P(None, None, "head"), P(None, "head"), P("head", None), P("head", None),
    )
    return jax.shard_map(
        body, mesh=mesh, in_specs=in_specs, out_specs=P("patch", "head"), check_vma=False
    )
```

time: 519 us -> 217 us (0.42)
  the two profiles are of different devices: /device:TPU:0 before, /device:TPU:8 now
where the time goes in v1:
time: 217 us; the launch traced here: 216 us
  Pallas kernels  70.8 us (33%)
  waiting for transfers between devices  68.8 us (32%)
  starting transfers between devices  35.7 us (16%)
  local copies, waits for them, and re-layouts  33.4 us (15%)
  other arithmetic  6.28 us (3%)
    pallas_call x1, Pallas kernels, attend(): pl.pallas_call(attend_kernel, grid_spec=pltpu.PrefetchScalarGridSpec(num_...  41.1 us
    ppermute x6, waiting for transfers between devices, along_z(): lax.ppermute(a, 'head', [(z * 2 + c, (z + k) % 4 * 2 + c) for z in range(...  28.4 us
    ppermute x9, waiting for transfers between devices, along_x(): lax.ppermute(a, 'patch', [(y * 4 + x, y * 4 + (x + k) % 4) for y in range...  23.5 us
    unnamed x41, local copies, waits for them, and re-layouts  23 us
    ppermute x6, waiting for transfers between devices, along_y(): lax.ppermute(a, 'patch', [(y * 4 + x, (y + k) % 4 * 4 + x) for y in range...  16.9 us
    pallas_call x1, Pallas kernels, project(): pl.pallas_call(project_kernel, grid_spec=pltpu.PrefetchScalarGridSpec(num...  14.7 us
    ppermute x6, starting transfers between devices, along_z(): lax.ppermute(a, 'head', [(z * 2 + c, (z + k) % 4 * 2 + c) for z in range(...  13.8 us
    ppermute x9, starting transfers between devices, along_x(): lax.ppermute(a, 'patch', [(y * 4 + x, y * 4 + (x + k) % 4) for y in range...  12.9 us
  transfers between devices with their start and end apart: 26, of which 15 were waited for; matrix products, arithmetic and copies ran while one was open for 10% of the time, Pallas kernels for 11%

profile of v1, /device:TPU:8, one launch (start us, length us, event | category | flops | bytes accessed | tf_op | source)
XLA Modules:
  0.0 215.9 jit_solution(10138525894082093823)
XLA Ops:
  0.0 1.1 copy-done.3
  1.1 0.7 copy-done.5
  1.8 0.7 pick_rows.1.r0
  2.5 2.0 collective-permute-start.3
  4.4 3.6 %collective-permute-start.4 = (bf16[512,384]{1,0:T(8,128)(2,1)S(1)}, bf16[512,384]{1,0:T(8,128)(2,1)}, u32[]{:S(2)}, u32[]{:S(2)}) collective-permute-start(bf16[512,384]{1,0:T(8,128)(2,1)S(1)} %pick_rows.1.r0), channel_id=1, source_target_pairs={{0,4},{1,5},{2,6},{3,7},{4,0},{5,1},{6,2},{7,3},{8,12},{9,13},{10,... | collective-permute-start | bytes 1179656 | tf_op jit(solution)/shard_map/ppermute | solution.py:363
  8.0 1.0 collective-permute-start.5
  9.0 6.6 %collective-permute-done.3.r1 = bf16[512,384]{1,0:T(8,128)(2,1)S(1)} collective-permute-done((bf16[512,384]{1,0:T(8,128)(2,1)S(1)}, bf16[512,384]{1,0:T(8,128)(2,1)S(1)}, u32[]{:S(2)}, u32[]{:S(2)}) %collective-permute-start.3) | collective-permute-done | bytes 393248 | tf_op jit(solution)/shard_map/ppermute | solution.py:363
  15.7 0.0 collective-permute-start.7
  15.7 1.1 copy-done.1
  16.8 1.1 copy-done.2
  17.9 0.8 pick_cache.1
  18.7 0.9 copy-done.7
  19.6 1.6 collective-permute-start.13
  21.2 4.2 %collective-permute-done.4.r2 = bf16[512,384]{1,0:T(8,128)(2,1)} collective-permute-done((bf16[512,384]{1,0:T(8,128)(2,1)S(1)}, bf16[512,384]{1,0:T(8,128)(2,1)}, u32[]{:S(2)}, u32[]{:S(2)}) %collective-permute-start.4) | collective-permute-done | bytes 393248 | tf_op jit(solution)/shard_map/ppermute | solution.py:363
  25.4 2.3 %collective-permute-start.14 = (bf16[512,768]{1,0:T(8,128)(2,1)S(1)}, bf16[512,768]{1,0:T(8,128)(2,1)S(1)}, u32[]{:S(2)}, u32[]{:S(2)}) collective-permute-start(bf16[512,768]{1,0:T(8,128)(2,1)S(1)} %get-tuple-element.18.refs_4_.refs_12_), channel_id=1, source_target_pairs={{0,64},{8,72},{16,80},{24,88},{32,96},{40,104},{48,112},{56,120},{... | collective-permute-start | bytes 2359304 | tf_op jit(solution)/shard_map/ppermute | solution.py:359
  27.7 0.0 copy-start.10
  27.7 0.7 copy-done.10
  28.4 0.5 collective-permute-start.9
  29.6 1.4 collective-permute-start.15
  31.0 0.1 pad_add_fusion.1.place
  31.1 10.1 %copy.14 = bf16[3072,3,384]{0,2,1:T(8,128)(2,1)} copy(bf16[3072,3,384]{2,0,1:T(8,128)(2,1)} %param.20) | data formatting | bytes 14155776 | tf_op args[8]
  41.2 10.3 %copy.15.w_ref = bf16[3072,1152]{1,0:T(8,128)(2,1)} copy(bf16[3072,1152]{0,1:T(8,128)(2,1)} %bitcast.35) | data formatting | bytes 14155776 | tf_op jit(solution)/shard_map/reshape | solution.py:393
  51.4 2.8 %collective-permute-start.2 = (s32[1]{0:T(128)}, s32[1]{0:T(128)}, u32[]{:S(2)}, u32[]{:S(2)}) collective-permute-start(s32[1]{0:T(128)} %param.16), channel_id=1, source_target_pairs={{0,24},{8,0},{16,8},{24,16},{32,56},{40,32},{48,40},{56,48},{64,88... | collective-permute-start | bytes 20 | tf_op jit(solution)/shard_map/ppermute | solution.py:355
  54.2 0.8 collective-permute-start.1
  55.0 1.1 copy-done.8
  56.1 1.0 copy-done.11
  57.1 14.7 %project.1 = (bf16[512,384]{1,0:T(8,128)(2,1)S(1)}, bf16[512,768]{1,0:T(8,128)(2,1)S(1)}, bf16[512,3072]{1,0:T(8,128)(2,1)}) custom-call(s32[3]{0:T(128)S(1)} %pad_add_fusion.1.place, bf16[512,384]{1,0:T(8,128)(2,1)S(1)} %pick_rows.1.r0, bf16[512,384]{1,0:T(8,128)(2,1)S(1)} %collective-permute-done.3.r1, bf16[512,384]{1,0:T(8,128)(2,1)} %collective-permute-done.4.r2, ...), custom_call_target="tpu_custom_call" | custom-call | flops 3623878656 | bytes 14000000 | tf_op jit(solution)/shard_map/project/pallas_call | solution.py:154
  71.8 0.9 collective-permute-start
  72.8 1.8 collective-permute-start.10
  74.6 2.2 %collective-permute-done = s32[1]{0:T(128)} collective-permute-done((s32[1]{0:T(128)}, s32[1]{0:T(128)}, u32[]{:S(2)}, u32[]{:S(2)}) %collective-permute-start) | collective-permute-done | bytes 36 | tf_op jit(solution)/shard_map/ppermute | solution.py:355
  76.8 0.7 collective-permute-start.16
  77.4 2.5 %collective-permute-start.17 = (bf16[512,768]{1,0:T(8,128)(2,1)S(1)}, bf16[512,768]{1,0:T(8,128)(2,1)S(1)}, u32[]{:S(2)}, u32[]{:S(2)}) collective-permute-start(bf16[512,768]{1,0:T(8,128)(2,1)S(1)} %get-tuple-element.19.refs_8_.refs_16_), channel_id=1, source_target_pairs={{0,64},{8,72},{16,80},{24,88},{32,96},{40,104},{48,112},{56,120},{... | collective-permute-start | bytes 2359304 | tf_op jit(solution)/shard_map/ppermute | solution.py:359
  79.9 1.6 collective-permute-start.11
  81.5 3.9 %collective-permute-done.10.refs_1_ = bf16[512,384]{1,0:T(8,128)(2,1)S(1)} collective-permute-done((bf16[512,384]{1,0:T(8,128)(2,1)S(1)}, bf16[512,384]{1,0:T(8,128)(2,1)S(1)}, u32[]{:S(2)}, u32[]{:S(2)}) %collective-permute-start.10) | collective-permute-done | bytes 393248 | tf_op jit(solution)/shard_map/ppermute | solution.py:355
  85.5 1.7 collective-permute-start.12
  87.2 1.9 pad_add_fusion.counts
  89.1 3.8 %collective-permute-done.11.refs_2_ = bf16[512,384]{1,0:T(8,128)(2,1)S(1)} collective-permute-done((bf16[512,384]{1,0:T(8,128)(2,1)S(1)}, bf16[512,384]{1,0:T(8,128)(2,1)S(1)}, u32[]{:S(2)}, u32[]{:S(2)}) %collective-permute-start.11) | collective-permute-done | bytes 393248 | tf_op jit(solution)/shard_map/ppermute | solution.py:355
  92.9 3.3 %collective-permute-done.12.refs_3_ = bf16[512,384]{1,0:T(8,128)(2,1)S(1)} collective-permute-done((bf16[512,384]{1,0:T(8,128)(2,1)S(1)}, bf16[512,384]{1,0:T(8,128)(2,1)S(1)}, u32[]{:S(2)}, u32[]{:S(2)}) %collective-permute-start.12) | collective-permute-done | bytes 393248 | tf_op jit(solution)/shard_map/ppermute | solution.py:355
  96.2 1.1 collective-permute-done.16.refs_9_.refs_17_
  97.3 2.2 %collective-permute-done.17.refs_10_.refs_18_ = bf16[512,768]{1,0:T(8,128)(2,1)S(1)} collective-permute-done((bf16[512,768]{1,0:T(8,128)(2,1)S(1)}, bf16[512,768]{1,0:T(8,128)(2,1)S(1)}, u32[]{:S(2)}, u32[]{:S(2)}) %collective-permute-start.17) | collective-permute-done | bytes 786464 | tf_op jit(solution)/shard_map/ppermute | solution.py:359
  99.4 13.6 %collective-permute-done.18.refs_11_.refs_19_ = bf16[512,768]{1,0:T(8,128)(2,1)S(1)} collective-permute-done((bf16[512,768]{1,0:T(8,128)(2,1)S(1)}, bf16[512,768]{1,0:T(8,128)(2,1)S(1)}, u32[]{:S(2)}, u32[]{:S(2)}) %collective-permute-start.18) | collective-permute-done | bytes 786464 | tf_op jit(solution)/shard_map/ppermute | solution.py:359
  113.1 0.9 copy-done.17
  114.0 41.1 %attend.1 = (bf16[528,384]{1,0:T(8,128)(2,1)S(1)}, bf16[528,384]{1,0:T(8,128)(2,1)S(1)}, bf16[528,384]{1,0:T(8,128)(2,1)S(1)}, bf16[528,384]{1,0:T(8,128)(2,1)S(1)}) custom-call(s32[4]{0:T(128)S(1)} %pad_add_fusion.counts, bf16[512,384]{1,0:T(8,128)(2,1)S(1)} %get-tuple-element.17.refs_0_, bf16[512,384]{1,0:T(8,128)(2,1)S(1)} %collective-permute-done.10.refs_1_, ...), custom_call_target="tpu_custom_call" | custom-call | flops 12000000000 | bytes 10000000 | tf_op jit(solution)/shard_map/attend/pallas_call | solution.py:268
  155.0 0.6 collective-permute-start.19
  155.7 1.4 collective-permute-start.20
  157.1 1.2 collective-permute-start.21
  158.3 2.3 %copy-done.6 = bf16[3072,768]{1,0:T(8,128)(2,1)S(1)} copy-done((bf16[3072,768]{1,0:T(8,128)(2,1)S(1)}, bf16[3072,768]{1,0:T(8,128)(2,1)}, u32[]{:S(2)}) %copy-start.6) | copy-done | bytes 4718616
  160.6 1.9 copy-done.14
  162.5 4.1 %mlp_in.1.mlp_ref = bf16[512,768]{1,0:T(8,128)(2,1)S(1)} custom-call(bf16[512,3072]{1,0:T(8,128)(2,1)S(1)} %copy-done.14, bf16[3072,768]{1,0:T(8,128)(2,1)S(1)} %copy-done.6), custom_call_target="tpu_custom_call" | custom-call | flops 2415919104 | bytes 9000000 | tf_op jit(solution)/shard_map/mlp_in/pallas_call | solution.py:191
  166.6 0.9 collective-permute-done.19.p1
  167.5 1.9 collective-permute-done.20.p2
  169.5 7.4 %collective-permute-done.21.p3 = bf16[528,384]{1,0:T(8,128)(2,1)S(1)} collective-permute-done((bf16[528,384]{1,0:T(8,128)(2,1)S(1)}, bf16[528,384]{1,0:T(8,128)(2,1)S(1)}, u32[]{:S(2)}, u32[]{:S(2)}) %collective-permute-start.21) | collective-permute-done | bytes 405536 | tf_op jit(solution)/shard_map/ppermute | solution.py:355
  176.9 5.3 %branch_send.1 = (bf16[4,512,384]{2,1,0:T(8,128)(2,1)S(1)}, bf16[512,384]{1,0:T(8,128)(2,1)S(1)}) custom-call(s32[4]{0:T(128)S(1)} %add_subtract_fusion.cols, bf16[528,384]{1,0:T(8,128)(2,1)S(1)} %get-tuple-element.20.p0, bf16[528,384]{1,0:T(8,128)(2,1)S(1)} %collective-permute-done.19.p1, bf16[528,384]{1,0:T(8,128)(2,1)S(1)} %collective-permute-done.20.p2, ...), custom_call_target="tpu_custom_call" | custom-call | flops 1811939328 | bytes 7000000 | tf_op jit(solution)/shard_map/branch_send/pallas_call | solution.py:338
  182.2 0.1 collective-permute-start.22
  182.3 4.3 %branch_keep.1 = bf16[4,512,384]{2,1,0:T(8,128)(2,1)S(1)} custom-call(s32[4]{0:T(128)S(1)} %broadcast_add_fusion.cols, bf16[512,384]{1,0:T(8,128)(2,1)S(1)} %get-tuple-element.25.attn_ref, bf16[512,768]{1,0:T(8,128)(2,1)S(1)} %mlp_in.1.mlp_ref, bf16[384,3072]{1,0:T(8,128)(2,1)S(1)} %copy-done, bf16[768,3072]{1,0:T(8,128)(2,1)S(1)} %bitcast.30), custom_call_target="tpu_custom_call" | custom-call | flops 1811939328 | bytes 7000000 | tf_op jit(solution)/shard_map/branch_keep/pallas_call | solution.py:338
  186.7 2.1 convert_add_fusion
  188.7 0.1 slice_bitcast_fusion.3
  188.8 0.2 collective-permute-start.25
  189.0 2.6 %collective-permute-start.24 = (bf16[512,384]{1,0:T(8,128)(2,1)S(1)}, bf16[512,384]{1,0:T(8,128)(2,1)S(1)}, u32[]{:S(2)}, u32[]{:S(2)}) collective-permute-start(bf16[512,384]{1,0:T(8,128)(2,1)S(1)} %get-tuple-element.31), channel_id=1, source_target_pairs={{0,2},{1,3},{2,4},{3,5},{4,6},{5,7},{6,0},{7,1},{8,10},{9,11},{10,... | collective-permute-start | bytes 1179656 | tf_op jit(solution)/shard_map/ppermute | solution.py:363
  191.7 4.4 %collective-permute-start.23 = (bf16[512,384]{1,0:T(8,128)(2,1)S(1)}, bf16[512,384]{1,0:T(8,128)(2,1)S(1)}, u32[]{:S(2)}, u32[]{:S(2)}) collective-permute-start(bf16[512,384]{1,0:T(8,128)(2,1)S(1)} %get-tuple-element.29), channel_id=1, source_target_pairs={{0,4},{1,5},{2,6},{3,7},{4,0},{5,1},{6,2},{7,3},{8,12},{9,13},{10,... | collective-permute-start | bytes 1179656 | tf_op jit(solution)/shard_map/ppermute | solution.py:363
  196.1 5.4 %collective-permute-done.25 = bf16[512,384]{1,0:T(8,128)(2,1)S(1)} collective-permute-done((bf16[512,384]{1,0:T(8,128)(2,1)S(1)}, bf16[512,384]{1,0:T(8,128)(2,1)S(1)}, u32[]{:S(2)}, u32[]{:S(2)}) %collective-permute-start.25) | collective-permute-done | bytes 393248 | tf_op jit(solution)/shard_map/ppermute | solution.py:363
  201.5 2.6 %collective-permute-done.24 = bf16[512,384]{1,0:T(8,128)(2,1)S(1)} collective-permute-done((bf16[512,384]{1,0:T(8,128)(2,1)S(1)}, bf16[512,384]{1,0:T(8,128)(2,1)S(1)}, u32[]{:S(2)}, u32[]{:S(2)}) %collective-permute-start.24) | collective-permute-done | bytes 393248 | tf_op jit(solution)/shard_map/ppermute | solution.py:363
  204.1 9.6 %collective-permute-done.23 = bf16[512,384]{1,0:T(8,128)(2,1)S(1)} collective-permute-done((bf16[512,384]{1,0:T(8,128)(2,1)S(1)}, bf16[512,384]{1,0:T(8,128)(2,1)S(1)}, u32[]{:S(2)}, u32[]{:S(2)}) %collective-permute-start.23) | collective-permute-done | bytes 393248 | tf_op jit(solution)/shard_map/ppermute | solution.py:363
  213.7 2.2 %fusion.6 = bf16[512,384]{1,0:T(8,128)(2,1)} fusion(bf16[512,384]{1,0:T(8,128)(2,1)S(1)} %collective-permute-done.25, bf16[512,384]{1,0:T(8,128)(2,1)S(1)} %collective-permute-done.24, bf16[512,384]{1,0:T(8,128)(2,1)S(1)} %collective-permute-done.23, f32[4,512,384]{2,1,0:T(8,128)} %get-tuple-element.27, bf16[512,384]{1,0:T(8,128)(2,1)S(1)} %pick_rows.1.r0, ...), kind=kLoop, calls=%fused_computation.8 | loop fusion | flops 2162688 | bytes 2754560 | tf_op jit(solution)/shard_map/jit(_where)/select_n | solution.py:421
  (48 shorter events, 0.2 us)
Async XLA Ops:
  0.0 1.1 copy-start.3
  1.1 0.7 copy-start.5
  2.5 13.2 %collective-permute-start.3 = (bf16[512,384]{1,0:T(8,128)(2,1)S(1)}, bf16[512,384]{1,0:T(8,128)(2,1)S(1)}, u32[]{:S(2)}, u32[]{:S(2)}) collective-permute-start(bf16[512,384]{1,0:T(8,128)(2,1)S(1)} %pick_rows.1.r0), channel_id=1, source_target_pairs={{0,2},{1,3},{2,4},{3,5},{4,6},{5,7},{6,0},{7,1},{8,10},{9,11},{10,... | collective-permute-start | bytes 1179656 | tf_op jit(solution)/shard_map/ppermute | solution.py:363
  4.4 20.9 %collective-permute-start.4 = (bf16[512,384]{1,0:T(8,128)(2,1)S(1)}, bf16[512,384]{1,0:T(8,128)(2,1)}, u32[]{:S(2)}, u32[]{:S(2)}) collective-permute-start(bf16[512,384]{1,0:T(8,128)(2,1)S(1)} %pick_rows.1.r0), channel_id=1, source_target_pairs={{0,4},{1,5},{2,6},{3,7},{4,0},{5,1},{6,2},{7,3},{8,12},{9,13},{10,... | collective-permute-start | bytes 1179656 | tf_op jit(solution)/shard_map/ppermute | solution.py:363
  8.0 19.7 %collective-permute-start.5 = (bf16[512,384]{1,0:T(8,128)(2,1)S(1)}, bf16[512,384]{1,0:T(8,128)(2,1)}, u32[]{:S(2)}, u32[]{:S(2)}) collective-permute-start(bf16[512,384]{1,0:T(8,128)(2,1)S(1)} %pick_rows.1.r0), channel_id=1, source_target_pairs={{0,6},{1,7},{2,0},{3,1},{4,2},{5,3},{6,4},{7,5},{8,14},{9,15},{10,... | collective-permute-start | bytes 1179656 | tf_op jit(solution)/shard_map/ppermute | solution.py:363
  9.0 18.7 %collective-permute-start.6 = (bf16[512,384]{1,0:T(8,128)(2,1)S(1)}, bf16[512,384]{1,0:T(8,128)(2,1)S(1)}, u32[]{:S(2)}, u32[]{:S(2)}) collective-permute-start(bf16[512,384]{1,0:T(8,128)(2,1)S(1)} %pick_rows.1.r0), channel_id=1, source_target_pairs={{0,1},{1,0},{2,3},{3,2},{4,5},{5,4},{6,7},{7,6},{8,9},{9,8},{10,11... | collective-permute-start | bytes 1179656 | tf_op jit(solution)/shard_map/ppermute | solution.py:367
  15.7 13.9 %collective-permute-start.7 = (bf16[512,384]{1,0:T(8,128)(2,1)S(1)}, bf16[512,384]{1,0:T(8,128)(2,1)}, u32[]{:S(2)}, u32[]{:S(2)}) collective-permute-start(bf16[512,384]{1,0:T(8,128)(2,1)S(1)} %collective-permute-done.3.r1), channel_id=1, source_target_pairs={{0,1},{1,0},{2,3},{3,2},{4,5},{5,4},{6,7},{7,6},{8,9},{9,8},{10,11... | collective-permute-start | bytes 1179656 | tf_op jit(solution)/shard_map/ppermute | solution.py:367
  15.7 1.1 copy-start.1
  16.8 1.1 copy-start.2
  18.7 0.9 copy-start.7
  19.6 57.8 %collective-permute-start.13 = (bf16[512,768]{1,0:T(8,128)(2,1)S(1)}, bf16[512,768]{1,0:T(8,128)(2,1)S(1)}, u32[]{:S(2)}, u32[]{:S(2)}) collective-permute-start(bf16[512,768]{1,0:T(8,128)(2,1)S(1)} %get-tuple-element.18.refs_4_.refs_12_), channel_id=1, source_target_pairs={{0,32},{8,40},{16,48},{24,56},{32,64},{40,72},{48,80},{56,88},{64,... | collective-permute-start | bytes 2359304 | tf_op jit(solution)/shard_map/ppermute | solution.py:359
  25.4 54.5 %collective-permute-start.14 = (bf16[512,768]{1,0:T(8,128)(2,1)S(1)}, bf16[512,768]{1,0:T(8,128)(2,1)S(1)}, u32[]{:S(2)}, u32[]{:S(2)}) collective-permute-start(bf16[512,768]{1,0:T(8,128)(2,1)S(1)} %get-tuple-element.18.refs_4_.refs_12_), channel_id=1, source_target_pairs={{0,64},{8,72},{16,80},{24,88},{32,96},{40,104},{48,112},{56,120},{... | collective-permute-start | bytes 2359304 | tf_op jit(solution)/shard_map/ppermute | solution.py:359
  27.7 23.8 %collective-permute-start.8 = (bf16[512,384]{1,0:T(8,128)(2,1)}, bf16[512,384]{1,0:T(8,128)(2,1)}, u32[]{:S(2)}, u32[]{:S(2)}) collective-permute-start(bf16[512,384]{1,0:T(8,128)(2,1)} %collective-permute-done.4.r2), channel_id=1, source_target_pairs={{0,1},{1,0},{2,3},{3,2},{4,5},{5,4},{6,7},{7,6},{8,9},{9,8},{10,11... | collective-permute-start | bytes 1179656 | tf_op jit(solution)/shard_map/ppermute | solution.py:367
  27.7 0.7 copy-start.10
  28.4 25.8 %collective-permute-start.9 = (bf16[512,384]{1,0:T(8,128)(2,1)}, bf16[512,384]{1,0:T(8,128)(2,1)}, u32[]{:S(2)}, u32[]{:S(2)}) collective-permute-start(bf16[512,384]{1,0:T(8,128)(2,1)} %collective-permute-done.5.r3), channel_id=1, source_target_pairs={{0,1},{1,0},{2,3},{3,2},{4,5},{5,4},{6,7},{7,6},{8,9},{9,8},{10,11... | collective-permute-start | bytes 1179656 | tf_op jit(solution)/shard_map/ppermute | solution.py:367
  29.6 50.3 %collective-permute-start.15 = (bf16[512,768]{1,0:T(8,128)(2,1)S(1)}, bf16[512,768]{1,0:T(8,128)(2,1)}, u32[]{:S(2)}, u32[]{:S(2)}) collective-permute-start(bf16[512,768]{1,0:T(8,128)(2,1)S(1)} %get-tuple-element.18.refs_4_.refs_12_), channel_id=1, source_target_pairs={{0,96},{8,104},{16,112},{24,120},{32,0},{40,8},{48,16},{56,24},{64... | collective-permute-start | bytes 2359304 | tf_op jit(solution)/shard_map/ppermute | solution.py:359
  41.2 13.8 %copy-start.4 = (f32[3,3072]{1,0:T(4,128)S(1)}, f32[3,3072]{1,0:T(4,128)}, u32[]{:S(2)}) copy-start(f32[3,3072]{1,0:T(4,128)} %mod_ref.1) | copy-start | bytes 110596
  41.2 13.8 %copy-start.12 = (f32[128]{0:T(128)S(1)}, f32[128]{0:T(128)}, u32[]{:S(2)}) copy-start(f32[128]{0:T(128)} %param.18) | copy-start | bytes 1540
  41.2 13.8 %copy-start.13 = (f32[128]{0:T(128)S(1)}, f32[128]{0:T(128)}, u32[]{:S(2)}) copy-start(f32[128]{0:T(128)} %param.19) | copy-start | bytes 1540
  51.4 20.4 %collective-permute-start.2 = (s32[1]{0:T(128)}, s32[1]{0:T(128)}, u32[]{:S(2)}, u32[]{:S(2)}) collective-permute-start(s32[1]{0:T(128)} %param.16), channel_id=1, source_target_pairs={{0,24},{8,0},{16,8},{24,16},{32,56},{40,32},{48,40},{56,48},{64,88... | collective-permute-start | bytes 20 | tf_op jit(solution)/shard_map/ppermute | solution.py:355
  54.2 18.6 %collective-permute-start.1 = (s32[1]{0:T(128)}, s32[1]{0:T(128)}, u32[]{:S(2)}, u32[]{:S(2)}) collective-permute-start(s32[1]{0:T(128)} %param.16), channel_id=1, source_target_pairs={{0,16},{8,24},{16,0},{24,8},{32,48},{40,56},{48,32},{56,40},{64,80... | collective-permute-start | bytes 20 | tf_op jit(solution)/shard_map/ppermute | solution.py:355
  55.0 1.1 copy-start.8
  56.1 1.0 copy-start.11
  57.1 119.7 %slice-start = ((s8[4718592]{0:T(1024)(128)(4,1)}), s8[4194304]{0:T(1024)(128)(4,1)S(1)}, s32[]{:S(2)}) async-start(s8[4718592]{0:T(1024)(128)(4,1)} %bitcast.29), calls=%async_computation | async-start | bytes 8388608
  71.8 41.3 %copy-start.9 = (bf16[512,768]{1,0:T(8,128)(2,1)}, bf16[512,768]{1,0:T(8,128)(2,1)S(1)}, u32[]{:S(2)}) copy-start(bf16[512,768]{1,0:T(8,128)(2,1)S(1)} %get-tuple-element.19.refs_8_.refs_16_) | copy-start | bytes 2359300
  71.8 4.9 %collective-permute-start = (s32[1]{0:T(128)}, s32[1]{0:T(128)}, u32[]{:S(2)}, u32[]{:S(2)}) collective-permute-start(s32[1]{0:T(128)} %param.16), channel_id=1, source_target_pairs={{0,8},{8,16},{16,24},{24,0},{32,40},{40,48},{48,56},{56,32},{64,72... | collective-permute-start | bytes 20 | tf_op jit(solution)/shard_map/ppermute | solution.py:355
  72.8 12.7 %collective-permute-start.10 = (bf16[512,384]{1,0:T(8,128)(2,1)S(1)}, bf16[512,384]{1,0:T(8,128)(2,1)S(1)}, u32[]{:S(2)}, u32[]{:S(2)}) collective-permute-start(bf16[512,384]{1,0:T(8,128)(2,1)S(1)} %get-tuple-element.17.refs_0_), channel_id=1, source_target_pairs={{0,8},{8,16},{16,24},{24,0},{32,40},{40,48},{48,56},{56,32},{64,72... | collective-permute-start | bytes 1179656 | tf_op jit(solution)/shard_map/ppermute | solution.py:355
  76.8 20.5 %collective-permute-start.16 = (bf16[512,768]{1,0:T(8,128)(2,1)S(1)}, bf16[512,768]{1,0:T(8,128)(2,1)S(1)}, u32[]{:S(2)}, u32[]{:S(2)}) collective-permute-start(bf16[512,768]{1,0:T(8,128)(2,1)S(1)} %get-tuple-element.19.refs_8_.refs_16_), channel_id=1, source_target_pairs={{0,32},{8,40},{16,48},{24,56},{32,64},{40,72},{48,80},{56,88},{64,... | collective-permute-start | bytes 2359304 | tf_op jit(solution)/shard_map/ppermute | solution.py:359
  77.4 22.0 %collective-permute-start.17 = (bf16[512,768]{1,0:T(8,128)(2,1)S(1)}, bf16[512,768]{1,0:T(8,128)(2,1)S(1)}, u32[]{:S(2)}, u32[]{:S(2)}) collective-permute-start(bf16[512,768]{1,0:T(8,128)(2,1)S(1)} %get-tuple-element.19.refs_8_.refs_16_), channel_id=1, source_target_pairs={{0,64},{8,72},{16,80},{24,88},{32,96},{40,104},{48,112},{56,120},{... | collective-permute-start | bytes 2359304 | tf_op jit(solution)/shard_map/ppermute | solution.py:359
  79.9 33.2 %collective-permute-start.18 = (bf16[512,768]{1,0:T(8,128)(2,1)S(1)}, bf16[512,768]{1,0:T(8,128)(2,1)S(1)}, u32[]{:S(2)}, u32[]{:S(2)}) collective-permute-start(bf16[512,768]{1,0:T(8,128)(2,1)S(1)} %get-tuple-element.19.refs_8_.refs_16_), channel_id=1, source_target_pairs={{0,96},{8,104},{16,112},{24,120},{32,0},{40,8},{48,16},{56,24},{64... | collective-permute-start | bytes 2359304 | tf_op jit(solution)/shard_map/ppermute | solution.py:359
  79.9 13.0 %collective-permute-start.11 = (bf16[512,384]{1,0:T(8,128)(2,1)S(1)}, bf16[512,384]{1,0:T(8,128)(2,1)S(1)}, u32[]{:S(2)}, u32[]{:S(2)}) collective-permute-start(bf16[512,384]{1,0:T(8,128)(2,1)S(1)} %get-tuple-element.17.refs_0_), channel_id=1, source_target_pairs={{0,16},{8,24},{16,0},{24,8},{32,48},{40,56},{48,32},{56,40},{64,80... | collective-permute-start | bytes 1179656 | tf_op jit(solution)/shard_map/ppermute | solution.py:355
  85.5 10.7 %collective-permute-start.12 = (bf16[512,384]{1,0:T(8,128)(2,1)S(1)}, bf16[512,384]{1,0:T(8,128)(2,1)S(1)}, u32[]{:S(2)}, u32[]{:S(2)}) collective-permute-start(bf16[512,384]{1,0:T(8,128)(2,1)S(1)} %get-tuple-element.17.refs_0_), channel_id=1, source_target_pairs={{0,24},{8,0},{16,8},{24,16},{32,56},{40,32},{48,40},{56,48},{64,88... | collective-permute-start | bytes 1179656 | tf_op jit(solution)/shard_map/ppermute | solution.py:355
  89.1 87.8 %slice-start.1 = ((s8[4718592]{0:T(1024)(128)(4,1)}), s8[524288]{0:T(1024)(128)(4,1)S(1)}, s32[]{:S(2)}) async-start(s8[4718592]{0:T(1024)(128)(4,1)} %bitcast.29), calls=%async_computation.1 | async-start | bytes 1048576
  97.3 15.8 %copy-start.15 = (bf16[512,768]{1,0:T(8,128)(2,1)}, bf16[512,768]{1,0:T(8,128)(2,1)S(1)}, u32[]{:S(2)}) copy-start(bf16[512,768]{1,0:T(8,128)(2,1)S(1)} %collective-permute-done.16.refs_9_.refs_17_) | copy-start | bytes 2359300
  99.4 13.7 %copy-start.16 = (bf16[512,768]{1,0:T(8,128)(2,1)}, bf16[512,768]{1,0:T(8,128)(2,1)S(1)}, u32[]{:S(2)}) copy-start(bf16[512,768]{1,0:T(8,128)(2,1)S(1)} %collective-permute-done.17.refs_10_.refs_18_) | copy-start | bytes 2359300
  113.1 0.9 copy-start.17
  155.0 12.5 %collective-permute-start.19 = (bf16[528,384]{1,0:T(8,128)(2,1)S(1)}, bf16[528,384]{1,0:T(8,128)(2,1)S(1)}, u32[]{:S(2)}, u32[]{:S(2)}) collective-permute-start(bf16[528,384]{1,0:T(8,128)(2,1)S(1)} %get-tuple-element.21), channel_id=1, source_target_pairs={{0,24},{8,0},{16,8},{24,16},{32,56},{40,32},{48,40},{56,48},{64,88... | collective-permute-start | bytes 1216520 | tf_op jit(solution)/shard_map/ppermute | solution.py:355
  155.7 13.8 %collective-permute-start.20 = (bf16[528,384]{1,0:T(8,128)(2,1)S(1)}, bf16[528,384]{1,0:T(8,128)(2,1)S(1)}, u32[]{:S(2)}, u32[]{:S(2)}) collective-permute-start(bf16[528,384]{1,0:T(8,128)(2,1)S(1)} %get-tuple-element.22), channel_id=1, source_target_pairs={{0,16},{8,24},{16,0},{24,8},{32,48},{40,56},{48,32},{56,40},{64,80... | collective-permute-start | bytes 1216520 | tf_op jit(solution)/shard_map/ppermute | solution.py:355
  157.1 19.8 %collective-permute-start.21 = (bf16[528,384]{1,0:T(8,128)(2,1)S(1)}, bf16[528,384]{1,0:T(8,128)(2,1)S(1)}, u32[]{:S(2)}, u32[]{:S(2)}) collective-permute-start(bf16[528,384]{1,0:T(8,128)(2,1)S(1)} %get-tuple-element.23), channel_id=1, source_target_pairs={{0,8},{8,16},{16,24},{24,0},{32,40},{40,48},{48,56},{56,32},{64,72... | collective-permute-start | bytes 1216520 | tf_op jit(solution)/shard_map/ppermute | solution.py:355
  158.3 2.3 %copy-start.6 = (bf16[3072,768]{1,0:T(8,128)(2,1)S(1)}, bf16[3072,768]{1,0:T(8,128)(2,1)}, u32[]{:S(2)}) copy-start(bf16[3072,768]{1,0:T(8,128)(2,1)} %w_ref.1) | copy-start | bytes 14155780
  160.6 1.9 copy-start.14
  162.5 14.4 %copy-start = (bf16[384,3072]{1,0:T(8,128)(2,1)S(1)}, bf16[384,3072]{1,0:T(8,128)(2,1)}, u32[]{:S(2)}) copy-start(bf16[384,3072]{1,0:T(8,128)(2,1)} %wa_ref.3) | copy-start | bytes 7077892
  182.2 4.5 %collective-permute-start.22 = (bf16[4,512,384]{2,1,0:T(8,128)(2,1)S(1)}, bf16[4,512,384]{2,1,0:T(8,128)(2,1)S(1)}, u32[]{:S(2)}, u32[]{:S(2)}) collective-permute-start(bf16[4,512,384]{2,1,0:T(8,128)(2,1)S(1)} %get-tuple-element.26), channel_id=1, source_target_pairs={{0,1},{1,0},{2,3},{3,2},{4,5},{5,4},{6,7},{7,6},{8,9},{9,8},{10,11... | collective-permute-start | bytes 4718600 | tf_op jit(solution)/shard_map/ppermute | solution.py:367
  188.8 12.7 %collective-permute-start.25 = (bf16[512,384]{1,0:T(8,128)(2,1)S(1)}, bf16[512,384]{1,0:T(8,128)(2,1)S(1)}, u32[]{:S(2)}, u32[]{:S(2)}) collective-permute-start(bf16[512,384]{1,0:T(8,128)(2,1)S(1)} %get-tuple-element.30), channel_id=1, source_target_pairs={{0,6},{1,7},{2,0},{3,1},{4,2},{5,3},{6,4},{7,5},{8,14},{9,15},{10,... | collective-permute-start | bytes 1179656 | tf_op jit(solution)/shard_map/ppermute | solution.py:363
  189.0 15.1 %collective-permute-start.24 = (bf16[512,384]{1,0:T(8,128)(2,1)S(1)}, bf16[512,384]{1,0:T(8,128)(2,1)S(1)}, u32[]{:S(2)}, u32[]{:S(2)}) collective-permute-start(bf16[512,384]{1,0:T(8,128)(2,1)S(1)} %get-tuple-element.31), channel_id=1, source_target_pairs={{0,2},{1,3},{2,4},{3,5},{4,6},{5,7},{6,0},{7,1},{8,10},{9,11},{10,... | collective-permute-start | bytes 1179656 | tf_op jit(solution)/shard_map/ppermute | solution.py:363
  191.7 22.0 %collective-permute-start.23 = (bf16[512,384]{1,0:T(8,128)(2,1)S(1)}, bf16[512,384]{1,0:T(8,128)(2,1)S(1)}, u32[]{:S(2)}, u32[]{:S(2)}) collective-permute-start(bf16[512,384]{1,0:T(8,128)(2,1)S(1)} %get-tuple-element.29), channel_id=1, source_target_pairs={{0,4},{1,5},{2,6},{3,7},{4,0},{5,1},{6,2},{7,3},{8,12},{9,13},{10,... | collective-permute-start | bytes 1179656 | tf_op jit(solution)/shard_map/ppermute | solution.py:363

commit v2 on v0

v2 whole, which is shorter than its diff:
```python
import functools
import math

import jax
import jax.numpy as jnp
from jax import lax
from jax.experimental import pallas as pl
from jax.experimental.pallas import tpu as pltpu
from jax.sharding import PartitionSpec as P

HD = 128
BLOCK = 128
RMAX = 4
NZ = 4
SIDE = 4
LSE_ROWS = 16
NOTE_ROWS = 16
PER_US = 1_100_000_000
BF16 = jnp.bfloat16
F32 = jnp.float32
EXP2_SCALE = HD ** (-0.5) * math.log2(math.e)
VMEM = pltpu.VMEM


def spec(space):
    return pl.BlockSpec(memory_space=space)


def in_vmem(a):
    return pltpu.with_memory_space_constraint(a, VMEM)


def in_hbm(a):
    return pltpu.with_memory_space_constraint(a, pltpu.HBM)


def call(kernel, operands, outs, scalars=None, far=(), scratch=(), mib=16, cost=0, name=None):
    specs = [spec(VMEM)] * len(operands) + [spec(pltpu.HBM)] * len(far)
    operands = [in_vmem(a) for a in operands] + [in_hbm(a) for a in far]
    if scalars is not None:
        specs = [spec(pltpu.SMEM)] + specs
        operands = [scalars] + operands
    return pl.pallas_call(
        kernel,
        in_specs=specs,
        out_specs=[spec(VMEM)] * len(outs),
        out_shape=[VMEM(shape, dtype) for shape, dtype in outs],
        scratch_shapes=list(scratch),
        compiler_params=pltpu.CompilerParams(vmem_limit_bytes=mib * 2**20),
        cost_estimate=pl.CostEstimate(flops=cost, bytes_accessed=1000, transcendentals=0),
        name=name,
    )(*operands)


def copies_of(pairs, sems):
    copies = [pltpu.make_async_copy(src, dst, sems.at[n]) for n, (src, dst) in enumerate(pairs)]
    for copy in copies:
        copy.start()
    return copies


def block_at(order, place):
    return pl.ds(pl.multiple_of(order[0, place] * BLOCK, BLOCK), BLOCK)


def pick_rows_kernel(order, hidden, out, sems):
    pairs = [
        (hidden.at[block_at(order, i), :], out.at[pl.ds(i * BLOCK, BLOCK), :]) for i in range(RMAX)
    ]
    for copy in copies_of(pairs, sems):
        copy.wait()


def pick_rows(order, hidden):
    return call(
        pick_rows_kernel, [], [((RMAX * BLOCK, hidden.shape[1]), BF16)], scalars=order, far=[hidden],
        scratch=[pltpu.SemaphoreType.DMA((RMAX,))], name="pick_rows",
    )


def pick_cache_kernel(order, keys, values, rest_ref, old_ref, sems):
    pairs = []
    width = keys.shape[1]
    for i in range(2 * RMAX):
        here, to = block_at(order, (RMAX + i) % (2 * RMAX)), pl.ds(i % RMAX * BLOCK, BLOCK)
        for n, ref in enumerate((keys, values)):
            out = rest_ref if i < RMAX else old_ref
            pairs.append((ref.at[here, :], out.at[to, pl.ds(n * width, width)]))
    for copy in copies_of(pairs, sems):
        copy.wait()


def pick_cache(order, keys, values):
    return call(
        pick_cache_kernel, [], [((RMAX * BLOCK, 2 * keys.shape[1]), BF16)] * 2, scalars=order,
        far=[keys, values], scratch=[pltpu.SemaphoreType.DMA((4 * RMAX,))], name="pick_cache",
    )


def project_kernel(
    place, p0, p1, p2, p3, p4, p5, p6, p7, mod_ref, qg_ref, kg_ref, old_ref, w_ref,
    q_ref, kv_ref, modded_ref, w_vmem, sems,
):
    pieces = (p0, p1, p2, p3, p4, p5, p6, p7)
    z, core, count = place[0], place[1], place[2]
    rows, width = p0.shape
    features = width * len(pieces)
    weight_copies = copies_of([(w_ref.at[n], w_vmem.at[n]) for n in range(3)], sems)
    near = lax.rem(z + NZ - 1 + 2 * core, NZ)
    away = lax.rem(z + NZ + 1 - 2 * core, NZ)
    across = lax.rem(z + 2, NZ)
    homes = [
        zone * 2 + side
        for zone, side in (
            (z, core), (z, 1 - core), (near, core), (near, 1 - core),
            (across, core), (away, 1 - core), (away, core), (across, 1 - core),
        )
    ]
    tall = 32

    def norm(i, carry):
        here = pl.ds(pl.multiple_of(i * tall, tall), tall)
        total = jnp.zeros((tall, width), F32)
        for n in range(8):
            total = total + pieces[n][here, :].astype(F32)
        mean = jnp.sum(total, axis=-1, keepdims=True) * (1.0 / features)
        square = jnp.zeros((tall, width), F32)
        for n in range(8):
            center = pieces[n][here, :].astype(F32) - mean
            square = square + center * center
        spread = jnp.sum(square, axis=-1, keepdims=True) * (1.0 / features)
        inv = lax.rsqrt(spread + 1e-06)
        for n, h in enumerate(homes):
            cols = pl.ds(pl.multiple_of(h * width, 128), width)
            normed = (pieces[n][here, :].astype(F32) - mean) * inv
            out = normed * (1.0 + mod_ref[1:2, cols]) + mod_ref[0:1, cols]
            modded_ref[here, cols] = out.astype(BF16)
        return carry

    lax.fori_loop(0, rows // tall, norm, 0, unroll=2)

    def rms(acc, gain):
        out = []
        for j in range(width // HD):
            v = acc[:, j * HD : (j + 1) * HD]
            scale = lax.rsqrt(jnp.mean(v * v, axis=-1, keepdims=True) + 1e-06)
            out.append(v * scale * gain)
        return jnp.concatenate(out, axis=1)

    slices = [slice(i * 256, (i + 1) * 256) for i in range(rows // 256)]
    fresh = [
        i * 256 + lax.broadcasted_iota(jnp.int32, (256, width), 0) < count * BLOCK
        for i in range(rows // 256)
    ]

    def dot(here, n):
        return jnp.dot(modded_ref[here, :], w_vmem[n], preferred_element_type=F32)

    weight_copies[0].wait()
    for here in slices:
        q_ref[here, :] = rms(dot(here, 0), qg_ref[...]).astype(BF16)
    q_ref[rows : rows + NOTE_ROWS, :] = (
        jnp.full((NOTE_ROWS, width), count, jnp.int32).astype(F32).astype(BF16)
    )
    weight_copies[1].wait()
    for here, live in zip(slices, fresh):
        key = rms(dot(here, 1), kg_ref[...])
        kv_ref[here, :width] = jnp.where(live, key, old_ref[here, :width].astype(F32)).astype(BF16)
    weight_copies[2].wait()
    for here, live in zip(slices, fresh):
        value = dot(here, 2)
        kv_ref[here, width:] = jnp.where(live, value, old_ref[here, width:].astype(F32)).astype(BF16)


def project(place, pieces, modulation, query_gain, key_gain, w_qkv, old):
    rows, width = pieces[0].shape
    features = w_qkv.shape[1]
    return call(
        project_kernel,
        [*pieces, modulation, query_gain.reshape(1, HD), key_gain.reshape(1, HD), old],
        [((rows + NOTE_ROWS, width), BF16), ((rows, 2 * width), BF16), ((rows, features), BF16)],
        scalars=place, far=[w_qkv],
        scratch=[VMEM(w_qkv.shape, BF16), pltpu.SemaphoreType.DMA((3,))], cost=10 * PER_US, name="project",
    )


def mlp_kernel(modded_ref, w_ref, out_ref, w_vmem, sems):
    width = w_ref.shape[1] // 3
    tiles = [slice(j * width, (j + 1) * width) for j in range(3)]
    copies = copies_of(
        [(w_ref.at[:, pl.ds(j * width, width)], w_vmem.at[j]) for j in range(3)], sems
    )
    for j in range(3):
        copies[j].wait()
        for i in range(modded_ref.shape[0] // 256):
            here = slice(i * 256, (i + 1) * 256)
            acc = jnp.dot(modded_ref[here, :], w_vmem[j], preferred_element_type=F32)
            out_ref[here, tiles[j]] = jax.nn.gelu(acc, approximate=True).astype(BF16)


def mlp_in(modded, w_mlp):
    rows, features = modded.shape
    hidden = w_mlp.shape[1]
    return call(
        mlp_kernel, [modded], [((rows, hidden), BF16)], far=[w_mlp],
        scratch=[VMEM((3, features, hidden // 3), BF16), pltpu.SemaphoreType.DMA((3,))],
        cost=5 * PER_US, name="mlp_in",
    )[0]


def attend_kernel(*refs, n_keys, chained, last):
    refs = list(refs)

    def take(n):
        out = refs[:n]
        del refs[:n]
        return out

    q_refs, kv_refs = take(SIDE), take(n_keys)
    o_in, lse_in = take(2) if chained else (None, None)
    out_refs = take(SIDE) if last else None
    o_out, lse_out, qs = take(3)
    rows, width = q_refs[0].shape[0] - NOTE_ROWS, q_refs[0].shape[1]
    slots, heads = rows // BLOCK, width // HD

    starts, live, total = [], [], 0
    for s in range(SIDE):
        count = jnp.max(q_refs[s][rows : rows + NOTE_ROWS, :HD].astype(F32)).astype(jnp.int32)
        starts.append(total)
        live.append(count)
        total = total + count

    for s in range(SIDE):
        for i in range(slots):
            @pl.when(i < live[s])
            def _(s=s, i=i):
                to = pl.ds(pl.multiple_of((starts[s] + i) * BLOCK, BLOCK), BLOCK)
                qs[to, :] = q_refs[s][i * BLOCK : (i + 1) * BLOCK, :]

    def lanes(j):
        return slice(j * HD, (j + 1) * HD)

    def tile(t, carry):
        here = pl.ds(pl.multiple_of(t * 2 * BLOCK, 2 * BLOCK), 2 * BLOCK)

        def score(j):
            q = qs[here, lanes(j)]
            return [
                lax.dot_general(q, kv[:, lanes(j)], (((1,), (1,)), ((), ())), preferred_element_type=F32)
                for kv in kv_refs
            ]

        ahead = score(0)
        for j in range(heads):
            scores = ahead
            if j + 1 < heads:
                ahead = score(j + 1)
            top = functools.reduce(jnp.maximum, [jnp.max(s, axis=-1, keepdims=True) for s in scores])
            top = top * EXP2_SCALE
            if chained:
                lse = lse_in[here, lanes(j)]
                top = jnp.maximum(top, lse[:, :1])
                share = jnp.exp2(lse - top)
                acc = jnp.concatenate([o_in[here, lanes(j)] * share, share], axis=1)
            else:
                acc = jnp.zeros((2 * BLOCK, 2 * HD), F32)
            for s, kv in zip(scores, kv_refs):
                weights = jnp.exp2(s * EXP2_SCALE - top).astype(BF16)
                value = kv[:, width + j * HD : width + (j + 1) * HD]
                value = jnp.concatenate([value, jnp.ones(value.shape, BF16)], axis=1)
                acc = acc + jnp.dot(weights, value, preferred_element_type=F32)
            o_out[here, lanes(j)] = acc[:, :HD] / acc[:, HD:]
            lse_out[here, lanes(j)] = top + jnp.log2(acc[:, HD:])
        return carry

    lax.fori_loop(0, lax.div(total + 1, 2), tile, 0)
    if not last:
        return

    line = lax.broadcasted_iota(jnp.int32, (LSE_ROWS, BLOCK), 0)
    for s in range(SIDE):
        out_refs[s][rows : rows + LSE_ROWS, :] = jnp.zeros((LSE_ROWS, width), BF16)
        for i in range(slots):
            @pl.when(i < live[s])
            def _(s=s, i=i):
                here = pl.ds(pl.multiple_of((starts[s] + i) * BLOCK, BLOCK), BLOCK)
                out_refs[s][i * BLOCK : (i + 1) * BLOCK, :] = o_out[here, :].astype(BF16)
                for j in range(heads):
                    lse = jnp.transpose(lse_out[here, lanes(j)])[:LSE_ROWS, :]
                    high = lse.astype(BF16).astype(F32)
                    mid = (lse - high).astype(BF16).astype(F32)
                    low = lse - high - mid
                    packed = out_refs[s][rows : rows + LSE_ROWS, lanes(j)].astype(F32)
                    part = line - 4 * i
                    packed = jnp.where(part == 0, high, packed)
                    packed = jnp.where(part == 1, mid, packed)
                    packed = jnp.where(part == 2, low, packed)
                    out_refs[s][rows : rows + LSE_ROWS, lanes(j)] = packed.astype(BF16)


def attend(queries, caches, state, last):
    tall, width = queries[0].shape
    rows = tall - NOTE_ROWS
    states = [((SIDE * rows, width), F32)] * 2
    scratch = [VMEM((SIDE * rows, width), BF16)]
    if last:
        outs = [((rows + LSE_ROWS, width), BF16)] * SIDE
        scratch = [VMEM(shape, dtype) for shape, dtype in states] + scratch
    else:
        outs = states
    return call(
        functools.partial(attend_kernel, n_keys=len(caches), chained=bool(state), last=last),
        [*queries, *caches, *state], outs, scratch=scratch, mib=20, cost=9 * PER_US,
        name="attend_last" if last else "attend_first",
    )


def columns(place, n, width):
    z, core = place[0], place[1]
    side = 1 - core if n < NZ else core
    h = lax.rem(z + n % NZ, NZ) * 2 + side
    return pl.ds(pl.multiple_of(h * width, 128), width)


def mlp_out_kernel(place, mlp_ref, w_ref, out_ref):
    for n in range(2 * NZ):
        cols = columns(place, n, out_ref.shape[2])
        out_ref[n] = jnp.dot(mlp_ref[...], w_ref[:, cols], preferred_element_type=F32)


def mlp_out(place, mlp_hidden, w_out):
    rows, hidden = mlp_hidden.shape
    width = w_out.shape[1] // (2 * NZ)
    return call(
        mlp_out_kernel, [mlp_hidden, w_out], [((2 * NZ, rows, width), F32)], scalars=place,
        cost=4 * PER_US, name="mlp_out",
    )[0]


def branch_kernel(place, *refs):
    parts, mlp_ref, w_ref = refs[:4], refs[4], refs[5]
    send_ref, keep_ref, attn_ref = refs[6:]
    rows, width = attn_ref.shape
    for j in range(width // HD):
        cols = slice(j * HD, (j + 1) * HD)
        lses = [p[rows : rows + LSE_ROWS, cols].astype(F32) for p in parts]
        for i in range(rows // BLOCK):
            each = []
            for lse in lses:
                total = lse[4 * i : 4 * i + 1] + lse[4 * i + 1 : 4 * i + 2] + lse[4 * i + 2 : 4 * i + 3]
                each.append(total)
            top = functools.reduce(jnp.maximum, each)
            shares = [jnp.exp2(e - top) for e in each]
            scale = 1.0 / functools.reduce(jnp.add, shares)
            here = slice(i * BLOCK, (i + 1) * BLOCK)
            mixed = jnp.zeros((BLOCK, HD), F32)
            for share, p in zip(shares, parts):
                column = jnp.transpose(jnp.broadcast_to(share * scale, (BLOCK, BLOCK)))
                mixed = mixed + column * p[here, cols].astype(F32)
            attn_ref[here, cols] = mixed.astype(BF16)

    for n in range(2 * NZ):
        out_ref = send_ref if n < NZ else keep_ref
        cols = columns(place, n, width)
        acc = jnp.dot(attn_ref[...], w_ref[:, cols], preferred_element_type=F32) + mlp_ref[n]
        out_ref[n % NZ] = acc.astype(BF16)


def branch(place, parts, mlp_branch, w_attn):
    _, rows, width = mlp_branch.shape
    return call(
        branch_kernel, [*parts, mlp_branch, w_attn], [((NZ, rows, width), BF16)] * 2,
        scalars=place, scratch=[VMEM((rows, width), BF16)], name="branch",
    )


def partner(kind, at, core):
    if kind == "opposite":
        return (at + 2) % 4
    step = 1 if at % 2 == 0 else 3
    if (kind == "second") != (core == 1):
        step = 4 - step
    return (at + step) % 4


def along(axis, kind, a):
    pairs = []
    for y in range(4):
        for x in range(4):
            for h in range(8):
                core = h % 2
                if (axis == "a") == (core == 0):
                    to = partner(kind, y, core) * 4 + x
                else:
                    to = y * 4 + partner(kind, x, core)
                pairs.append(((y * 4 + x) * 8 + h, to * 8 + h))
    return lax.ppermute(a, ("patch", "head"), pairs)


def up_or_down(a):
    return lax.ppermute(
        a, "head", [(z * 2 + c, (z + (1, 3)[c]) % 4 * 2 + c) for z in range(4) for c in range(2)]
    )


def along_z(a, k):
    return lax.ppermute(a, "head", [(z * 2 + c, (z + k) % 4 * 2 + c) for z in range(4) for c in range(2)])


def other_core(a):
    return lax.ppermute(a, "head", [(i, i ^ 1) for i in range(8)])


def ring(axis, a):
    first, second = along(axis, "first", a), along(axis, "second", a)
    return [a, first, second, along(axis, "second", first)]


def body(
    hidden, key_cache, value_cache, block_order, refresh_counts, modulation,
    query_gain, key_gain, w_qkv, w_mlp, w_out_attn, w_out_mlp,
):
    width = hidden.shape[1]
    count = refresh_counts[0]
    head = lax.axis_index("head")
    z, core = head // 2, head % 2
    place = jnp.stack([z, core, count]).astype(jnp.int32)
    w_qkv = jnp.transpose(w_qkv, (1, 0, 2))

    (rows,) = pick_rows(block_order, hidden)
    rest, old = pick_cache(block_order, key_cache, value_cache)
    rows, rest = lax.optimization_barrier((rows, rest))
    beside = other_core(rows)
    near = up_or_down(rows)
    near_beside = up_or_down(beside)
    across = up_or_down(near)
    pieces = [
        rows, beside, near, near_beside, across,
        other_core(near), other_core(near_beside), other_core(across),
    ]
    rest_first, rest_second = along("a", "first", rest), along("a", "second", rest)
    pieces, rest_first, rest_second = lax.optimization_barrier((pieces, rest_first, rest_second))
    rest = [rest, rest_first, rest_second, along("a", "second", rest_first)]

    query, fresh, modded = project(place, pieces, modulation, query_gain, key_gain, w_qkv, old)
    fresh, queries = ring("a", fresh), ring("b", query)
    mlp_hidden = mlp_in(modded, w_mlp)
    queries, mlp_hidden, fresh[1] = lax.optimization_barrier((queries, mlp_hidden, fresh[1]))
    state = attend(queries, rest, [], False)
    parts = attend(queries, fresh, state, True)
    mlp_branch = mlp_out(place, mlp_hidden, w_out_mlp)

    kinds = ("first", "second", "opposite")
    back = [parts[0]] + [along("b", kind, parts[n + 1]) for n, kind in enumerate(kinds)]
    send, keep = branch(place, back, mlp_branch, w_out_attn)
    chip = keep.astype(F32) + other_core(send).astype(F32)
    summed = chip[0]
    for k in (2, 1, 3):
        summed = summed + along_z(chip[k].astype(BF16), k).astype(F32)

    gate = lax.dynamic_slice_in_dim(modulation[2], head * width, width)
    result = (rows.astype(F32) + gate * summed).astype(BF16)
    live = jnp.arange(result.shape[0]) < count * BLOCK
    return jnp.where(live[:, None], result, jnp.zeros((), BF16))


def solution(mesh):
    in_specs = (
        P("patch", "head"), P("patch", "head"), P("patch", "head"), P("patch", None), P("patch"),
        P(), P(), P(),
        P(None, None, "head"), P(None, "head"), P("head", None), P("head", None),
    )
    return jax.shard_map(
        body, mesh=mesh, in_specs=in_specs, out_specs=P("patch", "head"), check_vma=False
    )
```

time: 519 us -> 138 us (0.27)
  matrix products: 143 us -> 0 us
  waiting for transfers between devices: 175 us -> 43.8 us
  local copies, waits for them, and re-layouts: 111 us -> 6.4 us
  other arithmetic: 72.4 us -> 2.81 us
  Pallas kernels: 0 us -> 44.9 us
  starting transfers between devices: 0.31 us -> 36.4 us
  between operations: 14 us -> 0.81 us
    dot_general x19 -> x0, matrix products: 143 us -> none  [the longest x8 62.3 us: attend_block(): jnp.einsum('hqd,khd->hqk', queries, key_heads, preferred_element_type=jnp...]
    all_gather x3 -> x0, waiting for transfers between devices: 140 us -> none  [the longest x1 65.6 us: body(): lax.all_gather(value_patched, 'patch', axis=0, tiled=True)]
    unnamed x38 -> x18, local copies, waits for them, and re-layouts: 84.6 us -> 4.52 us
    reduce_sum x12 -> x0, other arithmetic: 60.8 us -> none  [the longest x8 53 us: attend_block(): acc_total = acc_total * factor + jnp.sum(weights, axis=-1)]
    pallas_call x0 -> x8, Pallas kernels: none -> 44.9 us  [call(): pl.pallas_call(kernel, in_specs=specs, out_specs=[spec(VMEM)] * len(outs)...]
    ppermute x0 -> x23, waiting for transfers between devices: none -> 43.8 us  [the longest x3 16.8 us: along_z(): lax.ppermute(a, 'head', [(z * 2 + c, (z + k) % 4 * 2 + c) for z in range(...]
    ppermute x0 -> x23, starting transfers between devices: none -> 36.4 us  [the longest x12 26.2 us: along(): return lax.ppermute(a, ('patch', 'head'), pairs)]
    unnamed x5 -> x0, waiting for transfers between devices: 35.1 us -> none
  transfers between devices with their start and end apart: 4 -> 23, of which waited for: 4 -> 10; matrix products, arithmetic and copies ran while one was open for 14% -> 1% of each run, Pallas kernels for 0% -> 13%
where the time goes in v2:
time: 138 us; the launch traced here: 135 us
  Pallas kernels  44.9 us (33%)
  waiting for transfers between devices  43.8 us (32%)
  starting transfers between devices  36.4 us (26%)
  local copies, waits for them, and re-layouts  6.4 us (5%)
  other arithmetic  2.81 us (2%)
    pallas_call x8, Pallas kernels, call(): pl.pallas_call(kernel, in_specs=specs, out_specs=[spec(VMEM)] * len(outs)...  44.9 us
    ppermute x12, starting transfers between devices, along(): return lax.ppermute(a, ('patch', 'head'), pairs)  26.2 us
    ppermute x3, waiting for transfers between devices, along_z(): lax.ppermute(a, 'head', [(z * 2 + c, (z + k) % 4 * 2 + c) for z in range(...  16.8 us
    ppermute x3, waiting for transfers between devices, up_or_down(): lax.ppermute(a, 'head', [(z * 2 + c, (z + (1, 3)[c]) % 4 * 2 + c) for z i...  13.5 us
    ppermute x12, waiting for transfers between devices, along(): return lax.ppermute(a, ('patch', 'head'), pairs)  9.19 us
    unnamed x18, local copies, waits for them, and re-layouts  4.52 us
    ppermute x5, waiting for transfers between devices, other_core(): return lax.ppermute(a, 'head', [(i, i ^ 1) for i in range(8)])  4.35 us
    ppermute x3, starting transfers between devices, along_z(): lax.ppermute(a, 'head', [(z * 2 + c, (z + k) % 4 * 2 + c) for z in range(...  3.94 us
  transfers between devices with their start and end apart: 23, of which 10 were waited for; matrix products, arithmetic and copies ran while one was open for 1% of the time, Pallas kernels for 13%

profile of v2, /device:TPU:0, one launch (start us, length us, event | category | flops | bytes accessed | tf_op | source)
XLA Modules:
  0.0 135.2 jit_solution(15195121391292304292)
XLA Ops:
  0.0 0.7 copy-done.2
  0.7 1.6 %pick_rows.1.p0 = bf16[512,384]{1,0:T(8,128)(2,1)S(1)} custom-call(s32[1,8]{1,0:T(1,128)S(1)} %copy-done.2, bf16[1024,384]{1,0:T(8,128)(2,1)} %hidden.1), custom_call_target="tpu_custom_call" | custom-call | bytes 1000 | tf_op jit(solution)/shard_map/pick_rows/pallas_call | solution.py:43
  2.3 2.1 %pick_cache.1 = (bf16[512,768]{1,0:T(8,128)(2,1)S(1)}, bf16[512,768]{1,0:T(8,128)(2,1)S(1)}) custom-call(s32[1,8]{1,0:T(1,128)S(1)} %copy-done.2, bf16[1024,384]{1,0:T(8,128)(2,1)} %keys.1, bf16[1024,384]{1,0:T(8,128)(2,1)} %values.1), custom_call_target="tpu_custom_call" | custom-call | bytes 1000 | tf_op jit(solution)/shard_map/pick_cache/pallas_call | solution.py:43
  4.4 2.1 %collective-permute-start.1 = (bf16[512,384]{1,0:T(8,128)(2,1)S(1)}, bf16[512,384]{1,0:T(8,128)(2,1)}, u32[]{:S(2)}, u32[]{:S(2)}) collective-permute-start(bf16[512,384]{1,0:T(8,128)(2,1)S(1)} %pick_rows.1.p0), channel_id=1, source_target_pairs={{0,2},{1,7},{2,4},{3,1},{4,6},{5,3},{6,0},{7,5},{8,10},{9,15},{10,... | collective-permute-start | bytes 1179656 | tf_op jit(solution)/shard_map/ppermute | solution.py:401
  6.5 1.7 %collective-permute-start = (bf16[512,384]{1,0:T(8,128)(2,1)S(1)}, bf16[512,384]{1,0:T(8,128)(2,1)S(1)}, u32[]{:S(2)}, u32[]{:S(2)}) collective-permute-start(bf16[512,384]{1,0:T(8,128)(2,1)S(1)} %pick_rows.1.p0), channel_id=1, source_target_pairs={{0,1},{1,0},{2,3},{3,2},{4,5},{5,4},{6,7},{7,6},{8,9},{9,8},{10,11... | collective-permute-start | bytes 1179656 | tf_op jit(solution)/shard_map/ppermute | solution.py:411
  8.2 1.6 %collective-permute-start.7 = (bf16[512,768]{1,0:T(8,128)(2,1)S(1)}, bf16[512,768]{1,0:T(8,128)(2,1)S(1)}, u32[]{:S(2)}, u32[]{:S(2)}) collective-permute-start(bf16[512,768]{1,0:T(8,128)(2,1)S(1)} %get-tuple-element.38.refs_4_), channel_id=1, source_target_pairs={{0,32},{1,25},{2,34},{3,27},{4,36},{5,29},{6,38},{7,31},{8,40},{9,... | collective-permute-start | bytes 2359304 | tf_op jit(solution)/shard_map/ppermute | solution.py:397
  9.7 2.2 %collective-permute-start.8 = (bf16[512,768]{1,0:T(8,128)(2,1)S(1)}, bf16[512,768]{1,0:T(8,128)(2,1)S(1)}, u32[]{:S(2)}, u32[]{:S(2)}) collective-permute-start(bf16[512,768]{1,0:T(8,128)(2,1)S(1)} %get-tuple-element.38.refs_4_), channel_id=1, source_target_pairs={{0,96},{1,9},{2,98},{3,11},{4,100},{5,13},{6,102},{7,15},{8,104},{... | collective-permute-start | bytes 2359304 | tf_op jit(solution)/shard_map/ppermute | solution.py:397
  11.9 2.5 %collective-permute-done.1.p2 = bf16[512,384]{1,0:T(8,128)(2,1)} collective-permute-done((bf16[512,384]{1,0:T(8,128)(2,1)S(1)}, bf16[512,384]{1,0:T(8,128)(2,1)}, u32[]{:S(2)}, u32[]{:S(2)}) %collective-permute-start.1) | collective-permute-done | bytes 393248 | tf_op jit(solution)/shard_map/ppermute | solution.py:401
  14.5 0.0 collective-permute-start.3
  14.5 0.0 collective-permute-done.p1
  14.5 1.8 %collective-permute-start.2 = (bf16[512,384]{1,0:T(8,128)(2,1)S(1)}, bf16[512,384]{1,0:T(8,128)(2,1)}, u32[]{:S(2)}, u32[]{:S(2)}) collective-permute-start(bf16[512,384]{1,0:T(8,128)(2,1)S(1)} %collective-permute-done.p1), channel_id=1, source_target_pairs={{0,2},{1,7},{2,4},{3,1},{4,6},{5,3},{6,0},{7,5},{8,10},{9,15},{10,... | collective-permute-start | bytes 1179656 | tf_op jit(solution)/shard_map/ppermute | solution.py:401
  16.3 0.7 copy-done.3
  17.0 0.0 collective-permute-start.4
  17.1 6.7 %collective-permute-done.3.p4 = bf16[512,384]{1,0:T(8,128)(2,1)} collective-permute-done((bf16[512,384]{1,0:T(8,128)(2,1)}, bf16[512,384]{1,0:T(8,128)(2,1)}, u32[]{:S(2)}, u32[]{:S(2)}) %collective-permute-start.3) | collective-permute-done | bytes 393248 | tf_op jit(solution)/shard_map/ppermute | solution.py:401
  23.8 0.0 collective-permute-start.6
  23.8 4.2 %collective-permute-done.2.p3 = bf16[512,384]{1,0:T(8,128)(2,1)} collective-permute-done((bf16[512,384]{1,0:T(8,128)(2,1)S(1)}, bf16[512,384]{1,0:T(8,128)(2,1)}, u32[]{:S(2)}, u32[]{:S(2)}) %collective-permute-start.2) | collective-permute-done | bytes 393248 | tf_op jit(solution)/shard_map/ppermute | solution.py:401
  28.0 0.0 collective-permute-start.5
  28.7 0.1 pad_add_fusion.place
  28.7 0.0 collective-permute-done.4.p5
  28.7 0.0 collective-permute-done.7.refs_5_
  28.7 0.0 collective-permute-done.8.refs_6_
  28.7 0.0 collective-permute-done.6.p7
  28.8 1.3 collective-permute-done.5.p6
  30.1 0.8 copy-done.1
  30.9 1.0 copy-done.4
  31.9 0.7 copy-done.5
  32.5 0.7 copy-done.6
  33.2 10.5 %project.1 = (bf16[528,384]{1,0:T(8,128)(2,1)S(1)}, bf16[512,768]{1,0:T(8,128)(2,1)S(1)}, bf16[512,3072]{1,0:T(8,128)(2,1)S(1)}) custom-call(s32[3]{0:T(128)S(1)} %pad_add_fusion.place, bf16[512,384]{1,0:T(8,128)(2,1)S(1)} %pick_rows.1.p0, bf16[512,384]{1,0:T(8,128)(2,1)S(1)} %copy-done.4, bf16[512,384]{1,0:T(8,128)(2,1)} %collective-permute-done.1.p2, ...), custom_call_target="tpu_custom_call" | custom-call | flops 11000000512 | bytes 1000 | tf_op jit(solution)/shard_map/project/pallas_call | solution.py:43
  43.6 1.6 %collective-permute-start.9 = (bf16[528,384]{1,0:T(8,128)(2,1)S(1)}, bf16[528,384]{1,0:T(8,128)(2,1)S(1)}, u32[]{:S(2)}, u32[]{:S(2)}) collective-permute-start(bf16[528,384]{1,0:T(8,128)(2,1)S(1)} %get-tuple-element.51.refs_0_), channel_id=1, source_target_pairs={{0,8},{1,97},{2,10},{3,99},{4,12},{5,101},{6,14},{7,103},{8,0},{9,... | collective-permute-start | bytes 1216520 | tf_op jit(solution)/shard_map/ppermute | solution.py:397
  45.2 1.6 %collective-permute-start.12 = (bf16[512,768]{1,0:T(8,128)(2,1)S(1)}, bf16[512,768]{1,0:T(8,128)(2,1)S(1)}, u32[]{:S(2)}, u32[]{:S(2)}) collective-permute-start(bf16[512,768]{1,0:T(8,128)(2,1)S(1)} %get-tuple-element.50.refs_4_), channel_id=1, source_target_pairs={{0,32},{1,25},{2,34},{3,27},{4,36},{5,29},{6,38},{7,31},{8,40},{9,... | collective-permute-start | bytes 2359304 | tf_op jit(solution)/shard_map/ppermute | solution.py:397
  46.8 2.2 %collective-permute-start.15 = (bf16[512,768]{1,0:T(8,128)(2,1)S(1)}, bf16[512,768]{1,0:T(8,128)(2,1)S(1)}, u32[]{:S(2)}, u32[]{:S(2)}) collective-permute-start(bf16[512,768]{1,0:T(8,128)(2,1)S(1)} %collective-permute-done.7.refs_5_), channel_id=1, source_target_pairs={{0,96},{1,9},{2,98},{3,11},{4,100},{5,13},{6,102},{7,15},{8,104},{... | collective-permute-start | bytes 2359304 | tf_op jit(solution)/shard_map/ppermute | solution.py:397
  49.0 2.1 %collective-permute-start.10 = (bf16[528,384]{1,0:T(8,128)(2,1)S(1)}, bf16[528,384]{1,0:T(8,128)(2,1)S(1)}, u32[]{:S(2)}, u32[]{:S(2)}) collective-permute-start(bf16[528,384]{1,0:T(8,128)(2,1)S(1)} %get-tuple-element.51.refs_0_), channel_id=1, source_target_pairs={{0,24},{1,33},{2,26},{3,35},{4,28},{5,37},{6,30},{7,39},{8,16},{9,... | collective-permute-start | bytes 1216520 | tf_op jit(solution)/shard_map/ppermute | solution.py:397
  51.1 1.1 collective-permute-start.13
  52.1 0.0 collective-permute-done.9.refs_1_
  52.1 4.4 %collective-permute-start.11 = (bf16[528,384]{1,0:T(8,128)(2,1)S(1)}, bf16[528,384]{1,0:T(8,128)(2,1)S(1)}, u32[]{:S(2)}, u32[]{:S(2)}) collective-permute-start(bf16[528,384]{1,0:T(8,128)(2,1)S(1)} %collective-permute-done.9.refs_1_), channel_id=1, source_target_pairs={{0,24},{1,33},{2,26},{3,35},{4,28},{5,37},{6,30},{7,39},{8,16},{9,... | collective-permute-start | bytes 1216520 | tf_op jit(solution)/shard_map/ppermute | solution.py:397
  56.5 4.7 %mlp_in.1.mlp_ref = bf16[512,768]{1,0:T(8,128)(2,1)S(1)} custom-call(bf16[512,3072]{1,0:T(8,128)(2,1)S(1)} %get-tuple-element.49.modded_ref, bf16[3072,768]{1,0:T(8,128)(2,1)} %w_ref.2), custom_call_target="tpu_custom_call" | custom-call | flops 5500000256 | bytes 1000 | tf_op jit(solution)/shard_map/mlp_in/pallas_call | solution.py:43
  61.2 1.8 %collective-permute-done.12.refs_5_ = bf16[512,768]{1,0:T(8,128)(2,1)S(1)} collective-permute-done((bf16[512,768]{1,0:T(8,128)(2,1)S(1)}, bf16[512,768]{1,0:T(8,128)(2,1)S(1)}, u32[]{:S(2)}, u32[]{:S(2)}) %collective-permute-start.12) | collective-permute-done | bytes 786464 | tf_op jit(solution)/shard_map/ppermute | solution.py:397
  63.0 5.3 %collective-permute-start.14 = (bf16[512,768]{1,0:T(8,128)(2,1)S(1)}, bf16[512,768]{1,0:T(8,128)(2,1)S(1)}, u32[]{:S(2)}, u32[]{:S(2)}) collective-permute-start(bf16[512,768]{1,0:T(8,128)(2,1)S(1)} %collective-permute-done.12.refs_5_), channel_id=1, source_target_pairs={{0,96},{1,9},{2,98},{3,11},{4,100},{5,13},{6,102},{7,15},{8,104},{... | collective-permute-start | bytes 2359304 | tf_op jit(solution)/shard_map/ppermute | solution.py:397
  68.4 0.0 collective-permute-done.10.refs_2_
  68.4 0.0 collective-permute-done.11.refs_3_
  68.4 0.0 collective-permute-done.15.refs_7_
  68.4 0.0 slice-start
  68.4 8.4 %attend_first.1 = (f32[2048,384]{1,0:T(8,128)S(1)}, f32[2048,384]{1,0:T(8,128)S(1)}) custom-call(bf16[528,384]{1,0:T(8,128)(2,1)S(1)} %get-tuple-element.51.refs_0_, bf16[528,384]{1,0:T(8,128)(2,1)S(1)} %collective-permute-done.9.refs_1_, bf16[528,384]{1,0:T(8,128)(2,1)S(1)} %collective-permute-done.10.refs_2_, ...), custom_call_target="tpu_custom_call" | custom-call | flops 9900000256 | bytes 1000 | tf_op jit(solution)/shard_map/attend_first/pallas_call | solution.py:43
  76.8 0.0 collective-permute-done.13.refs_6_
  76.8 1.5 %collective-permute-done.14.refs_7_ = bf16[512,768]{1,0:T(8,128)(2,1)S(1)} collective-permute-done((bf16[512,768]{1,0:T(8,128)(2,1)S(1)}, bf16[512,768]{1,0:T(8,128)(2,1)S(1)}, u32[]{:S(2)}, u32[]{:S(2)}) %collective-permute-start.14) | collective-permute-done | bytes 786464 | tf_op jit(solution)/shard_map/ppermute | solution.py:397
  78.3 10.0 %attend_last.1 = (bf16[528,384]{1,0:T(8,128)(2,1)S(1)}, bf16[528,384]{1,0:T(8,128)(2,1)S(1)}, bf16[528,384]{1,0:T(8,128)(2,1)S(1)}, bf16[528,384]{1,0:T(8,128)(2,1)S(1)}) custom-call(bf16[528,384]{1,0:T(8,128)(2,1)S(1)} %get-tuple-element.51.refs_0_, bf16[528,384]{1,0:T(8,128)(2,1)S(1)} %collective-permute-done.9.refs_1_, ...), custom_call_target="tpu_custom_call" | custom-call | flops 9900000256 | bytes 1000 | tf_op jit(solution)/shard_map/attend_last/pallas_call | solution.py:43
  88.3 0.6 collective-permute-start.16
  88.9 2.3 %collective-permute-start.17 = (bf16[528,384]{1,0:T(8,128)(2,1)S(1)}, bf16[528,384]{1,0:T(8,128)(2,1)S(1)}, u32[]{:S(2)}, u32[]{:S(2)}) collective-permute-start(bf16[528,384]{1,0:T(8,128)(2,1)S(1)} %get-tuple-element.62), channel_id=1, source_target_pairs={{0,24},{1,33},{2,26},{3,35},{4,28},{5,37},{6,30},{7,39},{8,16},{9,... | collective-permute-start | bytes 1216520 | tf_op jit(solution)/shard_map/ppermute | solution.py:397
  91.2 1.3 collective-permute-start.18
  92.5 4.0 %mlp_out.1.refs_4_ = f32[8,512,384]{2,1,0:T(8,128)S(1)} custom-call(s32[3]{0:T(128)S(1)} %pad_add_fusion.place, bf16[512,768]{1,0:T(8,128)(2,1)S(1)} %mlp_in.1.mlp_ref, bf16[768,3072]{1,0:T(8,128)(2,1)S(1)} %bitcast.29), custom_call_target="tpu_custom_call" | custom-call | flops 4400000000 | bytes 1000 | tf_op jit(solution)/shard_map/mlp_out/pallas_call | solution.py:43
  96.5 5.9 %collective-permute-done.17.refs_2_ = bf16[528,384]{1,0:T(8,128)(2,1)S(1)} collective-permute-done((bf16[528,384]{1,0:T(8,128)(2,1)S(1)}, bf16[528,384]{1,0:T(8,128)(2,1)S(1)}, u32[]{:S(2)}, u32[]{:S(2)}) %collective-permute-start.17) | collective-permute-done | bytes 405536 | tf_op jit(solution)/shard_map/ppermute | solution.py:397
  102.4 3.6 %branch.1 = (bf16[4,512,384]{2,1,0:T(8,128)(2,1)S(1)}, bf16[4,512,384]{2,1,0:T(8,128)(2,1)S(1)}) custom-call(s32[3]{0:T(128)S(1)} %pad_add_fusion.place, bf16[528,384]{1,0:T(8,128)(2,1)S(1)} %get-tuple-element.60.refs_0_, bf16[528,384]{1,0:T(8,128)(2,1)S(1)} %collective-permute-done.16.refs_1_, bf16[528,384]{1,0:T(8,128)(2,1)S(1)} %collective-permute-done.17.refs_2_, ...), custom_call_target="tpu_custom_call" | custom-call | bytes 1000 | tf_op jit(solution)/shard_map/branch/pallas_call | solution.py:43
  106.0 0.7 collective-permute-start.19
  106.7 3.0 %collective-permute-done.19 = bf16[4,512,384]{2,1,0:T(8,128)(2,1)S(1)} collective-permute-done((bf16[4,512,384]{2,1,0:T(8,128)(2,1)S(1)}, bf16[4,512,384]{2,1,0:T(8,128)(2,1)S(1)}, u32[]{:S(2)}, u32[]{:S(2)}) %collective-permute-start.19) | collective-permute-done | bytes 1572896 | tf_op jit(solution)/shard_map/ppermute | solution.py:411
  109.7 0.5 convert_add_fusion
  110.2 1.1 slice_bitcast_fusion.3
  111.3 0.7 collective-permute-start.20
  112.0 1.0 collective-permute-start.21
  113.0 2.2 %collective-permute-start.22 = (bf16[512,384]{1,0:T(8,128)(2,1)}, bf16[512,384]{1,0:T(8,128)(2,1)}, u32[]{:S(2)}, u32[]{:S(2)}) collective-permute-start(bf16[512,384]{1,0:T(8,128)(2,1)} %get-tuple-element.70), channel_id=1, source_target_pairs={{0,6},{1,7},{2,0},{3,1},{4,2},{5,3},{6,4},{7,5},{8,14},{9,15},{10,... | collective-permute-start | bytes 1179656 | tf_op jit(solution)/shard_map/ppermute | solution.py:407
  115.2 0.8 slice.18
  116.1 9.0 %collective-permute-done.20 = bf16[512,384]{1,0:T(8,128)(2,1)} collective-permute-done((bf16[512,384]{1,0:T(8,128)(2,1)}, bf16[512,384]{1,0:T(8,128)(2,1)}, u32[]{:S(2)}, u32[]{:S(2)}) %collective-permute-start.20) | collective-permute-done | bytes 393248 | tf_op jit(solution)/shard_map/ppermute | solution.py:407
  125.1 7.8 %collective-permute-done.21 = bf16[512,384]{1,0:T(8,128)(2,1)} collective-permute-done((bf16[512,384]{1,0:T(8,128)(2,1)}, bf16[512,384]{1,0:T(8,128)(2,1)}, u32[]{:S(2)}, u32[]{:S(2)}) %collective-permute-start.21) | collective-permute-done | bytes 393248 | tf_op jit(solution)/shard_map/ppermute | solution.py:407
  132.9 0.0 collective-permute-done.22
  132.9 2.3 %fusion.6 = bf16[512,384]{1,0:T(8,128)(2,1)} fusion(bf16[512,384]{1,0:T(8,128)(2,1)} %collective-permute-done.22, bf16[512,384]{1,0:T(8,128)(2,1)} %collective-permute-done.21, bf16[512,384]{1,0:T(8,128)(2,1)} %collective-permute-done.20, f32[4,512,384]{2,1,0:T(8,128)S(1)} %get-tuple-element.67, bf16[512,384]{1,0:T(8,128)(2,1)S(1)} %pick_rows.1.p0, ...), kind=kLoop, calls=%fused_computation.8 | loop fusion | flops 2162688 | bytes 2754560 | tf_op jit(solution)/shard_map/jit(_where)/select_n | solution.py:464
  (16 shorter events, 0.1 us)
Async XLA Ops:
  0.0 0.7 copy-start.2
  4.4 10.1 %collective-permute-start.1 = (bf16[512,384]{1,0:T(8,128)(2,1)S(1)}, bf16[512,384]{1,0:T(8,128)(2,1)}, u32[]{:S(2)}, u32[]{:S(2)}) collective-permute-start(bf16[512,384]{1,0:T(8,128)(2,1)S(1)} %pick_rows.1.p0), channel_id=1, source_target_pairs={{0,2},{1,7},{2,4},{3,1},{4,6},{5,3},{6,0},{7,5},{8,10},{9,15},{10,... | collective-permute-start | bytes 1179656 | tf_op jit(solution)/shard_map/ppermute | solution.py:401
  6.5 8.0 %collective-permute-start = (bf16[512,384]{1,0:T(8,128)(2,1)S(1)}, bf16[512,384]{1,0:T(8,128)(2,1)S(1)}, u32[]{:S(2)}, u32[]{:S(2)}) collective-permute-start(bf16[512,384]{1,0:T(8,128)(2,1)S(1)} %pick_rows.1.p0), channel_id=1, source_target_pairs={{0,1},{1,0},{2,3},{3,2},{4,5},{5,4},{6,7},{7,6},{8,9},{9,8},{10,11... | collective-permute-start | bytes 1179656 | tf_op jit(solution)/shard_map/ppermute | solution.py:411
  8.2 20.6 %collective-permute-start.7 = (bf16[512,768]{1,0:T(8,128)(2,1)S(1)}, bf16[512,768]{1,0:T(8,128)(2,1)S(1)}, u32[]{:S(2)}, u32[]{:S(2)}) collective-permute-start(bf16[512,768]{1,0:T(8,128)(2,1)S(1)} %get-tuple-element.38.refs_4_), channel_id=1, source_target_pairs={{0,32},{1,25},{2,34},{3,27},{4,36},{5,29},{6,38},{7,31},{8,40},{9,... | collective-permute-start | bytes 2359304 | tf_op jit(solution)/shard_map/ppermute | solution.py:397
  9.7 19.0 %collective-permute-start.8 = (bf16[512,768]{1,0:T(8,128)(2,1)S(1)}, bf16[512,768]{1,0:T(8,128)(2,1)S(1)}, u32[]{:S(2)}, u32[]{:S(2)}) collective-permute-start(bf16[512,768]{1,0:T(8,128)(2,1)S(1)} %get-tuple-element.38.refs_4_), channel_id=1, source_target_pairs={{0,96},{1,9},{2,98},{3,11},{4,100},{5,13},{6,102},{7,15},{8,104},{... | collective-permute-start | bytes 2359304 | tf_op jit(solution)/shard_map/ppermute | solution.py:397
  14.5 9.3 %collective-permute-start.3 = (bf16[512,384]{1,0:T(8,128)(2,1)}, bf16[512,384]{1,0:T(8,128)(2,1)}, u32[]{:S(2)}, u32[]{:S(2)}) collective-permute-start(bf16[512,384]{1,0:T(8,128)(2,1)} %collective-permute-done.1.p2), channel_id=1, source_target_pairs={{0,2},{1,7},{2,4},{3,1},{4,6},{5,3},{6,0},{7,5},{8,10},{9,15},{10,... | collective-permute-start | bytes 1179656 | tf_op jit(solution)/shard_map/ppermute | solution.py:401
  14.5 13.5 %collective-permute-start.2 = (bf16[512,384]{1,0:T(8,128)(2,1)S(1)}, bf16[512,384]{1,0:T(8,128)(2,1)}, u32[]{:S(2)}, u32[]{:S(2)}) collective-permute-start(bf16[512,384]{1,0:T(8,128)(2,1)S(1)} %collective-permute-done.p1), channel_id=1, source_target_pairs={{0,2},{1,7},{2,4},{3,1},{4,6},{5,3},{6,0},{7,5},{8,10},{9,15},{10,... | collective-permute-start | bytes 1179656 | tf_op jit(solution)/shard_map/ppermute | solution.py:401
  16.3 0.7 copy-start.3
  17.0 11.7 %collective-permute-start.4 = (bf16[512,384]{1,0:T(8,128)(2,1)}, bf16[512,384]{1,0:T(8,128)(2,1)}, u32[]{:S(2)}, u32[]{:S(2)}) collective-permute-start(bf16[512,384]{1,0:T(8,128)(2,1)} %collective-permute-done.1.p2), channel_id=1, source_target_pairs={{0,1},{1,0},{2,3},{3,2},{4,5},{5,4},{6,7},{7,6},{8,9},{9,8},{10,11... | collective-permute-start | bytes 1179656 | tf_op jit(solution)/shard_map/ppermute | solution.py:411
  23.8 5.0 %collective-permute-start.6 = (bf16[512,384]{1,0:T(8,128)(2,1)}, bf16[512,384]{1,0:T(8,128)(2,1)}, u32[]{:S(2)}, u32[]{:S(2)}) collective-permute-start(bf16[512,384]{1,0:T(8,128)(2,1)} %collective-permute-done.3.p4), channel_id=1, source_target_pairs={{0,1},{1,0},{2,3},{3,2},{4,5},{5,4},{6,7},{7,6},{8,9},{9,8},{10,11... | collective-permute-start | bytes 1179656 | tf_op jit(solution)/shard_map/ppermute | solution.py:411
  28.0 2.1 %collective-permute-start.5 = (bf16[512,384]{1,0:T(8,128)(2,1)}, bf16[512,384]{1,0:T(8,128)(2,1)}, u32[]{:S(2)}, u32[]{:S(2)}) collective-permute-start(bf16[512,384]{1,0:T(8,128)(2,1)} %collective-permute-done.2.p3), channel_id=1, source_target_pairs={{0,1},{1,0},{2,3},{3,2},{4,5},{5,4},{6,7},{7,6},{8,9},{9,8},{10,11... | collective-permute-start | bytes 1179656 | tf_op jit(solution)/shard_map/ppermute | solution.py:411
  30.1 0.8 copy-start.1
  30.9 1.0 copy-start.4
  31.9 0.7 copy-start.5
  32.5 0.7 copy-start.6
  43.6 8.5 %collective-permute-start.9 = (bf16[528,384]{1,0:T(8,128)(2,1)S(1)}, bf16[528,384]{1,0:T(8,128)(2,1)S(1)}, u32[]{:S(2)}, u32[]{:S(2)}) collective-permute-start(bf16[528,384]{1,0:T(8,128)(2,1)S(1)} %get-tuple-element.51.refs_0_), channel_id=1, source_target_pairs={{0,8},{1,97},{2,10},{3,99},{4,12},{5,101},{6,14},{7,103},{8,0},{9,... | collective-permute-start | bytes 1216520 | tf_op jit(solution)/shard_map/ppermute | solution.py:397
  45.2 17.8 %collective-permute-start.12 = (bf16[512,768]{1,0:T(8,128)(2,1)S(1)}, bf16[512,768]{1,0:T(8,128)(2,1)S(1)}, u32[]{:S(2)}, u32[]{:S(2)}) collective-permute-start(bf16[512,768]{1,0:T(8,128)(2,1)S(1)} %get-tuple-element.50.refs_4_), channel_id=1, source_target_pairs={{0,32},{1,25},{2,34},{3,27},{4,36},{5,29},{6,38},{7,31},{8,40},{9,... | collective-permute-start | bytes 2359304 | tf_op jit(solution)/shard_map/ppermute | solution.py:397
  46.8 21.6 %collective-permute-start.15 = (bf16[512,768]{1,0:T(8,128)(2,1)S(1)}, bf16[512,768]{1,0:T(8,128)(2,1)S(1)}, u32[]{:S(2)}, u32[]{:S(2)}) collective-permute-start(bf16[512,768]{1,0:T(8,128)(2,1)S(1)} %collective-permute-done.7.refs_5_), channel_id=1, source_target_pairs={{0,96},{1,9},{2,98},{3,11},{4,100},{5,13},{6,102},{7,15},{8,104},{... | collective-permute-start | bytes 2359304 | tf_op jit(solution)/shard_map/ppermute | solution.py:397
  49.0 19.4 %collective-permute-start.10 = (bf16[528,384]{1,0:T(8,128)(2,1)S(1)}, bf16[528,384]{1,0:T(8,128)(2,1)S(1)}, u32[]{:S(2)}, u32[]{:S(2)}) collective-permute-start(bf16[528,384]{1,0:T(8,128)(2,1)S(1)} %get-tuple-element.51.refs_0_), channel_id=1, source_target_pairs={{0,24},{1,33},{2,26},{3,35},{4,28},{5,37},{6,30},{7,39},{8,16},{9,... | collective-permute-start | bytes 1216520 | tf_op jit(solution)/shard_map/ppermute | solution.py:397
  51.1 25.8 %collective-permute-start.13 = (bf16[512,768]{1,0:T(8,128)(2,1)S(1)}, bf16[512,768]{1,0:T(8,128)(2,1)S(1)}, u32[]{:S(2)}, u32[]{:S(2)}) collective-permute-start(bf16[512,768]{1,0:T(8,128)(2,1)S(1)} %get-tuple-element.50.refs_4_), channel_id=1, source_target_pairs={{0,96},{1,9},{2,98},{3,11},{4,100},{5,13},{6,102},{7,15},{8,104},{... | collective-permute-start | bytes 2359304 | tf_op jit(solution)/shard_map/ppermute | solution.py:397
  52.1 16.3 %collective-permute-start.11 = (bf16[528,384]{1,0:T(8,128)(2,1)S(1)}, bf16[528,384]{1,0:T(8,128)(2,1)S(1)}, u32[]{:S(2)}, u32[]{:S(2)}) collective-permute-start(bf16[528,384]{1,0:T(8,128)(2,1)S(1)} %collective-permute-done.9.refs_1_), channel_id=1, source_target_pairs={{0,24},{1,33},{2,26},{3,35},{4,28},{5,37},{6,30},{7,39},{8,16},{9,... | collective-permute-start | bytes 1216520 | tf_op jit(solution)/shard_map/ppermute | solution.py:397
  63.0 15.3 %collective-permute-start.14 = (bf16[512,768]{1,0:T(8,128)(2,1)S(1)}, bf16[512,768]{1,0:T(8,128)(2,1)S(1)}, u32[]{:S(2)}, u32[]{:S(2)}) collective-permute-start(bf16[512,768]{1,0:T(8,128)(2,1)S(1)} %collective-permute-done.12.refs_5_), channel_id=1, source_target_pairs={{0,96},{1,9},{2,98},{3,11},{4,100},{5,13},{6,102},{7,15},{8,104},{... | collective-permute-start | bytes 2359304 | tf_op jit(solution)/shard_map/ppermute | solution.py:397
  68.4 24.1 %slice-start = ((s8[4718592]{0:T(1024)(128)(4,1)}), s8[4194304]{0:T(1024)(128)(4,1)S(1)}, s32[]{:S(2)}) async-start(s8[4718592]{0:T(1024)(128)(4,1)} %bitcast.28), calls=%async_computation | async-start | bytes 8388608
  78.3 14.2 %slice-start.1 = ((s8[4718592]{0:T(1024)(128)(4,1)}), s8[524288]{0:T(1024)(128)(4,1)S(1)}, s32[]{:S(2)}) async-start(s8[4718592]{0:T(1024)(128)(4,1)} %bitcast.28), calls=%async_computation.1 | async-start | bytes 1048576
  88.3 8.2 %collective-permute-start.16 = (bf16[528,384]{1,0:T(8,128)(2,1)S(1)}, bf16[528,384]{1,0:T(8,128)(2,1)S(1)}, u32[]{:S(2)}, u32[]{:S(2)}) collective-permute-start(bf16[528,384]{1,0:T(8,128)(2,1)S(1)} %get-tuple-element.61), channel_id=1, source_target_pairs={{0,8},{1,97},{2,10},{3,99},{4,12},{5,101},{6,14},{7,103},{8,0},{9,... | collective-permute-start | bytes 1216520 | tf_op jit(solution)/shard_map/ppermute | solution.py:397
  88.9 13.5 %collective-permute-start.17 = (bf16[528,384]{1,0:T(8,128)(2,1)S(1)}, bf16[528,384]{1,0:T(8,128)(2,1)S(1)}, u32[]{:S(2)}, u32[]{:S(2)}) collective-permute-start(bf16[528,384]{1,0:T(8,128)(2,1)S(1)} %get-tuple-element.62), channel_id=1, source_target_pairs={{0,24},{1,33},{2,26},{3,35},{4,28},{5,37},{6,30},{7,39},{8,16},{9,... | collective-permute-start | bytes 1216520 | tf_op jit(solution)/shard_map/ppermute | solution.py:397
  91.2 11.2 %copy-start = (bf16[384,3072]{1,0:T(8,128)(2,1)S(1)}, bf16[384,3072]{1,0:T(8,128)(2,1)}, u32[]{:S(2)}) copy-start(bf16[384,3072]{1,0:T(8,128)(2,1)} %refs_5_.1) | copy-start | bytes 7077892
  91.2 11.2 %collective-permute-start.18 = (bf16[528,384]{1,0:T(8,128)(2,1)S(1)}, bf16[528,384]{1,0:T(8,128)(2,1)S(1)}, u32[]{:S(2)}, u32[]{:S(2)}) collective-permute-start(bf16[528,384]{1,0:T(8,128)(2,1)S(1)} %get-tuple-element.63), channel_id=1, source_target_pairs={{0,16},{1,65},{2,18},{3,67},{4,20},{5,69},{6,22},{7,71},{8,24},{9,... | collective-permute-start | bytes 1216520 | tf_op jit(solution)/shard_map/ppermute | solution.py:397
  106.0 3.8 %collective-permute-start.19 = (bf16[4,512,384]{2,1,0:T(8,128)(2,1)S(1)}, bf16[4,512,384]{2,1,0:T(8,128)(2,1)S(1)}, u32[]{:S(2)}, u32[]{:S(2)}) collective-permute-start(bf16[4,512,384]{2,1,0:T(8,128)(2,1)S(1)} %get-tuple-element.66), channel_id=1, source_target_pairs={{0,1},{1,0},{2,3},{3,2},{4,5},{5,4},{6,7},{7,6},{8,9},{9,8},{10,11... | collective-permute-start | bytes 4718600 | tf_op jit(solution)/shard_map/ppermute | solution.py:411
  111.3 13.8 %collective-permute-start.20 = (bf16[512,384]{1,0:T(8,128)(2,1)}, bf16[512,384]{1,0:T(8,128)(2,1)}, u32[]{:S(2)}, u32[]{:S(2)}) collective-permute-start(bf16[512,384]{1,0:T(8,128)(2,1)} %get-tuple-element.69), channel_id=1, source_target_pairs={{0,4},{1,5},{2,6},{3,7},{4,0},{5,1},{6,2},{7,3},{8,12},{9,13},{10,... | collective-permute-start | bytes 1179656 | tf_op jit(solution)/shard_map/ppermute | solution.py:407
  112.0 20.9 %collective-permute-start.21 = (bf16[512,384]{1,0:T(8,128)(2,1)}, bf16[512,384]{1,0:T(8,128)(2,1)}, u32[]{:S(2)}, u32[]{:S(2)}) collective-permute-start(bf16[512,384]{1,0:T(8,128)(2,1)} %get-tuple-element.71), channel_id=1, source_target_pairs={{0,2},{1,3},{2,4},{3,5},{4,6},{5,7},{6,0},{7,1},{8,10},{9,11},{10,... | collective-permute-start | bytes 1179656 | tf_op jit(solution)/shard_map/ppermute | solution.py:407
  113.0 19.9 %collective-permute-start.22 = (bf16[512,384]{1,0:T(8,128)(2,1)}, bf16[512,384]{1,0:T(8,128)(2,1)}, u32[]{:S(2)}, u32[]{:S(2)}) collective-permute-start(bf16[512,384]{1,0:T(8,128)(2,1)} %get-tuple-element.70), channel_id=1, source_target_pairs={{0,6},{1,7},{2,0},{3,1},{4,2},{5,3},{6,4},{7,5},{8,14},{9,15},{10,... | collective-permute-start | bytes 1179656 | tf_op jit(solution)/shard_map/ppermute | solution.py:407

commit v3 on v2

--- a/solution.py
+++ b/solution.py
@@ -63,24 +63,11 @@
     return pl.ds(pl.multiple_of(order[0, place] * BLOCK, BLOCK), BLOCK)
 
 
-def pick_rows_kernel(order, hidden, out, sems):
-    pairs = [
-        (hidden.at[block_at(order, i), :], out.at[pl.ds(i * BLOCK, BLOCK), :]) for i in range(RMAX)
-    ]
-    for copy in copies_of(pairs, sems):
-        copy.wait()
-
-
-def pick_rows(order, hidden):
-    return call(
-        pick_rows_kernel, [], [((RMAX * BLOCK, hidden.shape[1]), BF16)], scalars=order, far=[hidden],
-        scratch=[pltpu.SemaphoreType.DMA((RMAX,))], name="pick_rows",
-    )
-
-
-def pick_cache_kernel(order, keys, values, rest_ref, old_ref, sems):
+def pick_kernel(order, hidden, keys, values, rows_ref, rest_ref, old_ref, sems):
     pairs = []
     width = keys.shape[1]
+    for i in range(RMAX):
+        pairs.append((hidden.at[block_at(order, i), :], rows_ref.at[pl.ds(i * BLOCK, BLOCK), :]))
     for i in range(2 * RMAX):
         here, to = block_at(order, (RMAX + i) % (2 * RMAX)), pl.ds(i % RMAX * BLOCK, BLOCK)
         for n, ref in enumerate((keys, values)):
@@ -90,32 +77,33 @@
         copy.wait()
 
 
-def pick_cache(order, keys, values):
+def pick(order, hidden, keys, values):
+    tall, width = RMAX * BLOCK, hidden.shape[1]
     return call(
-        pick_cache_kernel, [], [((RMAX * BLOCK, 2 * keys.shape[1]), BF16)] * 2, scalars=order,
-        far=[keys, values], scratch=[pltpu.SemaphoreType.DMA((4 * RMAX,))], name="pick_cache",
+        pick_kernel, [], [((tall, width), BF16)] + [((tall, 2 * width), BF16)] * 2, scalars=order,
+        far=[hidden, keys, values], scratch=[pltpu.SemaphoreType.DMA((5 * RMAX,))], name="pick",
     )
 
 
 def project_kernel(
-    place, p0, p1, p2, p3, p4, p5, p6, p7, mod_ref, qg_ref, kg_ref, old_ref, w_ref,
-    q_ref, kv_ref, modded_ref, w_vmem, sems,
+    place, p0, p1, p2, p3, p4, p5, p6, p7, old_ref, mod_far, qg_far, kg_far, w_ref,
+    q_ref, kv_ref, modded_ref, mod_ref, qg_ref, kg_ref, w_vmem, sems,
 ):
     pieces = (p0, p1, p2, p3, p4, p5, p6, p7)
     z, core, count = place[0], place[1], place[2]
     rows, width = p0.shape
     features = width * len(pieces)
-    weight_copies = copies_of([(w_ref.at[n], w_vmem.at[n]) for n in range(3)], sems)
+    mod_copy, *weight_copies, qg_copy, kg_copy = copies_of(
+        [(mod_far, mod_ref)] + [(w_ref.at[n], w_vmem.at[n]) for n in range(3)]
+        + [(qg_far, qg_ref), (kg_far, kg_ref)],
+        sems,
+    )
     near = lax.rem(z + NZ - 1 + 2 * core, NZ)
     away = lax.rem(z + NZ + 1 - 2 * core, NZ)
     across = lax.rem(z + 2, NZ)
-    homes = [
-        zone * 2 + side
-        for zone, side in (
-            (z, core), (z, 1 - core), (near, core), (near, 1 - core),
-            (across, core), (away, 1 - core), (away, core), (across, 1 - core),
-        )
-    ]
+    homes = [zone * 2 + core for zone in (z, near, away, across)]
+    homes += [zone * 2 + 1 - core for zone in (z, away, near, across)]
+    mod_copy.wait()
     tall = 32
 
     def norm(i, carry):
@@ -139,37 +127,34 @@
 
     lax.fori_loop(0, rows // tall, norm, 0, unroll=2)
 
-    def rms(acc, gain):
-        out = []
-        for j in range(width // HD):
-            v = acc[:, j * HD : (j + 1) * HD]
-            scale = lax.rsqrt(jnp.mean(v * v, axis=-1, keepdims=True) + 1e-06)
-            out.append(v * scale * gain)
-        return jnp.concatenate(out, axis=1)
-
-    slices = [slice(i * 256, (i + 1) * 256) for i in range(rows // 256)]
-    fresh = [
-        i * 256 + lax.broadcasted_iota(jnp.int32, (256, width), 0) < count * BLOCK
-        for i in range(rows // 256)
-    ]
-
-    def dot(here, n):
-        return jnp.dot(modded_ref[here, :], w_vmem[n], preferred_element_type=F32)
-
-    weight_copies[0].wait()
-    for here in slices:
-        q_ref[here, :] = rms(dot(here, 0), qg_ref[...]).astype(BF16)
+    def rms(v, gain):
+        scale = lax.rsqrt(jnp.mean(v * v, axis=-1, keepdims=True) + 1e-06)
+        return v * scale * gain
+
+    heads = width // HD
+    waits = {0: [weight_copies[0], qg_copy, kg_copy], 2: [weight_copies[1]], 6: [weight_copies[2]]}
+    for first in range(0, 3 * heads, 2):
+        pair = range(first, min(first + 2, 3 * heads))
+        for copy in waits.get(first, ()):
+            copy.wait()
+        for i in range(rows // 256):
+            here = slice(i * 256, (i + 1) * 256)
+            weights = [w_vmem[h // heads][:, h % heads * HD : (h % heads + 1) * HD] for h in pair]
+            acc = jnp.dot(
+                modded_ref[here, :], jnp.concatenate(weights, axis=1), preferred_element_type=F32
+            )
+            live = i * 256 + lax.broadcasted_iota(jnp.int32, (256, HD), 0) < count * BLOCK
+            for n, h in enumerate(pair):
+                v = acc[:, n * HD : (n + 1) * HD]
+                if h < heads:
+                    q_ref[here, h * HD : (h + 1) * HD] = rms(v, qg_ref[...]).astype(BF16)
+                else:
+                    cols = slice((h - heads) * HD, (h - heads + 1) * HD)
+                    v = rms(v, kg_ref[...]) if h < 2 * heads else v
+                    kv_ref[here, cols] = jnp.where(live, v, old_ref[here, cols].astype(F32)).astype(BF16)
     q_ref[rows : rows + NOTE_ROWS, :] = (
         jnp.full((NOTE_ROWS, width), count, jnp.int32).astype(F32).astype(BF16)
     )
-    weight_copies[1].wait()
-    for here, live in zip(slices, fresh):
-        key = rms(dot(here, 1), kg_ref[...])
-        kv_ref[here, :width] = jnp.where(live, key, old_ref[here, :width].astype(F32)).astype(BF16)
-    weight_copies[2].wait()
-    for here, live in zip(slices, fresh):
-        value = dot(here, 2)
-        kv_ref[here, width:] = jnp.where(live, value, old_ref[here, width:].astype(F32)).astype(BF16)
 
 
 def project(place, pieces, modulation, query_gain, key_gain, w_qkv, old):
@@ -177,10 +162,14 @@
     features = w_qkv.shape[1]
     return call(
         project_kernel,
-        [*pieces, modulation, query_gain.reshape(1, HD), key_gain.reshape(1, HD), old],
+        [*pieces, old],
         [((rows + NOTE_ROWS, width), BF16), ((rows, 2 * width), BF16), ((rows, features), BF16)],
-        scalars=place, far=[w_qkv],
-        scratch=[VMEM(w_qkv.shape, BF16), pltpu.SemaphoreType.DMA((3,))], cost=10 * PER_US, name="project",
+        scalars=place, far=[modulation, query_gain.reshape(1, HD), key_gain.reshape(1, HD), w_qkv],
+        scratch=[
+            VMEM(modulation.shape, F32), VMEM((1, HD), F32), VMEM((1, HD), F32), VMEM(w_qkv.shape, BF16),
+            pltpu.SemaphoreType.DMA((6,)),
+        ],
+        cost=10 * PER_US, name="project",
     )
 
 
@@ -208,7 +197,7 @@
     )[0]
 
 
-def attend_kernel(*refs, n_keys, chained, last):
+def attend_kernel(*refs, n_keys, chained):
     refs = list(refs)
 
     def take(n):
@@ -218,7 +207,7 @@
 
     q_refs, kv_refs = take(SIDE), take(n_keys)
     o_in, lse_in = take(2) if chained else (None, None)
-    out_refs = take(SIDE) if last else None
+    out_refs = take(SIDE) if chained else None
     o_out, lse_out, qs = take(3)
     rows, width = q_refs[0].shape[0] - NOTE_ROWS, q_refs[0].shape[1]
     slots, heads = rows // BLOCK, width // HD
@@ -240,8 +229,8 @@
     def lanes(j):
         return slice(j * HD, (j + 1) * HD)
 
-    def tile(t, carry):
-        here = pl.ds(pl.multiple_of(t * 2 * BLOCK, 2 * BLOCK), 2 * BLOCK)
+    def tile(at, tall):
+        here = pl.ds(pl.multiple_of(at * BLOCK, BLOCK), tall)
 
         def score(j):
             q = qs[here, lanes(j)]
@@ -263,7 +252,7 @@
                 share = jnp.exp2(lse - top)
                 acc = jnp.concatenate([o_in[here, lanes(j)] * share, share], axis=1)
             else:
-                acc = jnp.zeros((2 * BLOCK, 2 * HD), F32)
+                acc = jnp.zeros((tall, 2 * HD), F32)
             for s, kv in zip(scores, kv_refs):
                 weights = jnp.exp2(s * EXP2_SCALE - top).astype(BF16)
                 value = kv[:, width + j * HD : width + (j + 1) * HD]
@@ -271,10 +260,21 @@
                 acc = acc + jnp.dot(weights, value, preferred_element_type=F32)
             o_out[here, lanes(j)] = acc[:, :HD] / acc[:, HD:]
             lse_out[here, lanes(j)] = top + jnp.log2(acc[:, HD:])
+
+    big = lax.div(total, 4)
+    done = 4 * big
+
+    def tall_tile(t, carry):
+        tile(4 * t, 4 * BLOCK)
         return carry
 
-    lax.fori_loop(0, lax.div(total + 1, 2), tile, 0)
-    if not last:
+    def short_tile(t, carry):
+        tile(done + 2 * t, 2 * BLOCK)
+        return carry
+
+    lax.fori_loop(0, big, tall_tile, 0)
+    lax.fori_loop(0, lax.div(total - done + 1, 2), short_tile, 0)
+    if not chained:
         return
 
     line = lax.broadcasted_iota(jnp.int32, (LSE_ROWS, BLOCK), 0)
@@ -298,28 +298,35 @@
                     out_refs[s][rows : rows + LSE_ROWS, lanes(j)] = packed.astype(BF16)
 
 
-def attend(queries, caches, state, last):
+def attend(queries, caches, state=()):
     tall, width = queries[0].shape
     rows = tall - NOTE_ROWS
-    states = [((SIDE * rows, width), F32)] * 2
-    scratch = [VMEM((SIDE * rows, width), BF16)]
-    if last:
+    most = SIDE * rows + BLOCK
+    states = [((most, width), F32)] * 2
+    scratch = [VMEM((most, width), BF16)]
+    if state:
         outs = [((rows + LSE_ROWS, width), BF16)] * SIDE
         scratch = [VMEM(shape, dtype) for shape, dtype in states] + scratch
     else:
         outs = states
     return call(
-        functools.partial(attend_kernel, n_keys=len(caches), chained=bool(state), last=last),
-        [*queries, *caches, *state], outs, scratch=scratch, mib=20, cost=9 * PER_US,
-        name="attend_last" if last else "attend_first",
-    )
+        functools.partial(attend_kernel, n_keys=len(caches), chained=bool(state)),
+        [*queries, *caches, *state], outs, scratch=scratch, mib=24, cost=9 * PER_US if state else 0,
+        name="attend_last" if state else "attend_first",
+    )
+
+
+CHUNKS = ("across", "near", "away", "own")
 
 
 def columns(place, n, width):
     z, core = place[0], place[1]
-    side = 1 - core if n < NZ else core
-    h = lax.rem(z + n % NZ, NZ) * 2 + side
-    return pl.ds(pl.multiple_of(h * width, 128), width)
+    step = lax.rem(1 + 2 * core, NZ)
+    if n >= NZ:
+        step = NZ - step
+    zone = lax.rem(z + (2, step, NZ - step, 0)[n % NZ], NZ)
+    side = core if n < NZ else 1 - core
+    return pl.ds(pl.multiple_of((zone * 2 + side) * width, 128), width)
 
 
 def mlp_out_kernel(place, mlp_ref, w_ref, out_ref):
@@ -337,9 +344,8 @@
     )[0]
 
 
-def branch_kernel(place, *refs):
-    parts, mlp_ref, w_ref = refs[:4], refs[4], refs[5]
-    send_ref, keep_ref, attn_ref = refs[6:]
+def mix_kernel(p0, p1, p2, p3, attn_ref):
+    parts = (p0, p1, p2, p3)
     rows, width = attn_ref.shape
     for j in range(width // HD):
         cols = slice(j * HD, (j + 1) * HD)
@@ -359,19 +365,53 @@
                 mixed = mixed + column * p[here, cols].astype(F32)
             attn_ref[here, cols] = mixed.astype(BF16)
 
-    for n in range(2 * NZ):
-        out_ref = send_ref if n < NZ else keep_ref
+
+def chunk_dots(place, k, attn_ref, mlp_ref, w_ref, send_ref, keep_ref):
+    width = attn_ref.shape[1]
+    for n, out_ref in ((NZ + k, send_ref), (k, keep_ref)):
         cols = columns(place, n, width)
         acc = jnp.dot(attn_ref[...], w_ref[:, cols], preferred_element_type=F32) + mlp_ref[n]
-        out_ref[n % NZ] = acc.astype(BF16)
-
-
-def branch(place, parts, mlp_branch, w_attn):
+        out_ref[...] = acc.astype(BF16)
+
+
+def branch_first_kernel(place, p0, p1, p2, p3, mlp_ref, w_ref, attn_ref, send_ref, keep_ref, *, k):
+    mix_kernel(p0, p1, p2, p3, attn_ref)
+    chunk_dots(place, k, attn_ref, mlp_ref, w_ref, send_ref, keep_ref)
+
+
+def branch_next_kernel(place, attn_ref, mlp_ref, w_ref, send_ref, keep_ref, *, k):
+    chunk_dots(place, k, attn_ref, mlp_ref, w_ref, send_ref, keep_ref)
+
+
+def branch(place, inputs, mlp_branch, w_attn, k):
     _, rows, width = mlp_branch.shape
+    first = len(inputs) == SIDE
     return call(
-        branch_kernel, [*parts, mlp_branch, w_attn], [((NZ, rows, width), BF16)] * 2,
-        scalars=place, scratch=[VMEM((rows, width), BF16)], name="branch",
-    )
+        functools.partial(branch_first_kernel if first else branch_next_kernel, k=k),
+        [*inputs, mlp_branch, w_attn], [((rows, width), BF16)] * (3 if first else 2),
+        scalars=place, name="branch",
+    )
+
+
+def finish_kernel(place, rows_ref, mine_ref, s1, s2, gate_ref, out_ref):
+    count = place[2]
+    for i in range(rows_ref.shape[0] // BLOCK):
+        here = slice(i * BLOCK, (i + 1) * BLOCK)
+        total = mine_ref[here, :] + s1[here, :].astype(F32) + s2[here, :].astype(F32)
+        result = rows_ref[here, :].astype(F32) + gate_ref[...] * total
+        out_ref[here, :] = jnp.where(i < count, result, 0.0).astype(BF16)
+
+
+def finish(place, rows, mine, sums, gate):
+    operands = [in_vmem(a) for a in (rows, mine, *sums, gate)]
+    return pl.pallas_call(
+        finish_kernel,
+        in_specs=[spec(pltpu.SMEM)] + [spec(VMEM)] * len(operands),
+        out_specs=spec(VMEM),
+        out_shape=jax.ShapeDtypeStruct(rows.shape, BF16),
+        compiler_params=pltpu.CompilerParams(vmem_limit_bytes=16 * 2**20),
+        name="finish",
+    )(place, *operands)
 
 
 def partner(kind, at, core):
@@ -397,9 +437,9 @@
     return lax.ppermute(a, ("patch", "head"), pairs)
 
 
-def up_or_down(a):
+def up_or_down(a, steps=(1, 3)):
     return lax.ppermute(
-        a, "head", [(z * 2 + c, (z + (1, 3)[c]) % 4 * 2 + c) for z in range(4) for c in range(2)]
+        a, "head", [(z * 2 + c, (z + steps[c]) % 4 * 2 + c) for z in range(4) for c in range(2)]
     )
 
 
@@ -411,57 +451,61 @@
     return lax.ppermute(a, "head", [(i, i ^ 1) for i in range(8)])
 
 
-def ring(axis, a):
-    first, second = along(axis, "first", a), along(axis, "second", a)
-    return [a, first, second, along(axis, "second", first)]
+def ring_near(axis, a):
+    return [a, along(axis, "first", a), along(axis, "second", a)]
+
+
+def ring_far(axis, buffers):
+    return [*buffers, along(axis, "second", buffers[1])]
 
 
 def body(
     hidden, key_cache, value_cache, block_order, refresh_counts, modulation,
     query_gain, key_gain, w_qkv, w_mlp, w_out_attn, w_out_mlp,
 ):
-    width = hidden.shape[1]
     count = refresh_counts[0]
     head = lax.axis_index("head")
     z, core = head // 2, head % 2
     place = jnp.stack([z, core, count]).astype(jnp.int32)
+    width = hidden.shape[1]
+    gate = lax.dynamic_slice(modulation, (2, head * width), (1, width))
     w_qkv = jnp.transpose(w_qkv, (1, 0, 2))
 
-    (rows,) = pick_rows(block_order, hidden)
-    rest, old = pick_cache(block_order, key_cache, value_cache)
-    rows, rest = lax.optimization_barrier((rows, rest))
-    beside = other_core(rows)
-    near = up_or_down(rows)
-    near_beside = up_or_down(beside)
-    across = up_or_down(near)
-    pieces = [
-        rows, beside, near, near_beside, across,
-        other_core(near), other_core(near_beside), other_core(across),
-    ]
+    rows, rest, old = pick(block_order, hidden, key_cache, value_cache)
+    near, away = up_or_down(rows), up_or_down(rows, (3, 1))
+    own = [rows, near, away, up_or_down(near)]
+    pieces = own + [other_core(a) for a in own]
     rest_first, rest_second = along("a", "first", rest), along("a", "second", rest)
     pieces, rest_first, rest_second = lax.optimization_barrier((pieces, rest_first, rest_second))
-    rest = [rest, rest_first, rest_second, along("a", "second", rest_first)]
+    rest_opposite = along("a", "second", rest_first)
 
     query, fresh, modded = project(place, pieces, modulation, query_gain, key_gain, w_qkv, old)
-    fresh, queries = ring("a", fresh), ring("b", query)
+    query, fresh, modded, rest_opposite = lax.optimization_barrier((query, fresh, modded, rest_opposite))
+    rest = [rest, rest_first, rest_second, rest_opposite]
+    queries, fresh = ring_near("b", query), ring_near("a", fresh)
     mlp_hidden = mlp_in(modded, w_mlp)
-    queries, mlp_hidden, fresh[1] = lax.optimization_barrier((queries, mlp_hidden, fresh[1]))
-    state = attend(queries, rest, [], False)
-    parts = attend(queries, fresh, state, True)
-    mlp_branch = mlp_out(place, mlp_hidden, w_out_mlp)
-
+    queries, mlp_hidden = lax.optimization_barrier((queries, mlp_hidden))
+    queries = ring_far("b", queries)
+    queries, fresh = lax.optimization_barrier((queries, fresh))
+    fresh = ring_far("a", fresh)
+    state = attend(queries, rest)
+    parts = attend(queries, fresh, state)
     kinds = ("first", "second", "opposite")
     back = [parts[0]] + [along("b", kind, parts[n + 1]) for n, kind in enumerate(kinds)]
-    send, keep = branch(place, back, mlp_branch, w_out_attn)
-    chip = keep.astype(F32) + other_core(send).astype(F32)
-    summed = chip[0]
+    mlp_branch = mlp_out(place, mlp_hidden, w_out_mlp)
+    attn, send, keep = branch(place, back, mlp_branch, w_out_attn, 0)
+    across = (keep.astype(F32) + other_core(send).astype(F32)).astype(BF16)
+    attn, across = lax.optimization_barrier((attn, across))
+    across = up_or_down(across)
+    chips = []
     for k in (2, 1, 3):
-        summed = summed + along_z(chip[k].astype(BF16), k).astype(F32)
-
-    gate = lax.dynamic_slice_in_dim(modulation[2], head * width, width)
-    result = (rows.astype(F32) + gate * summed).astype(BF16)
-    live = jnp.arange(result.shape[0]) < count * BLOCK
-    return jnp.where(live[:, None], result, jnp.zeros((), BF16))
+        if k == 3:
+            attn, across = lax.optimization_barrier((attn, across))
+        send, keep = branch(place, [attn], mlp_branch, w_out_attn, k)
+        chips.append(keep.astype(F32) + other_core(send).astype(F32))
+    near = up_or_down((chips[1] + across.astype(F32)).astype(BF16))
+    away = up_or_down(chips[0].astype(BF16), (3, 1))
+    return finish(place, rows, chips[2], [near, away], gate)
 
 
 def solution(mesh):

time: 138 us -> 135 us (0.978); the launches traced: 135 us -> 136 us
  Pallas kernels: 44.9 us -> 55.3 us
  starting transfers between devices: 36.4 us -> 30.7 us
  local copies, waits for them, and re-layouts: 6.4 us -> 3.18 us
  other arithmetic: 2.81 us -> 0.53 us
  waiting for transfers between devices: 43.8 us -> 45.3 us
    pallas_call x8 -> x10, Pallas kernels: 44.9 us -> 53.7 us  [call(): pl.pallas_call(kernel, in_specs=specs, out_specs=[spec(VMEM)] * len(outs)...]
    ppermute x12, waiting for transfers between devices: 9.19 us -> 17.8 us  [along(): return lax.ppermute(a, ('patch', 'head'), pairs)]
    ppermute x6, waiting for transfers between devices: 30.3 us -> 23.9 us  [up_or_down(): lax.ppermute(a, 'head', [(z * 2 + c, (z + steps[c]) % 4 * 2 + c) for z in...]
    ppermute x12, starting transfers between devices: 26.2 us -> 20 us  [along(): return lax.ppermute(a, ('patch', 'head'), pairs)]
    select_n x1 -> x0, other arithmetic: 2.27 us -> none  [body(): return jnp.where(live[:, None], result, jnp.zeros((), BF16))]
    unnamed x18 -> x12, local copies, waits for them, and re-layouts: 4.52 us -> 2.41 us
    ppermute x5 -> x8, starting transfers between devices: 2.45 us -> 4.02 us  [other_core(): return lax.ppermute(a, 'head', [(i, i ^ 1) for i in range(8)])]
    pallas_call x0 -> x1, Pallas kernels: none -> 1.53 us  [finish(): pl.pallas_call(finish_kernel, in_specs=[spec(pltpu.SMEM)] + [spec(VMEM)]...]
  transfers between devices with their start and end apart: 23 -> 26, of which waited for: 10 -> 13; matrix products, arithmetic and copies ran while one was open for 1% -> 1% of each run, Pallas kernels for 13% -> 24%
where the time goes in v3:
time: 135 us; the launch traced here: 136 us
  Pallas kernels  55.3 us (41%)
  waiting for transfers between devices  45.3 us (34%)
  starting transfers between devices  30.7 us (23%)
  local copies, waits for them, and re-layouts  3.18 us (2%)
    pallas_call x10, Pallas kernels, call(): pl.pallas_call(kernel, in_specs=specs, out_specs=[spec(VMEM)] * len(outs)...  53.7 us
    ppermute x6, waiting for transfers between devices, up_or_down(): lax.ppermute(a, 'head', [(z * 2 + c, (z + steps[c]) % 4 * 2 + c) for z in...  23.9 us
    ppermute x12, starting transfers between devices, along(): return lax.ppermute(a, ('patch', 'head'), pairs)  20 us
    ppermute x12, waiting for transfers between devices, along(): return lax.ppermute(a, ('patch', 'head'), pairs)  17.8 us
    ppermute x6, starting transfers between devices, up_or_down(): lax.ppermute(a, 'head', [(z * 2 + c, (z + steps[c]) % 4 * 2 + c) for z in...  6.69 us
    ppermute x8, starting transfers between devices, other_core(): return lax.ppermute(a, 'head', [(i, i ^ 1) for i in range(8)])  4.02 us
    ppermute x8, waiting for transfers between devices, other_core(): return lax.ppermute(a, 'head', [(i, i ^ 1) for i in range(8)])  3.7 us
  transfers between devices with their start and end apart: 26, of which 13 were waited for; matrix products, arithmetic and copies ran while one was open for 1% of the time, Pallas kernels for 24%

profile of v3, /device:TPU:0, one launch (start us, length us, event | category | flops | bytes accessed | tf_op | source)
XLA Modules:
  0.0 135.8 jit_solution(8989920102707026898)
XLA Ops:
  0.0 0.7 copy-done.1
  0.7 2.3 %pick.1 = (bf16[512,384]{1,0:T(8,128)(2,1)S(1)}, bf16[512,768]{1,0:T(8,128)(2,1)S(1)}, bf16[512,768]{1,0:T(8,128)(2,1)S(1)}) custom-call(s32[1,8]{1,0:T(1,128)S(1)} %copy-done.1, bf16[1024,384]{1,0:T(8,128)(2,1)} %hidden.1, bf16[1024,384]{1,0:T(8,128)(2,1)} %keys.1, bf16[1024,384]{1,0:T(8,128)(2,1)} %values.1), custom_call_target="tpu_custom_call" | custom-call | bytes 1000 | tf_op jit(solution)/shard_map/pick/pallas_call | solution.py:43
  3.0 2.1 %collective-permute-start = (bf16[512,384]{1,0:T(8,128)(2,1)S(1)}, bf16[512,384]{1,0:T(8,128)(2,1)}, u32[]{:S(2)}, u32[]{:S(2)}) collective-permute-start(bf16[512,384]{1,0:T(8,128)(2,1)S(1)} %get-tuple-element.57.p0.rows_ref), channel_id=1, source_target_pairs={{0,2},{1,7},{2,4},{3,1},{4,6},{5,3},{6,0},{7,5},{8,10},{9,15},{10,... | collective-permute-start | bytes 1179656 | tf_op jit(solution)/shard_map/ppermute | solution.py:441
  5.0 2.2 %collective-permute-start.1 = (bf16[512,384]{1,0:T(8,128)(2,1)S(1)}, bf16[512,384]{1,0:T(8,128)(2,1)}, u32[]{:S(2)}, u32[]{:S(2)}) collective-permute-start(bf16[512,384]{1,0:T(8,128)(2,1)S(1)} %get-tuple-element.57.p0.rows_ref), channel_id=1, source_target_pairs={{0,6},{1,3},{2,0},{3,5},{4,2},{5,7},{6,4},{7,1},{8,14},{9,11},{10,... | collective-permute-start | bytes 1179656 | tf_op jit(solution)/shard_map/ppermute | solution.py:441
  7.2 0.0 collective-permute-start.3
  7.2 1.6 %collective-permute-start.7 = (bf16[512,768]{1,0:T(8,128)(2,1)S(1)}, bf16[512,768]{1,0:T(8,128)(2,1)S(1)}, u32[]{:S(2)}, u32[]{:S(2)}) collective-permute-start(bf16[512,768]{1,0:T(8,128)(2,1)S(1)} %get-tuple-element.56.refs_4_), channel_id=1, source_target_pairs={{0,32},{1,25},{2,34},{3,27},{4,36},{5,29},{6,38},{7,31},{8,40},{9,... | collective-permute-start | bytes 2359304 | tf_op jit(solution)/shard_map/ppermute | solution.py:437
  8.8 2.2 %collective-permute-start.8 = (bf16[512,768]{1,0:T(8,128)(2,1)S(1)}, bf16[512,768]{1,0:T(8,128)(2,1)S(1)}, u32[]{:S(2)}, u32[]{:S(2)}) collective-permute-start(bf16[512,768]{1,0:T(8,128)(2,1)S(1)} %get-tuple-element.56.refs_4_), channel_id=1, source_target_pairs={{0,96},{1,9},{2,98},{3,11},{4,100},{5,13},{6,102},{7,15},{8,104},{... | collective-permute-start | bytes 2359304 | tf_op jit(solution)/shard_map/ppermute | solution.py:437
  11.0 4.3 %collective-permute-done.p1 = bf16[512,384]{1,0:T(8,128)(2,1)} collective-permute-done((bf16[512,384]{1,0:T(8,128)(2,1)S(1)}, bf16[512,384]{1,0:T(8,128)(2,1)}, u32[]{:S(2)}, u32[]{:S(2)}) %collective-permute-start) | collective-permute-done | bytes 393248 | tf_op jit(solution)/shard_map/ppermute | solution.py:441
  15.3 0.8 collective-permute-start.2
  16.1 1.8 %collective-permute-start.4 = (bf16[512,384]{1,0:T(8,128)(2,1)}, bf16[512,384]{1,0:T(8,128)(2,1)}, u32[]{:S(2)}, u32[]{:S(2)}) collective-permute-start(bf16[512,384]{1,0:T(8,128)(2,1)} %collective-permute-done.p1), channel_id=1, source_target_pairs={{0,1},{1,0},{2,3},{3,2},{4,5},{5,4},{6,7},{7,6},{8,9},{9,8},{10,11... | collective-permute-start | bytes 1179656 | tf_op jit(solution)/shard_map/ppermute | solution.py:451
  17.9 0.0 collective-permute-done.3.p4
  17.9 0.7 copy-done.2
  18.7 0.0 collective-permute-start.5
  18.7 6.0 %collective-permute-done.2.p3 = bf16[512,384]{1,0:T(8,128)(2,1)} collective-permute-done((bf16[512,384]{1,0:T(8,128)(2,1)}, bf16[512,384]{1,0:T(8,128)(2,1)}, u32[]{:S(2)}, u32[]{:S(2)}) %collective-permute-start.2) | collective-permute-done | bytes 393248 | tf_op jit(solution)/shard_map/ppermute | solution.py:441
  25.3 0.1 pad_add_fusion.place
  25.4 0.0 collective-permute-done.8.refs_6_
  25.4 1.3 collective-permute-done.6.p7
  26.7 3.0 %collective-permute-start.9 = (bf16[512,768]{1,0:T(8,128)(2,1)S(1)}, bf16[512,768]{1,0:T(8,128)(2,1)S(1)}, u32[]{:S(2)}, u32[]{:S(2)}) collective-permute-start(bf16[512,768]{1,0:T(8,128)(2,1)S(1)} %collective-permute-done.7.refs_5_), channel_id=1, source_target_pairs={{0,96},{1,9},{2,98},{3,11},{4,100},{5,13},{6,102},{7,15},{8,104},{... | collective-permute-start | bytes 2359304 | tf_op jit(solution)/shard_map/ppermute | solution.py:437
  29.7 1.0 copy-done.3
  30.7 10.5 %project.1 = (bf16[528,384]{1,0:T(8,128)(2,1)S(1)}, bf16[512,768]{1,0:T(8,128)(2,1)S(1)}, bf16[512,3072]{1,0:T(8,128)(2,1)S(1)}) custom-call(s32[3]{0:T(128)S(1)} %pad_add_fusion.place, bf16[512,384]{1,0:T(8,128)(2,1)S(1)} %get-tuple-element.57.p0.rows_ref, bf16[512,384]{1,0:T(8,128)(2,1)} %collective-permute-done.p1, ...), custom_call_target="tpu_custom_call" | custom-call | flops 11000000512 | bytes 1000 | tf_op jit(solution)/shard_map/project/pallas_call | solution.py:43
  41.2 0.0 collective-permute-done.9.refs_7_
  41.2 1.6 %collective-permute-start.10 = (bf16[528,384]{1,0:T(8,128)(2,1)S(1)}, bf16[528,384]{1,0:T(8,128)(2,1)S(1)}, u32[]{:S(2)}, u32[]{:S(2)}) collective-permute-start(bf16[528,384]{1,0:T(8,128)(2,1)S(1)} %get-tuple-element.76.refs_0_), channel_id=1, source_target_pairs={{0,8},{1,97},{2,10},{3,99},{4,12},{5,101},{6,14},{7,103},{8,0},{9,... | collective-permute-start | bytes 1216520 | tf_op jit(solution)/shard_map/ppermute | solution.py:437
  42.8 2.1 %collective-permute-start.11 = (bf16[528,384]{1,0:T(8,128)(2,1)S(1)}, bf16[528,384]{1,0:T(8,128)(2,1)S(1)}, u32[]{:S(2)}, u32[]{:S(2)}) collective-permute-start(bf16[528,384]{1,0:T(8,128)(2,1)S(1)} %get-tuple-element.76.refs_0_), channel_id=1, source_target_pairs={{0,24},{1,33},{2,26},{3,35},{4,28},{5,37},{6,30},{7,39},{8,16},{9,... | collective-permute-start | bytes 1216520 | tf_op jit(solution)/shard_map/ppermute | solution.py:437
  44.9 0.1 collective-permute-start.13
  45.0 1.5 %collective-permute-start.14 = (bf16[512,768]{1,0:T(8,128)(2,1)S(1)}, bf16[512,768]{1,0:T(8,128)(2,1)S(1)}, u32[]{:S(2)}, u32[]{:S(2)}) collective-permute-start(bf16[512,768]{1,0:T(8,128)(2,1)S(1)} %get-tuple-element.80.refs_4_), channel_id=1, source_target_pairs={{0,96},{1,9},{2,98},{3,11},{4,100},{5,13},{6,102},{7,15},{8,104},{... | collective-permute-start | bytes 2359304 | tf_op jit(solution)/shard_map/ppermute | solution.py:437
  46.5 4.7 %mlp_in.1.mlp_ref = bf16[512,768]{1,0:T(8,128)(2,1)S(1)} custom-call(bf16[512,3072]{1,0:T(8,128)(2,1)S(1)} %get-tuple-element.71.modded_ref, bf16[3072,768]{1,0:T(8,128)(2,1)} %w_ref.6), custom_call_target="tpu_custom_call" | custom-call | flops 5500000256 | bytes 1000 | tf_op jit(solution)/shard_map/mlp_in/pallas_call | solution.py:43
  51.2 0.3 collective-permute-done.10.refs_1_
  51.5 4.7 %collective-permute-done.11.refs_2_ = bf16[528,384]{1,0:T(8,128)(2,1)S(1)} collective-permute-done((bf16[528,384]{1,0:T(8,128)(2,1)S(1)}, bf16[528,384]{1,0:T(8,128)(2,1)S(1)}, u32[]{:S(2)}, u32[]{:S(2)}) %collective-permute-start.11) | collective-permute-done | bytes 405536 | tf_op jit(solution)/shard_map/ppermute | solution.py:437
  56.3 2.1 %collective-permute-start.12 = (bf16[528,384]{1,0:T(8,128)(2,1)S(1)}, bf16[528,384]{1,0:T(8,128)(2,1)S(1)}, u32[]{:S(2)}, u32[]{:S(2)}) collective-permute-start(bf16[528,384]{1,0:T(8,128)(2,1)S(1)} %collective-permute-done.10.refs_1_), channel_id=1, source_target_pairs={{0,24},{1,33},{2,26},{3,35},{4,28},{5,37},{6,30},{7,39},{8,16},{9,... | collective-permute-start | bytes 1216520 | tf_op jit(solution)/shard_map/ppermute | solution.py:437
  58.4 3.7 %collective-permute-done.13.refs_5_ = bf16[512,768]{1,0:T(8,128)(2,1)S(1)} collective-permute-done((bf16[512,768]{1,0:T(8,128)(2,1)S(1)}, bf16[512,768]{1,0:T(8,128)(2,1)S(1)}, u32[]{:S(2)}, u32[]{:S(2)}) %collective-permute-start.13) | collective-permute-done | bytes 786464 | tf_op jit(solution)/shard_map/ppermute | solution.py:437
  62.1 0.0 collective-permute-done.14.refs_6_
  62.1 3.3 %collective-permute-done.12.refs_3_ = bf16[528,384]{1,0:T(8,128)(2,1)S(1)} collective-permute-done((bf16[528,384]{1,0:T(8,128)(2,1)S(1)}, bf16[528,384]{1,0:T(8,128)(2,1)S(1)}, u32[]{:S(2)}, u32[]{:S(2)}) %collective-permute-start.12) | collective-permute-done | bytes 405536 | tf_op jit(solution)/shard_map/ppermute | solution.py:437
  65.4 1.6 %collective-permute-start.15 = (bf16[512,768]{1,0:T(8,128)(2,1)S(1)}, bf16[512,768]{1,0:T(8,128)(2,1)S(1)}, u32[]{:S(2)}, u32[]{:S(2)}) collective-permute-start(bf16[512,768]{1,0:T(8,128)(2,1)S(1)} %collective-permute-done.13.refs_5_), channel_id=1, source_target_pairs={{0,96},{1,9},{2,98},{3,11},{4,100},{5,13},{6,102},{7,15},{8,104},{... | collective-permute-start | bytes 2359304 | tf_op jit(solution)/shard_map/ppermute | solution.py:437
  67.1 11.6 %attend_first.1 = (f32[2176,384]{1,0:T(8,128)S(1)}, f32[2176,384]{1,0:T(8,128)S(1)}) custom-call(bf16[528,384]{1,0:T(8,128)(2,1)S(1)} %get-tuple-element.76.refs_0_, bf16[528,384]{1,0:T(8,128)(2,1)S(1)} %collective-permute-done.10.refs_1_, bf16[528,384]{1,0:T(8,128)(2,1)S(1)} %collective-permute-done.11.refs_2_, ...), custom_call_target="tpu_custom_call" | custom-call | bytes 1000 | tf_op jit(solution)/shard_map/attend_first/pallas_call | solution.py:43
  78.7 0.0 collective-permute-done.15.refs_7_
  78.7 0.0 slice-start.1
  78.7 15.0 %attend_last.1 = (bf16[528,384]{1,0:T(8,128)(2,1)S(1)}, bf16[528,384]{1,0:T(8,128)(2,1)S(1)}, bf16[528,384]{1,0:T(8,128)(2,1)S(1)}, bf16[528,384]{1,0:T(8,128)(2,1)S(1)}) custom-call(bf16[528,384]{1,0:T(8,128)(2,1)S(1)} %get-tuple-element.76.refs_0_, bf16[528,384]{1,0:T(8,128)(2,1)S(1)} %collective-permute-done.10.refs_1_, ...), custom_call_target="tpu_custom_call" | custom-call | flops 9900000256 | bytes 1000 | tf_op jit(solution)/shard_map/attend_last/pallas_call | solution.py:43
  93.7 0.1 collective-permute-start.16
  93.8 2.2 %collective-permute-start.17 = (bf16[528,384]{1,0:T(8,128)(2,1)S(1)}, bf16[528,384]{1,0:T(8,128)(2,1)S(1)}, u32[]{:S(2)}, u32[]{:S(2)}) collective-permute-start(bf16[528,384]{1,0:T(8,128)(2,1)S(1)} %get-tuple-element.89), channel_id=1, source_target_pairs={{0,24},{1,33},{2,26},{3,35},{4,28},{5,37},{6,30},{7,39},{8,16},{9,... | collective-permute-start | bytes 1216520 | tf_op jit(solution)/shard_map/ppermute | solution.py:437
  95.9 1.9 %collective-permute-start.18 = (bf16[528,384]{1,0:T(8,128)(2,1)S(1)}, bf16[528,384]{1,0:T(8,128)(2,1)S(1)}, u32[]{:S(2)}, u32[]{:S(2)}) collective-permute-start(bf16[528,384]{1,0:T(8,128)(2,1)S(1)} %get-tuple-element.90), channel_id=1, source_target_pairs={{0,16},{1,65},{2,18},{3,67},{4,20},{5,69},{6,22},{7,71},{8,24},{9,... | collective-permute-start | bytes 1216520 | tf_op jit(solution)/shard_map/ppermute | solution.py:437
  97.9 4.0 %mlp_out.1.mlp_ref = f32[8,512,384]{2,1,0:T(8,128)S(1)} custom-call(s32[3]{0:T(128)S(1)} %pad_add_fusion.place, bf16[512,768]{1,0:T(8,128)(2,1)S(1)} %mlp_in.1.mlp_ref, bf16[768,3072]{1,0:T(8,128)(2,1)S(1)} %bitcast.6), custom_call_target="tpu_custom_call" | custom-call | flops 4400000000 | bytes 1000 | tf_op jit(solution)/shard_map/mlp_out/pallas_call | solution.py:43
  101.9 0.0 collective-permute-done.16.p1
  101.9 3.9 %collective-permute-done.17.p2 = bf16[528,384]{1,0:T(8,128)(2,1)S(1)} collective-permute-done((bf16[528,384]{1,0:T(8,128)(2,1)S(1)}, bf16[528,384]{1,0:T(8,128)(2,1)S(1)}, u32[]{:S(2)}, u32[]{:S(2)}) %collective-permute-start.17) | collective-permute-done | bytes 405536 | tf_op jit(solution)/shard_map/ppermute | solution.py:437
  105.7 1.8 %collective-permute-done.18.p3 = bf16[528,384]{1,0:T(8,128)(2,1)S(1)} collective-permute-done((bf16[528,384]{1,0:T(8,128)(2,1)S(1)}, bf16[528,384]{1,0:T(8,128)(2,1)S(1)}, u32[]{:S(2)}, u32[]{:S(2)}) %collective-permute-start.18) | collective-permute-done | bytes 405536 | tf_op jit(solution)/shard_map/ppermute | solution.py:437
  107.5 2.1 %branch.4 = (bf16[512,384]{1,0:T(8,128)(2,1)S(1)}, bf16[512,384]{1,0:T(8,128)(2,1)S(1)}, bf16[512,384]{1,0:T(8,128)(2,1)S(1)}) custom-call(s32[3]{0:T(128)S(1)} %pad_add_fusion.place, bf16[528,384]{1,0:T(8,128)(2,1)S(1)} %get-tuple-element.87.p0, bf16[528,384]{1,0:T(8,128)(2,1)S(1)} %collective-permute-done.16.p1, ...), custom_call_target="tpu_custom_call" | custom-call | bytes 1000 | tf_op jit(solution)/shard_map/branch/pallas_call | solution.py:43
  109.6 0.1 collective-permute-start.19
  109.7 1.7 %collective-permute-done.19 = bf16[512,384]{1,0:T(8,128)(2,1)S(1)} collective-permute-done((bf16[512,384]{1,0:T(8,128)(2,1)S(1)}, bf16[512,384]{1,0:T(8,128)(2,1)S(1)}, u32[]{:S(2)}, u32[]{:S(2)}) %collective-permute-start.19) | collective-permute-done | bytes 393248 | tf_op jit(solution)/shard_map/ppermute | solution.py:451
  111.4 0.1 add_convert_fusion.2
  111.5 1.2 branch.7
  112.7 0.2 collective-permute-start.24
  113.0 1.2 branch.6
  114.2 1.9 %collective-permute-start.22 = (bf16[512,384]{1,0:T(8,128)(2,1)S(1)}, bf16[512,384]{1,0:T(8,128)(2,1)S(1)}, u32[]{:S(2)}, u32[]{:S(2)}) collective-permute-start(bf16[512,384]{1,0:T(8,128)(2,1)S(1)} %get-tuple-element.101), channel_id=1, source_target_pairs={{0,1},{1,0},{2,3},{3,2},{4,5},{5,4},{6,7},{7,6},{8,9},{9,8},{10,11... | collective-permute-start | bytes 1179656 | tf_op jit(solution)/shard_map/ppermute | solution.py:451
  116.0 0.1 add_convert_fusion
  116.1 1.5 %collective-permute-start.25 = (bf16[512,384]{1,0:T(8,128)(2,1)S(1)}, bf16[512,384]{1,0:T(8,128)(2,1)S(1)}, u32[]{:S(2)}, u32[]{:S(2)}) collective-permute-start(bf16[512,384]{1,0:T(8,128)(2,1)S(1)} %add_convert_fusion), channel_id=1, source_target_pairs={{0,6},{1,3},{2,0},{3,5},{4,2},{5,7},{6,4},{7,1},{8,14},{9,11},{10,... | collective-permute-start | bytes 1179656 | tf_op jit(solution)/shard_map/ppermute | solution.py:441
  117.7 6.1 %collective-permute-done.20 = bf16[512,384]{1,0:T(8,128)(2,1)S(1)} collective-permute-done((bf16[512,384]{1,0:T(8,128)(2,1)S(1)}, bf16[512,384]{1,0:T(8,128)(2,1)S(1)}, u32[]{:S(2)}, u32[]{:S(2)}) %collective-permute-start.20) | collective-permute-done | bytes 393248 | tf_op jit(solution)/shard_map/ppermute | solution.py:441
  123.8 1.2 branch.5
  125.0 0.1 collective-permute-start.21
  125.1 0.2 add_convert_fusion.1
  125.3 0.1 collective-permute-start.23
  125.3 0.8 constant_dynamic-slice_fusion.gate_ref
  126.1 0.7 collective-permute-done.21
  126.8 0.1 convert_add_fusion.mine_ref
  126.9 7.4 %collective-permute-done.23.s1 = bf16[512,384]{1,0:T(8,128)(2,1)S(1)} collective-permute-done((bf16[512,384]{1,0:T(8,128)(2,1)S(1)}, bf16[512,384]{1,0:T(8,128)(2,1)S(1)}, u32[]{:S(2)}, u32[]{:S(2)}) %collective-permute-start.23) | collective-permute-done | bytes 393248 | tf_op jit(solution)/shard_map/ppermute | solution.py:441
  134.3 1.5 %finish.1 = bf16[512,384]{1,0:T(8,128)(2,1)} custom-call(s32[3]{0:T(128)S(1)} %pad_add_fusion.place, bf16[512,384]{1,0:T(8,128)(2,1)S(1)} %get-tuple-element.57.p0.rows_ref, f32[512,384]{1,0:T(8,128)S(1)} %convert_add_fusion.mine_ref, bf16[512,384]{1,0:T(8,128)(2,1)S(1)} %collective-permute-done.23.s1, bf16[512,384]{1,0:T(8,128)(2,1)S(1)} %collective-permute-done.25.s2, ...), custom_call_target="tpu_custom_call" | custom-call | tf_op jit(solution)/shard_map/finish/pallas_call | solution.py:407
  (18 shorter events, 0.0 us)
Async XLA Ops:
  0.0 0.7 copy-start.1
  3.0 12.4 %collective-permute-start = (bf16[512,384]{1,0:T(8,128)(2,1)S(1)}, bf16[512,384]{1,0:T(8,128)(2,1)}, u32[]{:S(2)}, u32[]{:S(2)}) collective-permute-start(bf16[512,384]{1,0:T(8,128)(2,1)S(1)} %get-tuple-element.57.p0.rows_ref), channel_id=1, source_target_pairs={{0,2},{1,7},{2,4},{3,1},{4,6},{5,3},{6,0},{7,5},{8,10},{9,15},{10,... | collective-permute-start | bytes 1179656 | tf_op jit(solution)/shard_map/ppermute | solution.py:441
  5.0 11.1 %collective-permute-start.1 = (bf16[512,384]{1,0:T(8,128)(2,1)S(1)}, bf16[512,384]{1,0:T(8,128)(2,1)}, u32[]{:S(2)}, u32[]{:S(2)}) collective-permute-start(bf16[512,384]{1,0:T(8,128)(2,1)S(1)} %get-tuple-element.57.p0.rows_ref), channel_id=1, source_target_pairs={{0,6},{1,3},{2,0},{3,5},{4,2},{5,7},{6,4},{7,1},{8,14},{9,11},{10,... | collective-permute-start | bytes 1179656 | tf_op jit(solution)/shard_map/ppermute | solution.py:441
  7.2 10.7 %collective-permute-start.3 = (bf16[512,384]{1,0:T(8,128)(2,1)S(1)}, bf16[512,384]{1,0:T(8,128)(2,1)S(1)}, u32[]{:S(2)}, u32[]{:S(2)}) collective-permute-start(bf16[512,384]{1,0:T(8,128)(2,1)S(1)} %get-tuple-element.57.p0.rows_ref), channel_id=1, source_target_pairs={{0,1},{1,0},{2,3},{3,2},{4,5},{5,4},{6,7},{7,6},{8,9},{9,8},{10,11... | collective-permute-start | bytes 1179656 | tf_op jit(solution)/shard_map/ppermute | solution.py:451
  7.2 18.2 %collective-permute-start.7 = (bf16[512,768]{1,0:T(8,128)(2,1)S(1)}, bf16[512,768]{1,0:T(8,128)(2,1)S(1)}, u32[]{:S(2)}, u32[]{:S(2)}) collective-permute-start(bf16[512,768]{1,0:T(8,128)(2,1)S(1)} %get-tuple-element.56.refs_4_), channel_id=1, source_target_pairs={{0,32},{1,25},{2,34},{3,27},{4,36},{5,29},{6,38},{7,31},{8,40},{9,... | collective-permute-start | bytes 2359304 | tf_op jit(solution)/shard_map/ppermute | solution.py:437
  8.8 16.6 %collective-permute-start.8 = (bf16[512,768]{1,0:T(8,128)(2,1)S(1)}, bf16[512,768]{1,0:T(8,128)(2,1)S(1)}, u32[]{:S(2)}, u32[]{:S(2)}) collective-permute-start(bf16[512,768]{1,0:T(8,128)(2,1)S(1)} %get-tuple-element.56.refs_4_), channel_id=1, source_target_pairs={{0,96},{1,9},{2,98},{3,11},{4,100},{5,13},{6,102},{7,15},{8,104},{... | collective-permute-start | bytes 2359304 | tf_op jit(solution)/shard_map/ppermute | solution.py:437
  15.3 9.3 %collective-permute-start.2 = (bf16[512,384]{1,0:T(8,128)(2,1)}, bf16[512,384]{1,0:T(8,128)(2,1)}, u32[]{:S(2)}, u32[]{:S(2)}) collective-permute-start(bf16[512,384]{1,0:T(8,128)(2,1)} %collective-permute-done.p1), channel_id=1, source_target_pairs={{0,2},{1,7},{2,4},{3,1},{4,6},{5,3},{6,0},{7,5},{8,10},{9,15},{10,... | collective-permute-start | bytes 1179656 | tf_op jit(solution)/shard_map/ppermute | solution.py:441
  16.1 9.2 %collective-permute-start.4 = (bf16[512,384]{1,0:T(8,128)(2,1)}, bf16[512,384]{1,0:T(8,128)(2,1)}, u32[]{:S(2)}, u32[]{:S(2)}) collective-permute-start(bf16[512,384]{1,0:T(8,128)(2,1)} %collective-permute-done.p1), channel_id=1, source_target_pairs={{0,1},{1,0},{2,3},{3,2},{4,5},{5,4},{6,7},{7,6},{8,9},{9,8},{10,11... | collective-permute-start | bytes 1179656 | tf_op jit(solution)/shard_map/ppermute | solution.py:451
  17.9 0.7 copy-start.2
  18.7 6.7 %collective-permute-start.5 = (bf16[512,384]{1,0:T(8,128)(2,1)}, bf16[512,384]{1,0:T(8,128)(2,1)}, u32[]{:S(2)}, u32[]{:S(2)}) collective-permute-start(bf16[512,384]{1,0:T(8,128)(2,1)} %collective-permute-done.1.p2), channel_id=1, source_target_pairs={{0,1},{1,0},{2,3},{3,2},{4,5},{5,4},{6,7},{7,6},{8,9},{9,8},{10,11... | collective-permute-start | bytes 1179656 | tf_op jit(solution)/shard_map/ppermute | solution.py:451
  24.6 2.1 %collective-permute-start.6 = (bf16[512,384]{1,0:T(8,128)(2,1)}, bf16[512,384]{1,0:T(8,128)(2,1)}, u32[]{:S(2)}, u32[]{:S(2)}) collective-permute-start(bf16[512,384]{1,0:T(8,128)(2,1)} %collective-permute-done.2.p3), channel_id=1, source_target_pairs={{0,1},{1,0},{2,3},{3,2},{4,5},{5,4},{6,7},{7,6},{8,9},{9,8},{10,11... | collective-permute-start | bytes 1179656 | tf_op jit(solution)/shard_map/ppermute | solution.py:451
  26.7 14.5 %collective-permute-start.9 = (bf16[512,768]{1,0:T(8,128)(2,1)S(1)}, bf16[512,768]{1,0:T(8,128)(2,1)S(1)}, u32[]{:S(2)}, u32[]{:S(2)}) collective-permute-start(bf16[512,768]{1,0:T(8,128)(2,1)S(1)} %collective-permute-done.7.refs_5_), channel_id=1, source_target_pairs={{0,96},{1,9},{2,98},{3,11},{4,100},{5,13},{6,102},{7,15},{8,104},{... | collective-permute-start | bytes 2359304 | tf_op jit(solution)/shard_map/ppermute | solution.py:437
  29.7 1.0 copy-start.3
  41.2 10.3 %collective-permute-start.10 = (bf16[528,384]{1,0:T(8,128)(2,1)S(1)}, bf16[528,384]{1,0:T(8,128)(2,1)S(1)}, u32[]{:S(2)}, u32[]{:S(2)}) collective-permute-start(bf16[528,384]{1,0:T(8,128)(2,1)S(1)} %get-tuple-element.76.refs_0_), channel_id=1, source_target_pairs={{0,8},{1,97},{2,10},{3,99},{4,12},{5,101},{6,14},{7,103},{8,0},{9,... | collective-permute-start | bytes 1216520 | tf_op jit(solution)/shard_map/ppermute | solution.py:437
  42.8 13.5 %collective-permute-start.11 = (bf16[528,384]{1,0:T(8,128)(2,1)S(1)}, bf16[528,384]{1,0:T(8,128)(2,1)S(1)}, u32[]{:S(2)}, u32[]{:S(2)}) collective-permute-start(bf16[528,384]{1,0:T(8,128)(2,1)S(1)} %get-tuple-element.76.refs_0_), channel_id=1, source_target_pairs={{0,24},{1,33},{2,26},{3,35},{4,28},{5,37},{6,30},{7,39},{8,16},{9,... | collective-permute-start | bytes 1216520 | tf_op jit(solution)/shard_map/ppermute | solution.py:437
  44.9 17.2 %collective-permute-start.13 = (bf16[512,768]{1,0:T(8,128)(2,1)S(1)}, bf16[512,768]{1,0:T(8,128)(2,1)S(1)}, u32[]{:S(2)}, u32[]{:S(2)}) collective-permute-start(bf16[512,768]{1,0:T(8,128)(2,1)S(1)} %get-tuple-element.80.refs_4_), channel_id=1, source_target_pairs={{0,32},{1,25},{2,34},{3,27},{4,36},{5,29},{6,38},{7,31},{8,40},{9,... | collective-permute-start | bytes 2359304 | tf_op jit(solution)/shard_map/ppermute | solution.py:437
  45.0 17.1 %collective-permute-start.14 = (bf16[512,768]{1,0:T(8,128)(2,1)S(1)}, bf16[512,768]{1,0:T(8,128)(2,1)S(1)}, u32[]{:S(2)}, u32[]{:S(2)}) collective-permute-start(bf16[512,768]{1,0:T(8,128)(2,1)S(1)} %get-tuple-element.80.refs_4_), channel_id=1, source_target_pairs={{0,96},{1,9},{2,98},{3,11},{4,100},{5,13},{6,102},{7,15},{8,104},{... | collective-permute-start | bytes 2359304 | tf_op jit(solution)/shard_map/ppermute | solution.py:437
  56.3 9.1 %collective-permute-start.12 = (bf16[528,384]{1,0:T(8,128)(2,1)S(1)}, bf16[528,384]{1,0:T(8,128)(2,1)S(1)}, u32[]{:S(2)}, u32[]{:S(2)}) collective-permute-start(bf16[528,384]{1,0:T(8,128)(2,1)S(1)} %collective-permute-done.10.refs_1_), channel_id=1, source_target_pairs={{0,24},{1,33},{2,26},{3,35},{4,28},{5,37},{6,30},{7,39},{8,16},{9,... | collective-permute-start | bytes 1216520 | tf_op jit(solution)/shard_map/ppermute | solution.py:437
  65.4 13.3 %collective-permute-start.15 = (bf16[512,768]{1,0:T(8,128)(2,1)S(1)}, bf16[512,768]{1,0:T(8,128)(2,1)S(1)}, u32[]{:S(2)}, u32[]{:S(2)}) collective-permute-start(bf16[512,768]{1,0:T(8,128)(2,1)S(1)} %collective-permute-done.13.refs_5_), channel_id=1, source_target_pairs={{0,96},{1,9},{2,98},{3,11},{4,100},{5,13},{6,102},{7,15},{8,104},{... | collective-permute-start | bytes 2359304 | tf_op jit(solution)/shard_map/ppermute | solution.py:437
  67.1 30.8 %slice-start = ((s8[4718592]{0:T(1024)(128)(4,1)}), s8[4194304]{0:T(1024)(128)(4,1)S(1)}, s32[]{:S(2)}) async-start(s8[4718592]{0:T(1024)(128)(4,1)} %bitcast.5), calls=%async_computation | async-start | bytes 8388608
  78.7 19.2 %slice-start.1 = ((s8[4718592]{0:T(1024)(128)(4,1)}), s8[524288]{0:T(1024)(128)(4,1)S(1)}, s32[]{:S(2)}) async-start(s8[4718592]{0:T(1024)(128)(4,1)} %bitcast.5), calls=%async_computation.1 | async-start | bytes 1048576
  93.7 8.2 %collective-permute-start.16 = (bf16[528,384]{1,0:T(8,128)(2,1)S(1)}, bf16[528,384]{1,0:T(8,128)(2,1)S(1)}, u32[]{:S(2)}, u32[]{:S(2)}) collective-permute-start(bf16[528,384]{1,0:T(8,128)(2,1)S(1)} %get-tuple-element.88), channel_id=1, source_target_pairs={{0,8},{1,97},{2,10},{3,99},{4,12},{5,101},{6,14},{7,103},{8,0},{9,... | collective-permute-start | bytes 1216520 | tf_op jit(solution)/shard_map/ppermute | solution.py:437
  93.8 12.0 %collective-permute-start.17 = (bf16[528,384]{1,0:T(8,128)(2,1)S(1)}, bf16[528,384]{1,0:T(8,128)(2,1)S(1)}, u32[]{:S(2)}, u32[]{:S(2)}) collective-permute-start(bf16[528,384]{1,0:T(8,128)(2,1)S(1)} %get-tuple-element.89), channel_id=1, source_target_pairs={{0,24},{1,33},{2,26},{3,35},{4,28},{5,37},{6,30},{7,39},{8,16},{9,... | collective-permute-start | bytes 1216520 | tf_op jit(solution)/shard_map/ppermute | solution.py:437
  95.9 11.6 %copy-start = (bf16[384,3072]{1,0:T(8,128)(2,1)S(1)}, bf16[384,3072]{1,0:T(8,128)(2,1)}, u32[]{:S(2)}) copy-start(bf16[384,3072]{1,0:T(8,128)(2,1)} %w_ref.11) | copy-start | bytes 7077892
  95.9 11.6 %collective-permute-start.18 = (bf16[528,384]{1,0:T(8,128)(2,1)S(1)}, bf16[528,384]{1,0:T(8,128)(2,1)S(1)}, u32[]{:S(2)}, u32[]{:S(2)}) collective-permute-start(bf16[528,384]{1,0:T(8,128)(2,1)S(1)} %get-tuple-element.90), channel_id=1, source_target_pairs={{0,16},{1,65},{2,18},{3,67},{4,20},{5,69},{6,22},{7,71},{8,24},{9,... | collective-permute-start | bytes 1216520 | tf_op jit(solution)/shard_map/ppermute | solution.py:437
  109.6 1.8 %collective-permute-start.19 = (bf16[512,384]{1,0:T(8,128)(2,1)S(1)}, bf16[512,384]{1,0:T(8,128)(2,1)S(1)}, u32[]{:S(2)}, u32[]{:S(2)}) collective-permute-start(bf16[512,384]{1,0:T(8,128)(2,1)S(1)} %get-tuple-element.94), channel_id=1, source_target_pairs={{0,1},{1,0},{2,3},{3,2},{4,5},{5,4},{6,7},{7,6},{8,9},{9,8},{10,11... | collective-permute-start | bytes 1179656 | tf_op jit(solution)/shard_map/ppermute | solution.py:451
  112.7 3.3 %collective-permute-start.24 = (bf16[512,384]{1,0:T(8,128)(2,1)S(1)}, bf16[512,384]{1,0:T(8,128)(2,1)S(1)}, u32[]{:S(2)}, u32[]{:S(2)}) collective-permute-start(bf16[512,384]{1,0:T(8,128)(2,1)S(1)} %get-tuple-element.104), channel_id=1, source_target_pairs={{0,1},{1,0},{2,3},{3,2},{4,5},{5,4},{6,7},{7,6},{8,9},{9,8},{10,11... | collective-permute-start | bytes 1179656 | tf_op jit(solution)/shard_map/ppermute | solution.py:451
  112.9 10.8 %collective-permute-start.20 = (bf16[512,384]{1,0:T(8,128)(2,1)S(1)}, bf16[512,384]{1,0:T(8,128)(2,1)S(1)}, u32[]{:S(2)}, u32[]{:S(2)}) collective-permute-start(bf16[512,384]{1,0:T(8,128)(2,1)S(1)} %add_convert_fusion.2), channel_id=1, source_target_pairs={{0,2},{1,7},{2,4},{3,1},{4,6},{5,3},{6,0},{7,5},{8,10},{9,15},{10,... | collective-permute-start | bytes 1179656 | tf_op jit(solution)/shard_map/ppermute | solution.py:441
  114.2 10.9 %collective-permute-start.22 = (bf16[512,384]{1,0:T(8,128)(2,1)S(1)}, bf16[512,384]{1,0:T(8,128)(2,1)S(1)}, u32[]{:S(2)}, u32[]{:S(2)}) collective-permute-start(bf16[512,384]{1,0:T(8,128)(2,1)S(1)} %get-tuple-element.101), channel_id=1, source_target_pairs={{0,1},{1,0},{2,3},{3,2},{4,5},{5,4},{6,7},{7,6},{8,9},{9,8},{10,11... | collective-permute-start | bytes 1179656 | tf_op jit(solution)/shard_map/ppermute | solution.py:451
  116.1 10.7 %collective-permute-start.25 = (bf16[512,384]{1,0:T(8,128)(2,1)S(1)}, bf16[512,384]{1,0:T(8,128)(2,1)S(1)}, u32[]{:S(2)}, u32[]{:S(2)}) collective-permute-start(bf16[512,384]{1,0:T(8,128)(2,1)S(1)} %add_convert_fusion), channel_id=1, source_target_pairs={{0,6},{1,3},{2,0},{3,5},{4,2},{5,7},{6,4},{7,1},{8,14},{9,11},{10,... | collective-permute-start | bytes 1179656 | tf_op jit(solution)/shard_map/ppermute | solution.py:441
  125.0 1.8 %collective-permute-start.21 = (bf16[512,384]{1,0:T(8,128)(2,1)S(1)}, bf16[512,384]{1,0:T(8,128)(2,1)S(1)}, u32[]{:S(2)}, u32[]{:S(2)}) collective-permute-start(bf16[512,384]{1,0:T(8,128)(2,1)S(1)} %get-tuple-element.99), channel_id=1, source_target_pairs={{0,1},{1,0},{2,3},{3,2},{4,5},{5,4},{6,7},{7,6},{8,9},{9,8},{10,11... | collective-permute-start | bytes 1179656 | tf_op jit(solution)/shard_map/ppermute | solution.py:451
  125.3 9.1 %collective-permute-start.23 = (bf16[512,384]{1,0:T(8,128)(2,1)S(1)}, bf16[512,384]{1,0:T(8,128)(2,1)S(1)}, u32[]{:S(2)}, u32[]{:S(2)}) collective-permute-start(bf16[512,384]{1,0:T(8,128)(2,1)S(1)} %add_convert_fusion.1), channel_id=1, source_target_pairs={{0,2},{1,7},{2,4},{3,1},{4,6},{5,3},{6,0},{7,5},{8,10},{9,15},{10,... | collective-permute-start | bytes 1179656 | tf_op jit(solution)/shard_map/ppermute | solution.py:441

commit v4 on v3

--- a/solution.py
+++ b/solution.py
@@ -63,16 +63,15 @@
     return pl.ds(pl.multiple_of(order[0, place] * BLOCK, BLOCK), BLOCK)
 
 
-def pick_kernel(order, hidden, keys, values, rows_ref, rest_ref, old_ref, sems):
+def pick_kernel(order, hidden, keys, values, rows_ref, rest_ref, sems):
     pairs = []
     width = keys.shape[1]
     for i in range(RMAX):
         pairs.append((hidden.at[block_at(order, i), :], rows_ref.at[pl.ds(i * BLOCK, BLOCK), :]))
-    for i in range(2 * RMAX):
-        here, to = block_at(order, (RMAX + i) % (2 * RMAX)), pl.ds(i % RMAX * BLOCK, BLOCK)
+    for i in range(RMAX):
+        here, to = block_at(order, RMAX + i), pl.ds(i * BLOCK, BLOCK)
         for n, ref in enumerate((keys, values)):
-            out = rest_ref if i < RMAX else old_ref
-            pairs.append((ref.at[here, :], out.at[to, pl.ds(n * width, width)]))
+            pairs.append((ref.at[here, :], rest_ref.at[to, pl.ds(n * width, width)]))
     for copy in copies_of(pairs, sems):
         copy.wait()
 
@@ -80,30 +79,41 @@
 def pick(order, hidden, keys, values):
     tall, width = RMAX * BLOCK, hidden.shape[1]
     return call(
-        pick_kernel, [], [((tall, width), BF16)] + [((tall, 2 * width), BF16)] * 2, scalars=order,
-        far=[hidden, keys, values], scratch=[pltpu.SemaphoreType.DMA((5 * RMAX,))], name="pick",
+        pick_kernel, [], [((tall, width), BF16), ((tall, 2 * width), BF16)], scalars=order,
+        far=[hidden, keys, values], scratch=[pltpu.SemaphoreType.DMA((3 * RMAX,))], name="pick",
     )
 
 
 def project_kernel(
-    place, p0, p1, p2, p3, p4, p5, p6, p7, old_ref, mod_far, qg_far, kg_far, w_ref,
-    q_ref, kv_ref, modded_ref, mod_ref, qg_ref, kg_ref, w_vmem, sems,
+    place, p0, p1, p2, p3, p4, p5, p6, p7, mod_far, qg_far, kg_far, w_ref, keys, values,
+    q_ref, kv_ref, modded_ref, pieces_ref, old_ref, mod_ref, qg_ref, kg_ref, w_vmem, sems,
 ):
-    pieces = (p0, p1, p2, p3, p4, p5, p6, p7)
-    z, core, count = place[0], place[1], place[2]
+    z, core, count = place[0, 0], place[0, 1], place[0, 2]
     rows, width = p0.shape
+    far_pieces = (p1, p2, p3, p4, p5, p6, p7)
+    pieces = [p0] + [pieces_ref.at[n] for n in range(len(far_pieces))]
     features = width * len(pieces)
-    mod_copy, *weight_copies, qg_copy, kg_copy = copies_of(
-        [(mod_far, mod_ref)] + [(w_ref.at[n], w_vmem.at[n]) for n in range(3)]
-        + [(qg_far, qg_ref), (kg_far, kg_ref)],
+    copies = copies_of(
+        [(ref, pieces_ref.at[n]) for n, ref in enumerate(far_pieces)]
+        + [(mod_far, mod_ref), (qg_far, qg_ref), (kg_far, kg_ref)]
+        + [(w_ref.at[n], w_vmem.at[n]) for n in range(3)]
+        + [
+            (ref.at[block_at(place, 3 + i), :], old_ref.at[pl.ds(i * BLOCK, BLOCK), pl.ds(n * width, width)])
+            for i in range(RMAX)
+            for n, ref in enumerate((keys, values))
+        ],
         sems,
+    )
+    piece_copies, (mod_copy, qg_copy, kg_copy), weight_copies, old_copies = (
+        copies[:7], copies[7:10], copies[10:13], copies[13:],
     )
     near = lax.rem(z + NZ - 1 + 2 * core, NZ)
     away = lax.rem(z + NZ + 1 - 2 * core, NZ)
     across = lax.rem(z + 2, NZ)
     homes = [zone * 2 + core for zone in (z, near, away, across)]
     homes += [zone * 2 + 1 - core for zone in (z, away, near, across)]
-    mod_copy.wait()
+    for copy in (*piece_copies, mod_copy):
+        copy.wait()
     tall = 32
 
     def norm(i, carry):
@@ -132,7 +142,7 @@
         return v * scale * gain
 
     heads = width // HD
-    waits = {0: [weight_copies[0], qg_copy, kg_copy], 2: [weight_copies[1]], 6: [weight_copies[2]]}
+    waits = {0: [weight_copies[0], qg_copy, kg_copy], 2: [weight_copies[1], *old_copies], 6: [weight_copies[2]]}
     for first in range(0, 3 * heads, 2):
         pair = range(first, min(first + 2, 3 * heads))
         for copy in waits.get(first, ()):
@@ -157,19 +167,22 @@
     )
 
 
-def project(place, pieces, modulation, query_gain, key_gain, w_qkv, old):
+def project(place, pieces, modulation, query_gain, key_gain, w_qkv, keys, values):
     rows, width = pieces[0].shape
     features = w_qkv.shape[1]
     return call(
         project_kernel,
-        [*pieces, old],
+        pieces[:1],
         [((rows + NOTE_ROWS, width), BF16), ((rows, 2 * width), BF16), ((rows, features), BF16)],
-        scalars=place, far=[modulation, query_gain.reshape(1, HD), key_gain.reshape(1, HD), w_qkv],
+        scalars=place, far=[
+            *pieces[1:], modulation, query_gain.reshape(1, HD), key_gain.reshape(1, HD), w_qkv, keys, values,
+        ],
         scratch=[
+            VMEM((7, rows, width), BF16), VMEM((rows, 2 * width), BF16),
             VMEM(modulation.shape, F32), VMEM((1, HD), F32), VMEM((1, HD), F32), VMEM(w_qkv.shape, BF16),
-            pltpu.SemaphoreType.DMA((6,)),
+            pltpu.SemaphoreType.DMA((13 + 2 * RMAX,)),
         ],
-        cost=10 * PER_US, name="project",
+        cost=10 * PER_US, mib=24, name="project",
     )
 
 
@@ -311,7 +324,7 @@
         outs = states
     return call(
         functools.partial(attend_kernel, n_keys=len(caches), chained=bool(state)),
-        [*queries, *caches, *state], outs, scratch=scratch, mib=24, cost=9 * PER_US if state else 0,
+        [*queries, *caches, *state], outs, scratch=scratch, mib=24, cost=9 * PER_US if state else 5 * PER_US,
         name="attend_last" if state else "attend_first",
     )
 
@@ -467,11 +480,12 @@
     head = lax.axis_index("head")
     z, core = head // 2, head % 2
     place = jnp.stack([z, core, count]).astype(jnp.int32)
+    ordered = jnp.concatenate([place, block_order[0, :RMAX]]).reshape(1, 3 + RMAX)
     width = hidden.shape[1]
     gate = lax.dynamic_slice(modulation, (2, head * width), (1, width))
     w_qkv = jnp.transpose(w_qkv, (1, 0, 2))
 
-    rows, rest, old = pick(block_order, hidden, key_cache, value_cache)
+    rows, rest = pick(block_order, hidden, key_cache, value_cache)
     near, away = up_or_down(rows), up_or_down(rows, (3, 1))
     own = [rows, near, away, up_or_down(near)]
     pieces = own + [other_core(a) for a in own]
@@ -479,15 +493,16 @@
     pieces, rest_first, rest_second = lax.optimization_barrier((pieces, rest_first, rest_second))
     rest_opposite = along("a", "second", rest_first)
 
-    query, fresh, modded = project(place, pieces, modulation, query_gain, key_gain, w_qkv, old)
+    query, fresh, modded = project(
+        ordered, pieces, modulation, query_gain, key_gain, w_qkv, key_cache, value_cache
+    )
     query, fresh, modded, rest_opposite = lax.optimization_barrier((query, fresh, modded, rest_opposite))
     rest = [rest, rest_first, rest_second, rest_opposite]
     queries, fresh = ring_near("b", query), ring_near("a", fresh)
     mlp_hidden = mlp_in(modded, w_mlp)
     queries, mlp_hidden = lax.optimization_barrier((queries, mlp_hidden))
-    queries = ring_far("b", queries)
-    queries, fresh = lax.optimization_barrier((queries, fresh))
-    fresh = ring_far("a", fresh)
+    fresh = lax.optimization_barrier(fresh)
+    queries, fresh = ring_far("b", queries), ring_far("a", fresh)
     state = attend(queries, rest)
     parts = attend(queries, fresh, state)
     kinds = ("first", "second", "opposite")

time: 135 us -> 131 us (0.970)
  the two profiles are of different devices: /device:TPU:0 before, /device:TPU:8 now
where the time goes in v4:
time: 131 us; the launch traced here: 133 us
  Pallas kernels  54.8 us (42%)
  waiting for transfers between devices  43.4 us (33%)
  starting transfers between devices  30.8 us (24%)
  local copies, waits for them, and re-layouts  2.11 us (2%)
    pallas_call x10, Pallas kernels, call(): pl.pallas_call(kernel, in_specs=specs, out_specs=[spec(VMEM)] * len(outs)...  53.3 us
    ppermute x6, waiting for transfers between devices, up_or_down(): lax.ppermute(a, 'head', [(z * 2 + c, (z + steps[c]) % 4 * 2 + c) for z in...  25.1 us
    ppermute x12, starting transfers between devices, along(): return lax.ppermute(a, ('patch', 'head'), pairs)  20.1 us
    ppermute x12, waiting for transfers between devices, along(): return lax.ppermute(a, ('patch', 'head'), pairs)  15.3 us
    ppermute x6, starting transfers between devices, up_or_down(): lax.ppermute(a, 'head', [(z * 2 + c, (z + steps[c]) % 4 * 2 + c) for z in...  6.6 us
    ppermute x8, starting transfers between devices, other_core(): return lax.ppermute(a, 'head', [(i, i ^ 1) for i in range(8)])  4.12 us
    ppermute x8, waiting for transfers between devices, other_core(): return lax.ppermute(a, 'head', [(i, i ^ 1) for i in range(8)])  3.05 us
  transfers between devices with their start and end apart: 26, of which 12 were waited for; matrix products, arithmetic and copies ran while one was open for 1% of the time, Pallas kernels for 25%

profile of v4, /device:TPU:8, one launch (start us, length us, event | category | flops | bytes accessed | tf_op | source)
XLA Modules:
  0.0 132.6 jit_solution(5021068617811805377)
XLA Ops:
  0.0 0.7 copy-done.1
  0.7 2.0 %pick.1 = (bf16[512,384]{1,0:T(8,128)(2,1)S(1)}, bf16[512,768]{1,0:T(8,128)(2,1)S(1)}) custom-call(s32[1,8]{1,0:T(1,128)S(1)} %copy-done.1, bf16[1024,384]{1,0:T(8,128)(2,1)} %hidden.1, bf16[1024,384]{1,0:T(8,128)(2,1)} %keys.3, bf16[1024,384]{1,0:T(8,128)(2,1)} %values.3), custom_call_target="tpu_custom_call" | custom-call | bytes 1000 | tf_op jit(solution)/shard_map/pick/pallas_call | solution.py:43
  2.6 2.0 %collective-permute-start = (bf16[512,384]{1,0:T(8,128)(2,1)S(1)}, bf16[512,384]{1,0:T(8,128)(2,1)S(1)}, u32[]{:S(2)}, u32[]{:S(2)}) collective-permute-start(bf16[512,384]{1,0:T(8,128)(2,1)S(1)} %get-tuple-element.52.p0.rows_ref), channel_id=1, source_target_pairs={{0,2},{1,7},{2,4},{3,1},{4,6},{5,3},{6,0},{7,5},{8,10},{9,15},{10,... | collective-permute-start | bytes 1179656 | tf_op jit(solution)/shard_map/ppermute | solution.py:454
  4.6 2.2 %collective-permute-start.1 = (bf16[512,384]{1,0:T(8,128)(2,1)S(1)}, bf16[512,384]{1,0:T(8,128)(2,1)S(1)}, u32[]{:S(2)}, u32[]{:S(2)}) collective-permute-start(bf16[512,384]{1,0:T(8,128)(2,1)S(1)} %get-tuple-element.52.p0.rows_ref), channel_id=1, source_target_pairs={{0,6},{1,3},{2,0},{3,5},{4,2},{5,7},{6,4},{7,1},{8,14},{9,11},{10,... | collective-permute-start | bytes 1179656 | tf_op jit(solution)/shard_map/ppermute | solution.py:454
  6.8 0.4 collective-permute-start.7
  7.3 2.4 %collective-permute-start.8 = (bf16[512,768]{1,0:T(8,128)(2,1)S(1)}, bf16[512,768]{1,0:T(8,128)(2,1)S(1)}, u32[]{:S(2)}, u32[]{:S(2)}) collective-permute-start(bf16[512,768]{1,0:T(8,128)(2,1)S(1)} %get-tuple-element.51.refs_4_), channel_id=1, source_target_pairs={{0,96},{1,9},{2,98},{3,11},{4,100},{5,13},{6,102},{7,15},{8,104},{... | collective-permute-start | bytes 2359304 | tf_op jit(solution)/shard_map/ppermute | solution.py:450
  9.7 5.1 %collective-permute-done.p1 = bf16[512,384]{1,0:T(8,128)(2,1)S(1)} collective-permute-done((bf16[512,384]{1,0:T(8,128)(2,1)S(1)}, bf16[512,384]{1,0:T(8,128)(2,1)S(1)}, u32[]{:S(2)}, u32[]{:S(2)}) %collective-permute-start) | collective-permute-done | bytes 393248 | tf_op jit(solution)/shard_map/ppermute | solution.py:454
  14.8 0.8 collective-permute-start.2
  15.6 1.8 %collective-permute-start.4 = (bf16[512,384]{1,0:T(8,128)(2,1)S(1)}, bf16[512,384]{1,0:T(8,128)(2,1)}, u32[]{:S(2)}, u32[]{:S(2)}) collective-permute-start(bf16[512,384]{1,0:T(8,128)(2,1)S(1)} %collective-permute-done.p1), channel_id=1, source_target_pairs={{0,1},{1,0},{2,3},{3,2},{4,5},{5,4},{6,7},{7,6},{8,9},{9,8},{10,11... | collective-permute-start | bytes 1179656 | tf_op jit(solution)/shard_map/ppermute | solution.py:464
  17.4 0.0 collective-permute-done.3.p4
  17.4 0.1 collective-permute-start.5
  17.5 6.4 %collective-permute-done.2.p3 = bf16[512,384]{1,0:T(8,128)(2,1)} collective-permute-done((bf16[512,384]{1,0:T(8,128)(2,1)S(1)}, bf16[512,384]{1,0:T(8,128)(2,1)}, u32[]{:S(2)}, u32[]{:S(2)}) %collective-permute-start.2) | collective-permute-done | bytes 393248 | tf_op jit(solution)/shard_map/ppermute | solution.py:454
  23.9 0.0 collective-permute-start.6
  24.6 0.7 slice_bitcast_fusion
  25.3 0.1 add_bitcast_fusion.place
  25.4 0.0 collective-permute-done.8.refs_6_
  25.4 0.6 collective-permute-done.6.p7
  26.0 1.6 %collective-permute-start.9 = (bf16[512,768]{1,0:T(8,128)(2,1)S(1)}, bf16[512,768]{1,0:T(8,128)(2,1)S(1)}, u32[]{:S(2)}, u32[]{:S(2)}) collective-permute-start(bf16[512,768]{1,0:T(8,128)(2,1)S(1)} %collective-permute-done.7.refs_5_), channel_id=1, source_target_pairs={{0,96},{1,9},{2,98},{3,11},{4,100},{5,13},{6,102},{7,15},{8,104},{... | collective-permute-start | bytes 2359304 | tf_op jit(solution)/shard_map/ppermute | solution.py:450
  27.6 10.2 %project.1 = (bf16[528,384]{1,0:T(8,128)(2,1)S(1)}, bf16[512,768]{1,0:T(8,128)(2,1)S(1)}, bf16[512,3072]{1,0:T(8,128)(2,1)S(1)}) custom-call(s32[1,7]{1,0:T(1,128)S(1)} %add_bitcast_fusion.place, bf16[512,384]{1,0:T(8,128)(2,1)S(1)} %get-tuple-element.52.p0.rows_ref, bf16[512,384]{1,0:T(8,128)(2,1)} %copy-done.2, bf16[512,384]{1,0:T(8,128)(2,1)} %copy-done.3, ...), custom_call_target="tpu_custom_call" | custom-call | flops 11000000512 | bytes 1000 | tf_op jit(solution)/shard_map/project/pallas_call | solution.py:43
  37.8 0.2 collective-permute-done.9.refs_7_
  38.0 1.8 %collective-permute-start.13 = (bf16[512,768]{1,0:T(8,128)(2,1)S(1)}, bf16[512,768]{1,0:T(8,128)(2,1)S(1)}, u32[]{:S(2)}, u32[]{:S(2)}) collective-permute-start(bf16[512,768]{1,0:T(8,128)(2,1)S(1)} %get-tuple-element.70.refs_4_), channel_id=1, source_target_pairs={{0,32},{1,25},{2,34},{3,27},{4,36},{5,29},{6,38},{7,31},{8,40},{9,... | collective-permute-start | bytes 2359304 | tf_op jit(solution)/shard_map/ppermute | solution.py:450
  39.8 2.3 %collective-permute-start.14 = (bf16[512,768]{1,0:T(8,128)(2,1)S(1)}, bf16[512,768]{1,0:T(8,128)(2,1)S(1)}, u32[]{:S(2)}, u32[]{:S(2)}) collective-permute-start(bf16[512,768]{1,0:T(8,128)(2,1)S(1)} %get-tuple-element.70.refs_4_), channel_id=1, source_target_pairs={{0,96},{1,9},{2,98},{3,11},{4,100},{5,13},{6,102},{7,15},{8,104},{... | collective-permute-start | bytes 2359304 | tf_op jit(solution)/shard_map/ppermute | solution.py:450
  42.1 1.5 %collective-permute-start.10 = (bf16[528,384]{1,0:T(8,128)(2,1)S(1)}, bf16[528,384]{1,0:T(8,128)(2,1)S(1)}, u32[]{:S(2)}, u32[]{:S(2)}) collective-permute-start(bf16[528,384]{1,0:T(8,128)(2,1)S(1)} %get-tuple-element.66.refs_0_), channel_id=1, source_target_pairs={{0,8},{1,97},{2,10},{3,99},{4,12},{5,101},{6,14},{7,103},{8,0},{9,... | collective-permute-start | bytes 1216520 | tf_op jit(solution)/shard_map/ppermute | solution.py:450
  43.6 2.1 %collective-permute-start.11 = (bf16[528,384]{1,0:T(8,128)(2,1)S(1)}, bf16[528,384]{1,0:T(8,128)(2,1)S(1)}, u32[]{:S(2)}, u32[]{:S(2)}) collective-permute-start(bf16[528,384]{1,0:T(8,128)(2,1)S(1)} %get-tuple-element.66.refs_0_), channel_id=1, source_target_pairs={{0,24},{1,33},{2,26},{3,35},{4,28},{5,37},{6,30},{7,39},{8,16},{9,... | collective-permute-start | bytes 1216520 | tf_op jit(solution)/shard_map/ppermute | solution.py:450
  45.7 4.7 %mlp_in.1.mlp_ref = bf16[512,768]{1,0:T(8,128)(2,1)S(1)} custom-call(bf16[512,3072]{1,0:T(8,128)(2,1)S(1)} %get-tuple-element.65.modded_ref, bf16[3072,768]{1,0:T(8,128)(2,1)} %w_ref.6), custom_call_target="tpu_custom_call" | custom-call | flops 5500000256 | bytes 1000 | tf_op jit(solution)/shard_map/mlp_in/pallas_call | solution.py:43
  50.3 4.0 %collective-permute-done.10.refs_1_ = bf16[528,384]{1,0:T(8,128)(2,1)S(1)} collective-permute-done((bf16[528,384]{1,0:T(8,128)(2,1)S(1)}, bf16[528,384]{1,0:T(8,128)(2,1)S(1)}, u32[]{:S(2)}, u32[]{:S(2)}) %collective-permute-start.10) | collective-permute-done | bytes 405536 | tf_op jit(solution)/shard_map/ppermute | solution.py:450
  54.4 2.2 %collective-permute-start.12 = (bf16[528,384]{1,0:T(8,128)(2,1)S(1)}, bf16[528,384]{1,0:T(8,128)(2,1)S(1)}, u32[]{:S(2)}, u32[]{:S(2)}) collective-permute-start(bf16[528,384]{1,0:T(8,128)(2,1)S(1)} %collective-permute-done.10.refs_1_), channel_id=1, source_target_pairs={{0,24},{1,33},{2,26},{3,35},{4,28},{5,37},{6,30},{7,39},{8,16},{9,... | collective-permute-start | bytes 1216520 | tf_op jit(solution)/shard_map/ppermute | solution.py:450
  56.6 0.0 collective-permute-done.13.refs_5_
  56.6 0.0 collective-permute-done.14.refs_6_
  56.6 1.6 %collective-permute-start.15 = (bf16[512,768]{1,0:T(8,128)(2,1)S(1)}, bf16[512,768]{1,0:T(8,128)(2,1)S(1)}, u32[]{:S(2)}, u32[]{:S(2)}) collective-permute-start(bf16[512,768]{1,0:T(8,128)(2,1)S(1)} %collective-permute-done.13.refs_5_), channel_id=1, source_target_pairs={{0,96},{1,9},{2,98},{3,11},{4,100},{5,13},{6,102},{7,15},{8,104},{... | collective-permute-start | bytes 2359304 | tf_op jit(solution)/shard_map/ppermute | solution.py:450
  58.2 0.1 pad_add_fusion.place
  58.3 5.2 %collective-permute-done.12.refs_3_ = bf16[528,384]{1,0:T(8,128)(2,1)S(1)} collective-permute-done((bf16[528,384]{1,0:T(8,128)(2,1)S(1)}, bf16[528,384]{1,0:T(8,128)(2,1)S(1)}, u32[]{:S(2)}, u32[]{:S(2)}) %collective-permute-start.12) | collective-permute-done | bytes 405536 | tf_op jit(solution)/shard_map/ppermute | solution.py:450
  63.5 11.8 %attend_first.1 = (f32[2176,384]{1,0:T(8,128)S(1)}, f32[2176,384]{1,0:T(8,128)S(1)}) custom-call(bf16[528,384]{1,0:T(8,128)(2,1)S(1)} %get-tuple-element.66.refs_0_, bf16[528,384]{1,0:T(8,128)(2,1)S(1)} %collective-permute-done.10.refs_1_, bf16[528,384]{1,0:T(8,128)(2,1)S(1)} %collective-permute-done.11.refs_2_, ...), custom_call_target="tpu_custom_call" | custom-call | flops 5500000256 | bytes 1000 | tf_op jit(solution)/shard_map/attend_first/pallas_call | solution.py:43
  75.4 0.0 collective-permute-done.15.refs_7_
  75.4 0.0 slice-start.1
  75.4 14.9 %attend_last.1 = (bf16[528,384]{1,0:T(8,128)(2,1)S(1)}, bf16[528,384]{1,0:T(8,128)(2,1)S(1)}, bf16[528,384]{1,0:T(8,128)(2,1)S(1)}, bf16[528,384]{1,0:T(8,128)(2,1)S(1)}) custom-call(bf16[528,384]{1,0:T(8,128)(2,1)S(1)} %get-tuple-element.66.refs_0_, bf16[528,384]{1,0:T(8,128)(2,1)S(1)} %collective-permute-done.10.refs_1_, ...), custom_call_target="tpu_custom_call" | custom-call | flops 9900000256 | bytes 1000 | tf_op jit(solution)/shard_map/attend_last/pallas_call | solution.py:43
  90.3 0.1 collective-permute-start.16
  90.4 2.3 %collective-permute-start.17 = (bf16[528,384]{1,0:T(8,128)(2,1)S(1)}, bf16[528,384]{1,0:T(8,128)(2,1)S(1)}, u32[]{:S(2)}, u32[]{:S(2)}) collective-permute-start(bf16[528,384]{1,0:T(8,128)(2,1)S(1)} %get-tuple-element.79), channel_id=1, source_target_pairs={{0,24},{1,33},{2,26},{3,35},{4,28},{5,37},{6,30},{7,39},{8,16},{9,... | collective-permute-start | bytes 1216520 | tf_op jit(solution)/shard_map/ppermute | solution.py:450
  92.7 1.8 %collective-permute-start.18 = (bf16[528,384]{1,0:T(8,128)(2,1)S(1)}, bf16[528,384]{1,0:T(8,128)(2,1)S(1)}, u32[]{:S(2)}, u32[]{:S(2)}) collective-permute-start(bf16[528,384]{1,0:T(8,128)(2,1)S(1)} %get-tuple-element.80), channel_id=1, source_target_pairs={{0,16},{1,65},{2,18},{3,67},{4,20},{5,69},{6,22},{7,71},{8,24},{9,... | collective-permute-start | bytes 1216520 | tf_op jit(solution)/shard_map/ppermute | solution.py:450
  94.5 4.0 %mlp_out.1.mlp_ref = f32[8,512,384]{2,1,0:T(8,128)S(1)} custom-call(s32[3]{0:T(128)S(1)} %pad_add_fusion.place, bf16[512,768]{1,0:T(8,128)(2,1)S(1)} %mlp_in.1.mlp_ref, bf16[768,3072]{1,0:T(8,128)(2,1)S(1)} %bitcast.10), custom_call_target="tpu_custom_call" | custom-call | flops 4400000000 | bytes 1000 | tf_op jit(solution)/shard_map/mlp_out/pallas_call | solution.py:43
  98.5 4.0 %collective-permute-done.17.p2 = bf16[528,384]{1,0:T(8,128)(2,1)S(1)} collective-permute-done((bf16[528,384]{1,0:T(8,128)(2,1)S(1)}, bf16[528,384]{1,0:T(8,128)(2,1)S(1)}, u32[]{:S(2)}, u32[]{:S(2)}) %collective-permute-start.17) | collective-permute-done | bytes 405536 | tf_op jit(solution)/shard_map/ppermute | solution.py:450
  102.5 1.8 %collective-permute-done.18.p3 = bf16[528,384]{1,0:T(8,128)(2,1)S(1)} collective-permute-done((bf16[528,384]{1,0:T(8,128)(2,1)S(1)}, bf16[528,384]{1,0:T(8,128)(2,1)S(1)}, u32[]{:S(2)}, u32[]{:S(2)}) %collective-permute-start.18) | collective-permute-done | bytes 405536 | tf_op jit(solution)/shard_map/ppermute | solution.py:450
  104.3 2.0 %branch.4 = (bf16[512,384]{1,0:T(8,128)(2,1)S(1)}, bf16[512,384]{1,0:T(8,128)(2,1)S(1)}, bf16[512,384]{1,0:T(8,128)(2,1)S(1)}) custom-call(s32[3]{0:T(128)S(1)} %pad_add_fusion.place, bf16[528,384]{1,0:T(8,128)(2,1)S(1)} %get-tuple-element.77.p0, bf16[528,384]{1,0:T(8,128)(2,1)S(1)} %collective-permute-done.16.p1, ...), custom_call_target="tpu_custom_call" | custom-call | bytes 1000 | tf_op jit(solution)/shard_map/branch/pallas_call | solution.py:43
  106.3 0.1 collective-permute-start.19
  106.4 1.7 %collective-permute-done.19 = bf16[512,384]{1,0:T(8,128)(2,1)S(1)} collective-permute-done((bf16[512,384]{1,0:T(8,128)(2,1)S(1)}, bf16[512,384]{1,0:T(8,128)(2,1)S(1)}, u32[]{:S(2)}, u32[]{:S(2)}) %collective-permute-start.19) | collective-permute-done | bytes 393248 | tf_op jit(solution)/shard_map/ppermute | solution.py:464
  108.1 0.1 add_convert_fusion.2
  108.3 1.2 branch.7
  109.5 0.2 collective-permute-start.24
  109.7 1.2 branch.6
  110.9 1.9 %collective-permute-start.22 = (bf16[512,384]{1,0:T(8,128)(2,1)S(1)}, bf16[512,384]{1,0:T(8,128)(2,1)S(1)}, u32[]{:S(2)}, u32[]{:S(2)}) collective-permute-start(bf16[512,384]{1,0:T(8,128)(2,1)S(1)} %get-tuple-element.91), channel_id=1, source_target_pairs={{0,1},{1,0},{2,3},{3,2},{4,5},{5,4},{6,7},{7,6},{8,9},{9,8},{10,11... | collective-permute-start | bytes 1179656 | tf_op jit(solution)/shard_map/ppermute | solution.py:464
  112.7 0.0 collective-permute-done.24
  112.7 0.1 add_convert_fusion
  112.9 1.5 %collective-permute-start.25 = (bf16[512,384]{1,0:T(8,128)(2,1)S(1)}, bf16[512,384]{1,0:T(8,128)(2,1)S(1)}, u32[]{:S(2)}, u32[]{:S(2)}) collective-permute-start(bf16[512,384]{1,0:T(8,128)(2,1)S(1)} %add_convert_fusion), channel_id=1, source_target_pairs={{0,6},{1,3},{2,0},{3,5},{4,2},{5,7},{6,4},{7,1},{8,14},{9,11},{10,... | collective-permute-start | bytes 1179656 | tf_op jit(solution)/shard_map/ppermute | solution.py:454
  114.4 6.1 %collective-permute-done.20 = bf16[512,384]{1,0:T(8,128)(2,1)S(1)} collective-permute-done((bf16[512,384]{1,0:T(8,128)(2,1)S(1)}, bf16[512,384]{1,0:T(8,128)(2,1)S(1)}, u32[]{:S(2)}, u32[]{:S(2)}) %collective-permute-start.20) | collective-permute-done | bytes 393248 | tf_op jit(solution)/shard_map/ppermute | solution.py:454
  120.5 1.2 branch.5
  121.7 0.1 collective-permute-start.21
  121.8 0.1 add_convert_fusion.1
  122.0 0.1 collective-permute-start.23
  122.1 0.8 constant_dynamic-slice_fusion.gate_ref
  122.8 0.7 collective-permute-done.21
  123.5 0.1 convert_add_fusion.mine_ref
  123.6 0.0 collective-permute-done.25.s2
  123.6 7.4 %collective-permute-done.23.s1 = bf16[512,384]{1,0:T(8,128)(2,1)S(1)} collective-permute-done((bf16[512,384]{1,0:T(8,128)(2,1)S(1)}, bf16[512,384]{1,0:T(8,128)(2,1)S(1)}, u32[]{:S(2)}, u32[]{:S(2)}) %collective-permute-start.23) | collective-permute-done | bytes 393248 | tf_op jit(solution)/shard_map/ppermute | solution.py:454
  131.0 1.5 %finish.1 = bf16[512,384]{1,0:T(8,128)(2,1)} custom-call(s32[3]{0:T(128)S(1)} %pad_add_fusion.place, bf16[512,384]{1,0:T(8,128)(2,1)S(1)} %get-tuple-element.52.p0.rows_ref, f32[512,384]{1,0:T(8,128)S(1)} %convert_add_fusion.mine_ref, bf16[512,384]{1,0:T(8,128)(2,1)S(1)} %collective-permute-done.23.s1, bf16[512,384]{1,0:T(8,128)(2,1)S(1)} %collective-permute-done.25.s2, ...), custom_call_target="tpu_custom_call" | custom-call | tf_op jit(solution)/shard_map/finish/pallas_call | solution.py:420
  (22 shorter events, 0.0 us)
Async XLA Ops:
  0.0 0.7 copy-start.1
  2.6 12.2 %collective-permute-start = (bf16[512,384]{1,0:T(8,128)(2,1)S(1)}, bf16[512,384]{1,0:T(8,128)(2,1)S(1)}, u32[]{:S(2)}, u32[]{:S(2)}) collective-permute-start(bf16[512,384]{1,0:T(8,128)(2,1)S(1)} %get-tuple-element.52.p0.rows_ref), channel_id=1, source_target_pairs={{0,2},{1,7},{2,4},{3,1},{4,6},{5,3},{6,0},{7,5},{8,10},{9,15},{10,... | collective-permute-start | bytes 1179656 | tf_op jit(solution)/shard_map/ppermute | solution.py:454
  4.6 11.0 %collective-permute-start.1 = (bf16[512,384]{1,0:T(8,128)(2,1)S(1)}, bf16[512,384]{1,0:T(8,128)(2,1)S(1)}, u32[]{:S(2)}, u32[]{:S(2)}) collective-permute-start(bf16[512,384]{1,0:T(8,128)(2,1)S(1)} %get-tuple-element.52.p0.rows_ref), channel_id=1, source_target_pairs={{0,6},{1,3},{2,0},{3,5},{4,2},{5,7},{6,4},{7,1},{8,14},{9,11},{10,... | collective-permute-start | bytes 1179656 | tf_op jit(solution)/shard_map/ppermute | solution.py:454
  6.8 10.6 %collective-permute-start.3 = (bf16[512,384]{1,0:T(8,128)(2,1)S(1)}, bf16[512,384]{1,0:T(8,128)(2,1)S(1)}, u32[]{:S(2)}, u32[]{:S(2)}) collective-permute-start(bf16[512,384]{1,0:T(8,128)(2,1)S(1)} %get-tuple-element.52.p0.rows_ref), channel_id=1, source_target_pairs={{0,1},{1,0},{2,3},{3,2},{4,5},{5,4},{6,7},{7,6},{8,9},{9,8},{10,11... | collective-permute-start | bytes 1179656 | tf_op jit(solution)/shard_map/ppermute | solution.py:464
  6.8 18.5 %collective-permute-start.7 = (bf16[512,768]{1,0:T(8,128)(2,1)S(1)}, bf16[512,768]{1,0:T(8,128)(2,1)S(1)}, u32[]{:S(2)}, u32[]{:S(2)}) collective-permute-start(bf16[512,768]{1,0:T(8,128)(2,1)S(1)} %get-tuple-element.51.refs_4_), channel_id=1, source_target_pairs={{0,32},{1,25},{2,34},{3,27},{4,36},{5,29},{6,38},{7,31},{8,40},{9,... | collective-permute-start | bytes 2359304 | tf_op jit(solution)/shard_map/ppermute | solution.py:450
  7.3 18.1 %collective-permute-start.8 = (bf16[512,768]{1,0:T(8,128)(2,1)S(1)}, bf16[512,768]{1,0:T(8,128)(2,1)S(1)}, u32[]{:S(2)}, u32[]{:S(2)}) collective-permute-start(bf16[512,768]{1,0:T(8,128)(2,1)S(1)} %get-tuple-element.51.refs_4_), channel_id=1, source_target_pairs={{0,96},{1,9},{2,98},{3,11},{4,100},{5,13},{6,102},{7,15},{8,104},{... | collective-permute-start | bytes 2359304 | tf_op jit(solution)/shard_map/ppermute | solution.py:450
  14.8 12.7 %copy-start.2 = (bf16[512,384]{1,0:T(8,128)(2,1)}, bf16[512,384]{1,0:T(8,128)(2,1)S(1)}, u32[]{:S(2)}) copy-start(bf16[512,384]{1,0:T(8,128)(2,1)S(1)} %collective-permute-done.p1) | copy-start | bytes 1179652
  14.8 9.1 %collective-permute-start.2 = (bf16[512,384]{1,0:T(8,128)(2,1)S(1)}, bf16[512,384]{1,0:T(8,128)(2,1)}, u32[]{:S(2)}, u32[]{:S(2)}) collective-permute-start(bf16[512,384]{1,0:T(8,128)(2,1)S(1)} %collective-permute-done.p1), channel_id=1, source_target_pairs={{0,2},{1,7},{2,4},{3,1},{4,6},{5,3},{6,0},{7,5},{8,10},{9,15},{10,... | collective-permute-start | bytes 1179656 | tf_op jit(solution)/shard_map/ppermute | solution.py:454
  15.6 11.9 %copy-start.3 = (bf16[512,384]{1,0:T(8,128)(2,1)}, bf16[512,384]{1,0:T(8,128)(2,1)S(1)}, u32[]{:S(2)}) copy-start(bf16[512,384]{1,0:T(8,128)(2,1)S(1)} %collective-permute-done.1.p2) | copy-start | bytes 1179652
  15.6 9.7 %collective-permute-start.4 = (bf16[512,384]{1,0:T(8,128)(2,1)S(1)}, bf16[512,384]{1,0:T(8,128)(2,1)}, u32[]{:S(2)}, u32[]{:S(2)}) collective-permute-start(bf16[512,384]{1,0:T(8,128)(2,1)S(1)} %collective-permute-done.p1), channel_id=1, source_target_pairs={{0,1},{1,0},{2,3},{3,2},{4,5},{5,4},{6,7},{7,6},{8,9},{9,8},{10,11... | collective-permute-start | bytes 1179656 | tf_op jit(solution)/shard_map/ppermute | solution.py:464
  17.4 6.5 %copy-start.4 = (bf16[512,384]{1,0:T(8,128)(2,1)}, bf16[512,384]{1,0:T(8,128)(2,1)S(1)}, u32[]{:S(2)}) copy-start(bf16[512,384]{1,0:T(8,128)(2,1)S(1)} %collective-permute-done.3.p4) | copy-start | bytes 1179652
  17.4 7.9 %collective-permute-start.5 = (bf16[512,384]{1,0:T(8,128)(2,1)S(1)}, bf16[512,384]{1,0:T(8,128)(2,1)}, u32[]{:S(2)}, u32[]{:S(2)}) collective-permute-start(bf16[512,384]{1,0:T(8,128)(2,1)S(1)} %collective-permute-done.1.p2), channel_id=1, source_target_pairs={{0,1},{1,0},{2,3},{3,2},{4,5},{5,4},{6,7},{7,6},{8,9},{9,8},{10,11... | collective-permute-start | bytes 1179656 | tf_op jit(solution)/shard_map/ppermute | solution.py:464
  23.9 2.1 %collective-permute-start.6 = (bf16[512,384]{1,0:T(8,128)(2,1)}, bf16[512,384]{1,0:T(8,128)(2,1)}, u32[]{:S(2)}, u32[]{:S(2)}) collective-permute-start(bf16[512,384]{1,0:T(8,128)(2,1)} %collective-permute-done.2.p3), channel_id=1, source_target_pairs={{0,1},{1,0},{2,3},{3,2},{4,5},{5,4},{6,7},{7,6},{8,9},{9,8},{10,11... | collective-permute-start | bytes 1179656 | tf_op jit(solution)/shard_map/ppermute | solution.py:464
  26.0 12.0 %collective-permute-start.9 = (bf16[512,768]{1,0:T(8,128)(2,1)S(1)}, bf16[512,768]{1,0:T(8,128)(2,1)S(1)}, u32[]{:S(2)}, u32[]{:S(2)}) collective-permute-start(bf16[512,768]{1,0:T(8,128)(2,1)S(1)} %collective-permute-done.7.refs_5_), channel_id=1, source_target_pairs={{0,96},{1,9},{2,98},{3,11},{4,100},{5,13},{6,102},{7,15},{8,104},{... | collective-permute-start | bytes 2359304 | tf_op jit(solution)/shard_map/ppermute | solution.py:450
  38.0 18.6 %collective-permute-start.13 = (bf16[512,768]{1,0:T(8,128)(2,1)S(1)}, bf16[512,768]{1,0:T(8,128)(2,1)S(1)}, u32[]{:S(2)}, u32[]{:S(2)}) collective-permute-start(bf16[512,768]{1,0:T(8,128)(2,1)S(1)} %get-tuple-element.70.refs_4_), channel_id=1, source_target_pairs={{0,32},{1,25},{2,34},{3,27},{4,36},{5,29},{6,38},{7,31},{8,40},{9,... | collective-permute-start | bytes 2359304 | tf_op jit(solution)/shard_map/ppermute | solution.py:450
  39.8 16.8 %collective-permute-start.14 = (bf16[512,768]{1,0:T(8,128)(2,1)S(1)}, bf16[512,768]{1,0:T(8,128)(2,1)S(1)}, u32[]{:S(2)}, u32[]{:S(2)}) collective-permute-start(bf16[512,768]{1,0:T(8,128)(2,1)S(1)} %get-tuple-element.70.refs_4_), channel_id=1, source_target_pairs={{0,96},{1,9},{2,98},{3,11},{4,100},{5,13},{6,102},{7,15},{8,104},{... | collective-permute-start | bytes 2359304 | tf_op jit(solution)/shard_map/ppermute | solution.py:450
  42.1 12.3 %collective-permute-start.10 = (bf16[528,384]{1,0:T(8,128)(2,1)S(1)}, bf16[528,384]{1,0:T(8,128)(2,1)S(1)}, u32[]{:S(2)}, u32[]{:S(2)}) collective-permute-start(bf16[528,384]{1,0:T(8,128)(2,1)S(1)} %get-tuple-element.66.refs_0_), channel_id=1, source_target_pairs={{0,8},{1,97},{2,10},{3,99},{4,12},{5,101},{6,14},{7,103},{8,0},{9,... | collective-permute-start | bytes 1216520 | tf_op jit(solution)/shard_map/ppermute | solution.py:450
  43.6 10.8 %collective-permute-start.11 = (bf16[528,384]{1,0:T(8,128)(2,1)S(1)}, bf16[528,384]{1,0:T(8,128)(2,1)S(1)}, u32[]{:S(2)}, u32[]{:S(2)}) collective-permute-start(bf16[528,384]{1,0:T(8,128)(2,1)S(1)} %get-tuple-element.66.refs_0_), channel_id=1, source_target_pairs={{0,24},{1,33},{2,26},{3,35},{4,28},{5,37},{6,30},{7,39},{8,16},{9,... | collective-permute-start | bytes 1216520 | tf_op jit(solution)/shard_map/ppermute | solution.py:450
  54.4 9.1 %collective-permute-start.12 = (bf16[528,384]{1,0:T(8,128)(2,1)S(1)}, bf16[528,384]{1,0:T(8,128)(2,1)S(1)}, u32[]{:S(2)}, u32[]{:S(2)}) collective-permute-start(bf16[528,384]{1,0:T(8,128)(2,1)S(1)} %collective-permute-done.10.refs_1_), channel_id=1, source_target_pairs={{0,24},{1,33},{2,26},{3,35},{4,28},{5,37},{6,30},{7,39},{8,16},{9,... | collective-permute-start | bytes 1216520 | tf_op jit(solution)/shard_map/ppermute | solution.py:450
  56.6 18.7 %collective-permute-start.15 = (bf16[512,768]{1,0:T(8,128)(2,1)S(1)}, bf16[512,768]{1,0:T(8,128)(2,1)S(1)}, u32[]{:S(2)}, u32[]{:S(2)}) collective-permute-start(bf16[512,768]{1,0:T(8,128)(2,1)S(1)} %collective-permute-done.13.refs_5_), channel_id=1, source_target_pairs={{0,96},{1,9},{2,98},{3,11},{4,100},{5,13},{6,102},{7,15},{8,104},{... | collective-permute-start | bytes 2359304 | tf_op jit(solution)/shard_map/ppermute | solution.py:450
  63.5 31.0 %slice-start = ((s8[4718592]{0:T(1024)(128)(4,1)}), s8[4194304]{0:T(1024)(128)(4,1)S(1)}, s32[]{:S(2)}) async-start(s8[4718592]{0:T(1024)(128)(4,1)} %bitcast.9), calls=%async_computation | async-start | bytes 8388608
  75.4 19.1 %slice-start.1 = ((s8[4718592]{0:T(1024)(128)(4,1)}), s8[524288]{0:T(1024)(128)(4,1)S(1)}, s32[]{:S(2)}) async-start(s8[4718592]{0:T(1024)(128)(4,1)} %bitcast.9), calls=%async_computation.1 | async-start | bytes 1048576
  90.3 8.2 %collective-permute-start.16 = (bf16[528,384]{1,0:T(8,128)(2,1)S(1)}, bf16[528,384]{1,0:T(8,128)(2,1)S(1)}, u32[]{:S(2)}, u32[]{:S(2)}) collective-permute-start(bf16[528,384]{1,0:T(8,128)(2,1)S(1)} %get-tuple-element.78), channel_id=1, source_target_pairs={{0,8},{1,97},{2,10},{3,99},{4,12},{5,101},{6,14},{7,103},{8,0},{9,... | collective-permute-start | bytes 1216520 | tf_op jit(solution)/shard_map/ppermute | solution.py:450
  90.4 12.1 %collective-permute-start.17 = (bf16[528,384]{1,0:T(8,128)(2,1)S(1)}, bf16[528,384]{1,0:T(8,128)(2,1)S(1)}, u32[]{:S(2)}, u32[]{:S(2)}) collective-permute-start(bf16[528,384]{1,0:T(8,128)(2,1)S(1)} %get-tuple-element.79), channel_id=1, source_target_pairs={{0,24},{1,33},{2,26},{3,35},{4,28},{5,37},{6,30},{7,39},{8,16},{9,... | collective-permute-start | bytes 1216520 | tf_op jit(solution)/shard_map/ppermute | solution.py:450
  92.7 11.6 %copy-start = (bf16[384,3072]{1,0:T(8,128)(2,1)S(1)}, bf16[384,3072]{1,0:T(8,128)(2,1)}, u32[]{:S(2)}) copy-start(bf16[384,3072]{1,0:T(8,128)(2,1)} %w_ref.11) | copy-start | bytes 7077892
  92.7 11.6 %collective-permute-start.18 = (bf16[528,384]{1,0:T(8,128)(2,1)S(1)}, bf16[528,384]{1,0:T(8,128)(2,1)S(1)}, u32[]{:S(2)}, u32[]{:S(2)}) collective-permute-start(bf16[528,384]{1,0:T(8,128)(2,1)S(1)} %get-tuple-element.80), channel_id=1, source_target_pairs={{0,16},{1,65},{2,18},{3,67},{4,20},{5,69},{6,22},{7,71},{8,24},{9,... | collective-permute-start | bytes 1216520 | tf_op jit(solution)/shard_map/ppermute | solution.py:450
  106.3 1.8 %collective-permute-start.19 = (bf16[512,384]{1,0:T(8,128)(2,1)S(1)}, bf16[512,384]{1,0:T(8,128)(2,1)S(1)}, u32[]{:S(2)}, u32[]{:S(2)}) collective-permute-start(bf16[512,384]{1,0:T(8,128)(2,1)S(1)} %get-tuple-element.84), channel_id=1, source_target_pairs={{0,1},{1,0},{2,3},{3,2},{4,5},{5,4},{6,7},{7,6},{8,9},{9,8},{10,11... | collective-permute-start | bytes 1179656 | tf_op jit(solution)/shard_map/ppermute | solution.py:464
  109.5 3.3 %collective-permute-start.24 = (bf16[512,384]{1,0:T(8,128)(2,1)S(1)}, bf16[512,384]{1,0:T(8,128)(2,1)S(1)}, u32[]{:S(2)}, u32[]{:S(2)}) collective-permute-start(bf16[512,384]{1,0:T(8,128)(2,1)S(1)} %get-tuple-element.94), channel_id=1, source_target_pairs={{0,1},{1,0},{2,3},{3,2},{4,5},{5,4},{6,7},{7,6},{8,9},{9,8},{10,11... | collective-permute-start | bytes 1179656 | tf_op jit(solution)/shard_map/ppermute | solution.py:464
  109.7 10.8 %collective-permute-start.20 = (bf16[512,384]{1,0:T(8,128)(2,1)S(1)}, bf16[512,384]{1,0:T(8,128)(2,1)S(1)}, u32[]{:S(2)}, u32[]{:S(2)}) collective-permute-start(bf16[512,384]{1,0:T(8,128)(2,1)S(1)} %add_convert_fusion.2), channel_id=1, source_target_pairs={{0,2},{1,7},{2,4},{3,1},{4,6},{5,3},{6,0},{7,5},{8,10},{9,15},{10,... | collective-permute-start | bytes 1179656 | tf_op jit(solution)/shard_map/ppermute | solution.py:454
  110.9 10.9 %collective-permute-start.22 = (bf16[512,384]{1,0:T(8,128)(2,1)S(1)}, bf16[512,384]{1,0:T(8,128)(2,1)S(1)}, u32[]{:S(2)}, u32[]{:S(2)}) collective-permute-start(bf16[512,384]{1,0:T(8,128)(2,1)S(1)} %get-tuple-element.91), channel_id=1, source_target_pairs={{0,1},{1,0},{2,3},{3,2},{4,5},{5,4},{6,7},{7,6},{8,9},{9,8},{10,11... | collective-permute-start | bytes 1179656 | tf_op jit(solution)/shard_map/ppermute | solution.py:464
  112.9 10.8 %collective-permute-start.25 = (bf16[512,384]{1,0:T(8,128)(2,1)S(1)}, bf16[512,384]{1,0:T(8,128)(2,1)S(1)}, u32[]{:S(2)}, u32[]{:S(2)}) collective-permute-start(bf16[512,384]{1,0:T(8,128)(2,1)S(1)} %add_convert_fusion), channel_id=1, source_target_pairs={{0,6},{1,3},{2,0},{3,5},{4,2},{5,7},{6,4},{7,1},{8,14},{9,11},{10,... | collective-permute-start | bytes 1179656 | tf_op jit(solution)/shard_map/ppermute | solution.py:454
  121.7 1.8 %collective-permute-start.21 = (bf16[512,384]{1,0:T(8,128)(2,1)S(1)}, bf16[512,384]{1,0:T(8,128)(2,1)S(1)}, u32[]{:S(2)}, u32[]{:S(2)}) collective-permute-start(bf16[512,384]{1,0:T(8,128)(2,1)S(1)} %get-tuple-element.89), channel_id=1, source_target_pairs={{0,1},{1,0},{2,3},{3,2},{4,5},{5,4},{6,7},{7,6},{8,9},{9,8},{10,11... | collective-permute-start | bytes 1179656 | tf_op jit(solution)/shard_map/ppermute | solution.py:464
  122.0 9.1 %collective-permute-start.23 = (bf16[512,384]{1,0:T(8,128)(2,1)S(1)}, bf16[512,384]{1,0:T(8,128)(2,1)S(1)}, u32[]{:S(2)}, u32[]{:S(2)}) collective-permute-start(bf16[512,384]{1,0:T(8,128)(2,1)S(1)} %add_convert_fusion.1), channel_id=1, source_target_pairs={{0,2},{1,7},{2,4},{3,1},{4,6},{5,3},{6,0},{7,5},{8,10},{9,15},{10,... | collective-permute-start | bytes 1179656 | tf_op jit(solution)/shard_map/ppermute | solution.py:454

commit v5 on v4

--- a/solution.py
+++ b/solution.py
@@ -206,7 +206,7 @@
     return call(
         mlp_kernel, [modded], [((rows, hidden), BF16)], far=[w_mlp],
         scratch=[VMEM((3, features, hidden // 3), BF16), pltpu.SemaphoreType.DMA((3,))],
-        cost=5 * PER_US, name="mlp_in",
+        cost=8 * PER_US, name="mlp_in",
     )[0]
 
 
@@ -379,31 +379,33 @@
             attn_ref[here, cols] = mixed.astype(BF16)
 
 
-def chunk_dots(place, k, attn_ref, mlp_ref, w_ref, send_ref, keep_ref):
+def branch_kernel(place, *refs, chunks, mixing):
+    refs = list(refs)
+    if mixing:
+        parts, (mlp_ref, w_ref, attn_ref), outs = refs[:SIDE], refs[SIDE : SIDE + 3], refs[SIDE + 3 :]
+        mix_kernel(*parts, attn_ref)
+    else:
+        (attn_ref, mlp_ref, w_ref), outs = refs[:3], refs[3:]
     width = attn_ref.shape[1]
-    for n, out_ref in ((NZ + k, send_ref), (k, keep_ref)):
-        cols = columns(place, n, width)
-        acc = jnp.dot(attn_ref[...], w_ref[:, cols], preferred_element_type=F32) + mlp_ref[n]
-        out_ref[...] = acc.astype(BF16)
-
-
-def branch_first_kernel(place, p0, p1, p2, p3, mlp_ref, w_ref, attn_ref, send_ref, keep_ref, *, k):
-    mix_kernel(p0, p1, p2, p3, attn_ref)
-    chunk_dots(place, k, attn_ref, mlp_ref, w_ref, send_ref, keep_ref)
-
-
-def branch_next_kernel(place, attn_ref, mlp_ref, w_ref, send_ref, keep_ref, *, k):
-    chunk_dots(place, k, attn_ref, mlp_ref, w_ref, send_ref, keep_ref)
-
-
-def branch(place, inputs, mlp_branch, w_attn, k):
+    for i, k in enumerate(chunks):
+        for n, out_ref in ((NZ + k, outs[2 * i]), (k, outs[2 * i + 1])):
+            cols = columns(place, n, width)
+            acc = jnp.dot(attn_ref[...], w_ref[:, cols], preferred_element_type=F32) + mlp_ref[n]
+            out_ref[...] = acc.astype(BF16)
+
+
+def branch(place, inputs, mlp_branch, w_attn, chunks):
     _, rows, width = mlp_branch.shape
-    first = len(inputs) == SIDE
+    mixing = len(inputs) == SIDE
     return call(
-        functools.partial(branch_first_kernel if first else branch_next_kernel, k=k),
-        [*inputs, mlp_branch, w_attn], [((rows, width), BF16)] * (3 if first else 2),
+        functools.partial(branch_kernel, chunks=chunks, mixing=mixing),
+        [*inputs, mlp_branch, w_attn], [((rows, width), BF16)] * (mixing + 2 * len(chunks)),
         scalars=place, name="branch",
     )
+
+
+def chip_sum(send, keep):
+    return keep.astype(F32) + other_core(send).astype(F32)
 
 
 def finish_kernel(place, rows_ref, mine_ref, s1, s2, gate_ref, out_ref):
@@ -486,10 +488,10 @@
     w_qkv = jnp.transpose(w_qkv, (1, 0, 2))
 
     rows, rest = pick(block_order, hidden, key_cache, value_cache)
+    rest_first, rest_second = along("a", "first", rest), along("a", "second", rest)
     near, away = up_or_down(rows), up_or_down(rows, (3, 1))
     own = [rows, near, away, up_or_down(near)]
     pieces = own + [other_core(a) for a in own]
-    rest_first, rest_second = along("a", "first", rest), along("a", "second", rest)
     pieces, rest_first, rest_second = lax.optimization_barrier((pieces, rest_first, rest_second))
     rest_opposite = along("a", "second", rest_first)
 
@@ -508,19 +510,15 @@
     kinds = ("first", "second", "opposite")
     back = [parts[0]] + [along("b", kind, parts[n + 1]) for n, kind in enumerate(kinds)]
     mlp_branch = mlp_out(place, mlp_hidden, w_out_mlp)
-    attn, send, keep = branch(place, back, mlp_branch, w_out_attn, 0)
-    across = (keep.astype(F32) + other_core(send).astype(F32)).astype(BF16)
+    attn, *pairs = branch(place, back, mlp_branch, w_out_attn, (0, 2))
+    across, away = chip_sum(*pairs[:2]).astype(BF16), chip_sum(*pairs[2:]).astype(BF16)
     attn, across = lax.optimization_barrier((attn, across))
     across = up_or_down(across)
-    chips = []
-    for k in (2, 1, 3):
-        if k == 3:
-            attn, across = lax.optimization_barrier((attn, across))
-        send, keep = branch(place, [attn], mlp_branch, w_out_attn, k)
-        chips.append(keep.astype(F32) + other_core(send).astype(F32))
-    near = up_or_down((chips[1] + across.astype(F32)).astype(BF16))
-    away = up_or_down(chips[0].astype(BF16), (3, 1))
-    return finish(place, rows, chips[2], [near, away], gate)
+    near = chip_sum(*branch(place, [attn], mlp_branch, w_out_attn, (1,)))
+    attn, across = lax.optimization_barrier((attn, across))
+    near = up_or_down((near + across.astype(F32)).astype(BF16))
+    mine = chip_sum(*branch(place, [attn], mlp_branch, w_out_attn, (3,)))
+    return finish(place, rows, mine, [near, up_or_down(away, (3, 1))], gate)
 
 
 def solution(mesh):

time: 131 us -> 128 us (0.977)
  the two profiles are of different devices: /device:TPU:8 before, /device:TPU:0 now
where the time goes in v5:
time: 128 us
  Pallas kernels  49.8 us (39%)
  waiting for transfers between devices  42 us (33%)
  starting transfers between devices  32.7 us (26%)
  local copies, waits for them, and re-layouts  2.11 us (2%)
    pallas_call x9, Pallas kernels, call(): pl.pallas_call(kernel, in_specs=specs, out_specs=[spec(VMEM)] * len(outs)...  48.2 us
    ppermute x6, waiting for transfers between devices, up_or_down(): lax.ppermute(a, 'head', [(z * 2 + c, (z + steps[c]) % 4 * 2 + c) for z in...  24.4 us
    ppermute x12, starting transfers between devices, along(): return lax.ppermute(a, ('patch', 'head'), pairs)  21.6 us
    ppermute x12, waiting for transfers between devices, along(): return lax.ppermute(a, ('patch', 'head'), pairs)  15 us
    ppermute x6, starting transfers between devices, up_or_down(): lax.ppermute(a, 'head', [(z * 2 + c, (z + steps[c]) % 4 * 2 + c) for z in...  7 us
    ppermute x8, starting transfers between devices, other_core(): return lax.ppermute(a, 'head', [(i, i ^ 1) for i in range(8)])  4.14 us
  transfers between devices with their start and end apart: 26, of which 11 were waited for; matrix products, arithmetic and copies ran while one was open for 2% of the time, Pallas kernels for 25%

profile of v5, /device:TPU:0, one launch (start us, length us, event | category | flops | bytes accessed | tf_op | source)
XLA Modules:
  0.0 128.0 jit_solution(13278068561450524653)
XLA Ops:
  0.0 0.7 copy-done.1
  0.7 2.0 %pick.1 = (bf16[512,384]{1,0:T(8,128)(2,1)S(1)}, bf16[512,768]{1,0:T(8,128)(2,1)S(1)}) custom-call(s32[1,8]{1,0:T(1,128)S(1)} %copy-done.1, bf16[1024,384]{1,0:T(8,128)(2,1)} %hidden.1, bf16[1024,384]{1,0:T(8,128)(2,1)} %keys.3, bf16[1024,384]{1,0:T(8,128)(2,1)} %values.3), custom_call_target="tpu_custom_call" | custom-call | bytes 1000 | tf_op jit(solution)/shard_map/pick/pallas_call | solution.py:43
  2.6 2.1 %collective-permute-start = (bf16[512,384]{1,0:T(8,128)(2,1)S(1)}, bf16[512,384]{1,0:T(8,128)(2,1)S(1)}, u32[]{:S(2)}, u32[]{:S(2)}) collective-permute-start(bf16[512,384]{1,0:T(8,128)(2,1)S(1)} %get-tuple-element.52.p0.rows_ref), channel_id=1, source_target_pairs={{0,2},{1,7},{2,4},{3,1},{4,6},{5,3},{6,0},{7,5},{8,10},{9,15},{10,... | collective-permute-start | bytes 1179656 | tf_op jit(solution)/shard_map/ppermute | solution.py:456
  4.7 2.2 %collective-permute-start.1 = (bf16[512,384]{1,0:T(8,128)(2,1)S(1)}, bf16[512,384]{1,0:T(8,128)(2,1)S(1)}, u32[]{:S(2)}, u32[]{:S(2)}) collective-permute-start(bf16[512,384]{1,0:T(8,128)(2,1)S(1)} %get-tuple-element.52.p0.rows_ref), channel_id=1, source_target_pairs={{0,6},{1,3},{2,0},{3,5},{4,2},{5,7},{6,4},{7,1},{8,14},{9,11},{10,... | collective-permute-start | bytes 1179656 | tf_op jit(solution)/shard_map/ppermute | solution.py:456
  6.9 0.0 collective-permute-start.3
  6.9 1.6 %collective-permute-start.7 = (bf16[512,768]{1,0:T(8,128)(2,1)S(1)}, bf16[512,768]{1,0:T(8,128)(2,1)S(1)}, u32[]{:S(2)}, u32[]{:S(2)}) collective-permute-start(bf16[512,768]{1,0:T(8,128)(2,1)S(1)} %get-tuple-element.51.refs_4_), channel_id=1, source_target_pairs={{0,32},{1,25},{2,34},{3,27},{4,36},{5,29},{6,38},{7,31},{8,40},{9,... | collective-permute-start | bytes 2359304 | tf_op jit(solution)/shard_map/ppermute | solution.py:452
  8.5 2.2 %collective-permute-start.8 = (bf16[512,768]{1,0:T(8,128)(2,1)S(1)}, bf16[512,768]{1,0:T(8,128)(2,1)S(1)}, u32[]{:S(2)}, u32[]{:S(2)}) collective-permute-start(bf16[512,768]{1,0:T(8,128)(2,1)S(1)} %get-tuple-element.51.refs_4_), channel_id=1, source_target_pairs={{0,96},{1,9},{2,98},{3,11},{4,100},{5,13},{6,102},{7,15},{8,104},{... | collective-permute-start | bytes 2359304 | tf_op jit(solution)/shard_map/ppermute | solution.py:452
  10.7 4.2 %collective-permute-done.p1 = bf16[512,384]{1,0:T(8,128)(2,1)S(1)} collective-permute-done((bf16[512,384]{1,0:T(8,128)(2,1)S(1)}, bf16[512,384]{1,0:T(8,128)(2,1)S(1)}, u32[]{:S(2)}, u32[]{:S(2)}) %collective-permute-start) | collective-permute-done | bytes 393248 | tf_op jit(solution)/shard_map/ppermute | solution.py:456
  14.9 0.8 collective-permute-start.2
  15.7 0.0 collective-permute-done.1.p2
  15.7 1.8 %collective-permute-start.4 = (bf16[512,384]{1,0:T(8,128)(2,1)S(1)}, bf16[512,384]{1,0:T(8,128)(2,1)}, u32[]{:S(2)}, u32[]{:S(2)}) collective-permute-start(bf16[512,384]{1,0:T(8,128)(2,1)S(1)} %collective-permute-done.p1), channel_id=1, source_target_pairs={{0,1},{1,0},{2,3},{3,2},{4,5},{5,4},{6,7},{7,6},{8,9},{9,8},{10,11... | collective-permute-start | bytes 1179656 | tf_op jit(solution)/shard_map/ppermute | solution.py:466
  17.5 0.0 collective-permute-done.3.p4
  17.5 0.1 collective-permute-start.5
  17.6 6.4 %collective-permute-done.2.p3 = bf16[512,384]{1,0:T(8,128)(2,1)} collective-permute-done((bf16[512,384]{1,0:T(8,128)(2,1)S(1)}, bf16[512,384]{1,0:T(8,128)(2,1)}, u32[]{:S(2)}, u32[]{:S(2)}) %collective-permute-start.2) | collective-permute-done | bytes 393248 | tf_op jit(solution)/shard_map/ppermute | solution.py:456
  24.7 0.7 slice_bitcast_fusion
  25.3 0.1 add_bitcast_fusion.place
  25.4 0.0 collective-permute-done.4.p5
  25.4 0.0 collective-permute-done.5.p6
  25.4 0.0 collective-permute-done.7.refs_5_
  25.4 0.6 collective-permute-done.6.p7
  26.1 3.0 %collective-permute-start.9 = (bf16[512,768]{1,0:T(8,128)(2,1)S(1)}, bf16[512,768]{1,0:T(8,128)(2,1)S(1)}, u32[]{:S(2)}, u32[]{:S(2)}) collective-permute-start(bf16[512,768]{1,0:T(8,128)(2,1)S(1)} %collective-permute-done.7.refs_5_), channel_id=1, source_target_pairs={{0,96},{1,9},{2,98},{3,11},{4,100},{5,13},{6,102},{7,15},{8,104},{... | collective-permute-start | bytes 2359304 | tf_op jit(solution)/shard_map/ppermute | solution.py:452
  29.1 10.2 %project.1 = (bf16[528,384]{1,0:T(8,128)(2,1)S(1)}, bf16[512,768]{1,0:T(8,128)(2,1)S(1)}, bf16[512,3072]{1,0:T(8,128)(2,1)S(1)}) custom-call(s32[1,7]{1,0:T(1,128)S(1)} %add_bitcast_fusion.place, bf16[512,384]{1,0:T(8,128)(2,1)S(1)} %get-tuple-element.52.p0.rows_ref, bf16[512,384]{1,0:T(8,128)(2,1)} %copy-done.2, bf16[512,384]{1,0:T(8,128)(2,1)} %copy-done.3, ...), custom_call_target="tpu_custom_call" | custom-call | flops 11000000512 | bytes 1000 | tf_op jit(solution)/shard_map/project/pallas_call | solution.py:43
  39.3 0.0 collective-permute-done.9.refs_7_
  39.3 1.6 %collective-permute-start.10 = (bf16[528,384]{1,0:T(8,128)(2,1)S(1)}, bf16[528,384]{1,0:T(8,128)(2,1)S(1)}, u32[]{:S(2)}, u32[]{:S(2)}) collective-permute-start(bf16[528,384]{1,0:T(8,128)(2,1)S(1)} %get-tuple-element.66.refs_0_), channel_id=1, source_target_pairs={{0,8},{1,97},{2,10},{3,99},{4,12},{5,101},{6,14},{7,103},{8,0},{9,... | collective-permute-start | bytes 1216520 | tf_op jit(solution)/shard_map/ppermute | solution.py:452
  40.9 2.1 %collective-permute-start.11 = (bf16[528,384]{1,0:T(8,128)(2,1)S(1)}, bf16[528,384]{1,0:T(8,128)(2,1)S(1)}, u32[]{:S(2)}, u32[]{:S(2)}) collective-permute-start(bf16[528,384]{1,0:T(8,128)(2,1)S(1)} %get-tuple-element.66.refs_0_), channel_id=1, source_target_pairs={{0,24},{1,33},{2,26},{3,35},{4,28},{5,37},{6,30},{7,39},{8,16},{9,... | collective-permute-start | bytes 1216520 | tf_op jit(solution)/shard_map/ppermute | solution.py:452
  43.0 0.2 collective-permute-start.13
  43.2 2.7 %collective-permute-start.14 = (bf16[512,768]{1,0:T(8,128)(2,1)S(1)}, bf16[512,768]{1,0:T(8,128)(2,1)S(1)}, u32[]{:S(2)}, u32[]{:S(2)}) collective-permute-start(bf16[512,768]{1,0:T(8,128)(2,1)S(1)} %get-tuple-element.70.refs_4_), channel_id=1, source_target_pairs={{0,96},{1,9},{2,98},{3,11},{4,100},{5,13},{6,102},{7,15},{8,104},{... | collective-permute-start | bytes 2359304 | tf_op jit(solution)/shard_map/ppermute | solution.py:452
  45.9 4.7 %mlp_in.1.mlp_ref = bf16[512,768]{1,0:T(8,128)(2,1)S(1)} custom-call(bf16[512,3072]{1,0:T(8,128)(2,1)S(1)} %get-tuple-element.65.modded_ref, bf16[3072,768]{1,0:T(8,128)(2,1)} %w_ref.2), custom_call_target="tpu_custom_call" | custom-call | flops 8800000000 | bytes 1000 | tf_op jit(solution)/shard_map/mlp_in/pallas_call | solution.py:43
  50.6 3.8 %collective-permute-done.11.refs_2_ = bf16[528,384]{1,0:T(8,128)(2,1)S(1)} collective-permute-done((bf16[528,384]{1,0:T(8,128)(2,1)S(1)}, bf16[528,384]{1,0:T(8,128)(2,1)S(1)}, u32[]{:S(2)}, u32[]{:S(2)}) %collective-permute-start.11) | collective-permute-done | bytes 405536 | tf_op jit(solution)/shard_map/ppermute | solution.py:452
  54.4 2.1 %collective-permute-start.12 = (bf16[528,384]{1,0:T(8,128)(2,1)S(1)}, bf16[528,384]{1,0:T(8,128)(2,1)S(1)}, u32[]{:S(2)}, u32[]{:S(2)}) collective-permute-start(bf16[528,384]{1,0:T(8,128)(2,1)S(1)} %collective-permute-done.10.refs_1_), channel_id=1, source_target_pairs={{0,24},{1,33},{2,26},{3,35},{4,28},{5,37},{6,30},{7,39},{8,16},{9,... | collective-permute-start | bytes 1216520 | tf_op jit(solution)/shard_map/ppermute | solution.py:452
  56.5 3.7 %collective-permute-done.13.refs_5_ = bf16[512,768]{1,0:T(8,128)(2,1)S(1)} collective-permute-done((bf16[512,768]{1,0:T(8,128)(2,1)S(1)}, bf16[512,768]{1,0:T(8,128)(2,1)S(1)}, u32[]{:S(2)}, u32[]{:S(2)}) %collective-permute-start.13) | collective-permute-done | bytes 786464 | tf_op jit(solution)/shard_map/ppermute | solution.py:452
  60.2 0.0 collective-permute-done.14.refs_6_
  60.2 2.0 %collective-permute-start.15 = (bf16[512,768]{1,0:T(8,128)(2,1)S(1)}, bf16[512,768]{1,0:T(8,128)(2,1)S(1)}, u32[]{:S(2)}, u32[]{:S(2)}) collective-permute-start(bf16[512,768]{1,0:T(8,128)(2,1)S(1)} %collective-permute-done.13.refs_5_), channel_id=1, source_target_pairs={{0,96},{1,9},{2,98},{3,11},{4,100},{5,13},{6,102},{7,15},{8,104},{... | collective-permute-start | bytes 2359304 | tf_op jit(solution)/shard_map/ppermute | solution.py:452
  62.2 0.1 pad_add_fusion.place
  62.3 1.2 collective-permute-done.12.refs_3_
  63.5 10.1 %attend_first.1 = (f32[2176,384]{1,0:T(8,128)S(1)}, f32[2176,384]{1,0:T(8,128)S(1)}) custom-call(bf16[528,384]{1,0:T(8,128)(2,1)S(1)} %get-tuple-element.66.refs_0_, bf16[528,384]{1,0:T(8,128)(2,1)S(1)} %collective-permute-done.10.refs_1_, bf16[528,384]{1,0:T(8,128)(2,1)S(1)} %collective-permute-done.11.refs_2_, ...), custom_call_target="tpu_custom_call" | custom-call | flops 5500000256 | bytes 1000 | tf_op jit(solution)/shard_map/attend_first/pallas_call | solution.py:43
  73.7 0.0 slice-start.1
  73.7 12.3 %attend_last.1 = (bf16[528,384]{1,0:T(8,128)(2,1)S(1)}, bf16[528,384]{1,0:T(8,128)(2,1)S(1)}, bf16[528,384]{1,0:T(8,128)(2,1)S(1)}, bf16[528,384]{1,0:T(8,128)(2,1)S(1)}) custom-call(bf16[528,384]{1,0:T(8,128)(2,1)S(1)} %get-tuple-element.66.refs_0_, bf16[528,384]{1,0:T(8,128)(2,1)S(1)} %collective-permute-done.10.refs_1_, ...), custom_call_target="tpu_custom_call" | custom-call | flops 9900000256 | bytes 1000 | tf_op jit(solution)/shard_map/attend_last/pallas_call | solution.py:43
  86.0 0.9 collective-permute-start.16
  86.9 1.3 %collective-permute-start.17 = (bf16[528,384]{1,0:T(8,128)(2,1)S(1)}, bf16[528,384]{1,0:T(8,128)(2,1)S(1)}, u32[]{:S(2)}, u32[]{:S(2)}) collective-permute-start(bf16[528,384]{1,0:T(8,128)(2,1)S(1)} %get-tuple-element.79), channel_id=1, source_target_pairs={{0,24},{1,33},{2,26},{3,35},{4,28},{5,37},{6,30},{7,39},{8,16},{9,... | collective-permute-start | bytes 1216520 | tf_op jit(solution)/shard_map/ppermute | solution.py:452
  88.3 1.9 %collective-permute-start.18 = (bf16[528,384]{1,0:T(8,128)(2,1)S(1)}, bf16[528,384]{1,0:T(8,128)(2,1)S(1)}, u32[]{:S(2)}, u32[]{:S(2)}) collective-permute-start(bf16[528,384]{1,0:T(8,128)(2,1)S(1)} %get-tuple-element.80), channel_id=1, source_target_pairs={{0,16},{1,65},{2,18},{3,67},{4,20},{5,69},{6,22},{7,71},{8,24},{9,... | collective-permute-start | bytes 1216520 | tf_op jit(solution)/shard_map/ppermute | solution.py:452
  90.2 4.0 %mlp_out.1.refs_4_.refs_1_ = f32[8,512,384]{2,1,0:T(8,128)S(1)} custom-call(s32[3]{0:T(128)S(1)} %pad_add_fusion.place, bf16[512,768]{1,0:T(8,128)(2,1)S(1)} %mlp_in.1.mlp_ref, bf16[768,3072]{1,0:T(8,128)(2,1)S(1)} %bitcast.10), custom_call_target="tpu_custom_call" | custom-call | flops 4400000000 | bytes 1000 | tf_op jit(solution)/shard_map/mlp_out/pallas_call | solution.py:43
  94.2 6.2 %collective-permute-done.17.refs_2_ = bf16[528,384]{1,0:T(8,128)(2,1)S(1)} collective-permute-done((bf16[528,384]{1,0:T(8,128)(2,1)S(1)}, bf16[528,384]{1,0:T(8,128)(2,1)S(1)}, u32[]{:S(2)}, u32[]{:S(2)}) %collective-permute-start.17) | collective-permute-done | bytes 405536 | tf_op jit(solution)/shard_map/ppermute | solution.py:452
  100.4 2.5 %branch.3 = (bf16[512,384]{1,0:T(8,128)(2,1)S(1)}, bf16[512,384]{1,0:T(8,128)(2,1)S(1)}, bf16[512,384]{1,0:T(8,128)(2,1)S(1)}, bf16[512,384]{1,0:T(8,128)(2,1)S(1)}, bf16[512,384]{1,0:T(8,128)(2,1)S(1)}) custom-call(s32[3]{0:T(128)S(1)} %pad_add_fusion.place, bf16[528,384]{1,0:T(8,128)(2,1)S(1)} %get-tuple-element.77.refs_0_, ...), custom_call_target="tpu_custom_call" | custom-call | bytes 1000 | tf_op jit(solution)/shard_map/branch/pallas_call | solution.py:43
  102.9 0.1 collective-permute-start.19
  103.0 0.5 collective-permute-start.24
  103.5 1.2 collective-permute-done.19
  104.7 0.1 add_convert_fusion.2
  104.8 0.1 collective-permute-start.20
  104.9 1.2 branch.5
  106.1 1.6 %collective-permute-start.22 = (bf16[512,384]{1,0:T(8,128)(2,1)S(1)}, bf16[512,384]{1,0:T(8,128)(2,1)S(1)}, u32[]{:S(2)}, u32[]{:S(2)}) collective-permute-start(bf16[512,384]{1,0:T(8,128)(2,1)S(1)} %get-tuple-element.91), channel_id=1, source_target_pairs={{0,1},{1,0},{2,3},{3,2},{4,5},{5,4},{6,7},{7,6},{8,9},{9,8},{10,11... | collective-permute-start | bytes 1179656 | tf_op jit(solution)/shard_map/ppermute | solution.py:466
  107.7 0.0 collective-permute-done.24
  107.7 0.1 add_convert_fusion
  107.8 1.8 %collective-permute-start.25 = (bf16[512,384]{1,0:T(8,128)(2,1)S(1)}, bf16[512,384]{1,0:T(8,128)(2,1)S(1)}, u32[]{:S(2)}, u32[]{:S(2)}) collective-permute-start(bf16[512,384]{1,0:T(8,128)(2,1)S(1)} %add_convert_fusion), channel_id=1, source_target_pairs={{0,6},{1,3},{2,0},{3,5},{4,2},{5,7},{6,4},{7,1},{8,14},{9,11},{10,... | collective-permute-start | bytes 1179656 | tf_op jit(solution)/shard_map/ppermute | solution.py:456
  109.6 6.4 %collective-permute-done.20 = bf16[512,384]{1,0:T(8,128)(2,1)S(1)} collective-permute-done((bf16[512,384]{1,0:T(8,128)(2,1)S(1)}, bf16[512,384]{1,0:T(8,128)(2,1)S(1)}, u32[]{:S(2)}, u32[]{:S(2)}) %collective-permute-start.20) | collective-permute-done | bytes 393248 | tf_op jit(solution)/shard_map/ppermute | solution.py:456
  116.0 1.2 branch.4
  117.2 0.1 collective-permute-start.21
  117.3 0.1 add_convert_fusion.1
  117.5 0.1 collective-permute-start.23
  117.5 0.8 constant_dynamic-slice_fusion.gate_ref
  118.3 0.7 collective-permute-done.21
  119.0 0.1 convert_add_fusion.mine_ref
  119.1 7.4 %collective-permute-done.23.s1 = bf16[512,384]{1,0:T(8,128)(2,1)S(1)} collective-permute-done((bf16[512,384]{1,0:T(8,128)(2,1)S(1)}, bf16[512,384]{1,0:T(8,128)(2,1)S(1)}, u32[]{:S(2)}, u32[]{:S(2)}) %collective-permute-start.23) | collective-permute-done | bytes 393248 | tf_op jit(solution)/shard_map/ppermute | solution.py:456
  126.5 1.5 %finish.1 = bf16[512,384]{1,0:T(8,128)(2,1)} custom-call(s32[3]{0:T(128)S(1)} %pad_add_fusion.place, bf16[512,384]{1,0:T(8,128)(2,1)S(1)} %get-tuple-element.52.p0.rows_ref, f32[512,384]{1,0:T(8,128)S(1)} %convert_add_fusion.mine_ref, bf16[512,384]{1,0:T(8,128)(2,1)S(1)} %collective-permute-done.23.s1, bf16[512,384]{1,0:T(8,128)(2,1)S(1)} %collective-permute-done.25.s2, ...), custom_call_target="tpu_custom_call" | custom-call | tf_op jit(solution)/shard_map/finish/pallas_call | solution.py:422
  (21 shorter events, 0.0 us)
Async XLA Ops:
  0.0 0.7 copy-start.1
  2.6 12.3 %collective-permute-start = (bf16[512,384]{1,0:T(8,128)(2,1)S(1)}, bf16[512,384]{1,0:T(8,128)(2,1)S(1)}, u32[]{:S(2)}, u32[]{:S(2)}) collective-permute-start(bf16[512,384]{1,0:T(8,128)(2,1)S(1)} %get-tuple-element.52.p0.rows_ref), channel_id=1, source_target_pairs={{0,2},{1,7},{2,4},{3,1},{4,6},{5,3},{6,0},{7,5},{8,10},{9,15},{10,... | collective-permute-start | bytes 1179656 | tf_op jit(solution)/shard_map/ppermute | solution.py:456
  4.7 11.0 %collective-permute-start.1 = (bf16[512,384]{1,0:T(8,128)(2,1)S(1)}, bf16[512,384]{1,0:T(8,128)(2,1)S(1)}, u32[]{:S(2)}, u32[]{:S(2)}) collective-permute-start(bf16[512,384]{1,0:T(8,128)(2,1)S(1)} %get-tuple-element.52.p0.rows_ref), channel_id=1, source_target_pairs={{0,6},{1,3},{2,0},{3,5},{4,2},{5,7},{6,4},{7,1},{8,14},{9,11},{10,... | collective-permute-start | bytes 1179656 | tf_op jit(solution)/shard_map/ppermute | solution.py:456
  6.9 10.6 %collective-permute-start.3 = (bf16[512,384]{1,0:T(8,128)(2,1)S(1)}, bf16[512,384]{1,0:T(8,128)(2,1)S(1)}, u32[]{:S(2)}, u32[]{:S(2)}) collective-permute-start(bf16[512,384]{1,0:T(8,128)(2,1)S(1)} %get-tuple-element.52.p0.rows_ref), channel_id=1, source_target_pairs={{0,1},{1,0},{2,3},{3,2},{4,5},{5,4},{6,7},{7,6},{8,9},{9,8},{10,11... | collective-permute-start | bytes 1179656 | tf_op jit(solution)/shard_map/ppermute | solution.py:466
  6.9 18.5 %collective-permute-start.7 = (bf16[512,768]{1,0:T(8,128)(2,1)S(1)}, bf16[512,768]{1,0:T(8,128)(2,1)S(1)}, u32[]{:S(2)}, u32[]{:S(2)}) collective-permute-start(bf16[512,768]{1,0:T(8,128)(2,1)S(1)} %get-tuple-element.51.refs_4_), channel_id=1, source_target_pairs={{0,32},{1,25},{2,34},{3,27},{4,36},{5,29},{6,38},{7,31},{8,40},{9,... | collective-permute-start | bytes 2359304 | tf_op jit(solution)/shard_map/ppermute | solution.py:452
  8.5 16.9 %collective-permute-start.8 = (bf16[512,768]{1,0:T(8,128)(2,1)S(1)}, bf16[512,768]{1,0:T(8,128)(2,1)S(1)}, u32[]{:S(2)}, u32[]{:S(2)}) collective-permute-start(bf16[512,768]{1,0:T(8,128)(2,1)S(1)} %get-tuple-element.51.refs_4_), channel_id=1, source_target_pairs={{0,96},{1,9},{2,98},{3,11},{4,100},{5,13},{6,102},{7,15},{8,104},{... | collective-permute-start | bytes 2359304 | tf_op jit(solution)/shard_map/ppermute | solution.py:452
  14.9 14.2 %copy-start.2 = (bf16[512,384]{1,0:T(8,128)(2,1)}, bf16[512,384]{1,0:T(8,128)(2,1)S(1)}, u32[]{:S(2)}) copy-start(bf16[512,384]{1,0:T(8,128)(2,1)S(1)} %collective-permute-done.p1) | copy-start | bytes 1179652
  14.9 9.1 %collective-permute-start.2 = (bf16[512,384]{1,0:T(8,128)(2,1)S(1)}, bf16[512,384]{1,0:T(8,128)(2,1)}, u32[]{:S(2)}, u32[]{:S(2)}) collective-permute-start(bf16[512,384]{1,0:T(8,128)(2,1)S(1)} %collective-permute-done.p1), channel_id=1, source_target_pairs={{0,2},{1,7},{2,4},{3,1},{4,6},{5,3},{6,0},{7,5},{8,10},{9,15},{10,... | collective-permute-start | bytes 1179656 | tf_op jit(solution)/shard_map/ppermute | solution.py:456
  15.7 13.4 %copy-start.3 = (bf16[512,384]{1,0:T(8,128)(2,1)}, bf16[512,384]{1,0:T(8,128)(2,1)S(1)}, u32[]{:S(2)}) copy-start(bf16[512,384]{1,0:T(8,128)(2,1)S(1)} %collective-permute-done.1.p2) | copy-start | bytes 1179652
  15.7 9.7 %collective-permute-start.4 = (bf16[512,384]{1,0:T(8,128)(2,1)S(1)}, bf16[512,384]{1,0:T(8,128)(2,1)}, u32[]{:S(2)}, u32[]{:S(2)}) collective-permute-start(bf16[512,384]{1,0:T(8,128)(2,1)S(1)} %collective-permute-done.p1), channel_id=1, source_target_pairs={{0,1},{1,0},{2,3},{3,2},{4,5},{5,4},{6,7},{7,6},{8,9},{9,8},{10,11... | collective-permute-start | bytes 1179656 | tf_op jit(solution)/shard_map/ppermute | solution.py:466
  17.5 6.5 %copy-start.4 = (bf16[512,384]{1,0:T(8,128)(2,1)}, bf16[512,384]{1,0:T(8,128)(2,1)S(1)}, u32[]{:S(2)}) copy-start(bf16[512,384]{1,0:T(8,128)(2,1)S(1)} %collective-permute-done.3.p4) | copy-start | bytes 1179652
  17.5 7.9 %collective-permute-start.5 = (bf16[512,384]{1,0:T(8,128)(2,1)S(1)}, bf16[512,384]{1,0:T(8,128)(2,1)}, u32[]{:S(2)}, u32[]{:S(2)}) collective-permute-start(bf16[512,384]{1,0:T(8,128)(2,1)S(1)} %collective-permute-done.1.p2), channel_id=1, source_target_pairs={{0,1},{1,0},{2,3},{3,2},{4,5},{5,4},{6,7},{7,6},{8,9},{9,8},{10,11... | collective-permute-start | bytes 1179656 | tf_op jit(solution)/shard_map/ppermute | solution.py:466
  24.0 2.1 %collective-permute-start.6 = (bf16[512,384]{1,0:T(8,128)(2,1)}, bf16[512,384]{1,0:T(8,128)(2,1)}, u32[]{:S(2)}, u32[]{:S(2)}) collective-permute-start(bf16[512,384]{1,0:T(8,128)(2,1)} %collective-permute-done.2.p3), channel_id=1, source_target_pairs={{0,1},{1,0},{2,3},{3,2},{4,5},{5,4},{6,7},{7,6},{8,9},{9,8},{10,11... | collective-permute-start | bytes 1179656 | tf_op jit(solution)/shard_map/ppermute | solution.py:466
  26.1 13.2 %collective-permute-start.9 = (bf16[512,768]{1,0:T(8,128)(2,1)S(1)}, bf16[512,768]{1,0:T(8,128)(2,1)S(1)}, u32[]{:S(2)}, u32[]{:S(2)}) collective-permute-start(bf16[512,768]{1,0:T(8,128)(2,1)S(1)} %collective-permute-done.7.refs_5_), channel_id=1, source_target_pairs={{0,96},{1,9},{2,98},{3,11},{4,100},{5,13},{6,102},{7,15},{8,104},{... | collective-permute-start | bytes 2359304 | tf_op jit(solution)/shard_map/ppermute | solution.py:452
  39.3 11.3 %collective-permute-start.10 = (bf16[528,384]{1,0:T(8,128)(2,1)S(1)}, bf16[528,384]{1,0:T(8,128)(2,1)S(1)}, u32[]{:S(2)}, u32[]{:S(2)}) collective-permute-start(bf16[528,384]{1,0:T(8,128)(2,1)S(1)} %get-tuple-element.66.refs_0_), channel_id=1, source_target_pairs={{0,8},{1,97},{2,10},{3,99},{4,12},{5,101},{6,14},{7,103},{8,0},{9,... | collective-permute-start | bytes 1216520 | tf_op jit(solution)/shard_map/ppermute | solution.py:452
  40.9 13.5 %collective-permute-start.11 = (bf16[528,384]{1,0:T(8,128)(2,1)S(1)}, bf16[528,384]{1,0:T(8,128)(2,1)S(1)}, u32[]{:S(2)}, u32[]{:S(2)}) collective-permute-start(bf16[528,384]{1,0:T(8,128)(2,1)S(1)} %get-tuple-element.66.refs_0_), channel_id=1, source_target_pairs={{0,24},{1,33},{2,26},{3,35},{4,28},{5,37},{6,30},{7,39},{8,16},{9,... | collective-permute-start | bytes 1216520 | tf_op jit(solution)/shard_map/ppermute | solution.py:452
  43.0 17.2 %collective-permute-start.13 = (bf16[512,768]{1,0:T(8,128)(2,1)S(1)}, bf16[512,768]{1,0:T(8,128)(2,1)S(1)}, u32[]{:S(2)}, u32[]{:S(2)}) collective-permute-start(bf16[512,768]{1,0:T(8,128)(2,1)S(1)} %get-tuple-element.70.refs_4_), channel_id=1, source_target_pairs={{0,32},{1,25},{2,34},{3,27},{4,36},{5,29},{6,38},{7,31},{8,40},{9,... | collective-permute-start | bytes 2359304 | tf_op jit(solution)/shard_map/ppermute | solution.py:452
  43.2 17.0 %collective-permute-start.14 = (bf16[512,768]{1,0:T(8,128)(2,1)S(1)}, bf16[512,768]{1,0:T(8,128)(2,1)S(1)}, u32[]{:S(2)}, u32[]{:S(2)}) collective-permute-start(bf16[512,768]{1,0:T(8,128)(2,1)S(1)} %get-tuple-element.70.refs_4_), channel_id=1, source_target_pairs={{0,96},{1,9},{2,98},{3,11},{4,100},{5,13},{6,102},{7,15},{8,104},{... | collective-permute-start | bytes 2359304 | tf_op jit(solution)/shard_map/ppermute | solution.py:452
  54.4 9.1 %collective-permute-start.12 = (bf16[528,384]{1,0:T(8,128)(2,1)S(1)}, bf16[528,384]{1,0:T(8,128)(2,1)S(1)}, u32[]{:S(2)}, u32[]{:S(2)}) collective-permute-start(bf16[528,384]{1,0:T(8,128)(2,1)S(1)} %collective-permute-done.10.refs_1_), channel_id=1, source_target_pairs={{0,24},{1,33},{2,26},{3,35},{4,28},{5,37},{6,30},{7,39},{8,16},{9,... | collective-permute-start | bytes 1216520 | tf_op jit(solution)/shard_map/ppermute | solution.py:452
  60.2 13.5 %collective-permute-start.15 = (bf16[512,768]{1,0:T(8,128)(2,1)S(1)}, bf16[512,768]{1,0:T(8,128)(2,1)S(1)}, u32[]{:S(2)}, u32[]{:S(2)}) collective-permute-start(bf16[512,768]{1,0:T(8,128)(2,1)S(1)} %collective-permute-done.13.refs_5_), channel_id=1, source_target_pairs={{0,96},{1,9},{2,98},{3,11},{4,100},{5,13},{6,102},{7,15},{8,104},{... | collective-permute-start | bytes 2359304 | tf_op jit(solution)/shard_map/ppermute | solution.py:452
  63.5 26.7 %slice-start = ((s8[4718592]{0:T(1024)(128)(4,1)}), s8[4194304]{0:T(1024)(128)(4,1)S(1)}, s32[]{:S(2)}) async-start(s8[4718592]{0:T(1024)(128)(4,1)} %bitcast.9), calls=%async_computation | async-start | bytes 8388608
  73.7 16.5 %slice-start.1 = ((s8[4718592]{0:T(1024)(128)(4,1)}), s8[524288]{0:T(1024)(128)(4,1)S(1)}, s32[]{:S(2)}) async-start(s8[4718592]{0:T(1024)(128)(4,1)} %bitcast.9), calls=%async_computation.1 | async-start | bytes 1048576
  86.0 8.2 %collective-permute-start.16 = (bf16[528,384]{1,0:T(8,128)(2,1)S(1)}, bf16[528,384]{1,0:T(8,128)(2,1)S(1)}, u32[]{:S(2)}, u32[]{:S(2)}) collective-permute-start(bf16[528,384]{1,0:T(8,128)(2,1)S(1)} %get-tuple-element.78), channel_id=1, source_target_pairs={{0,8},{1,97},{2,10},{3,99},{4,12},{5,101},{6,14},{7,103},{8,0},{9,... | collective-permute-start | bytes 1216520 | tf_op jit(solution)/shard_map/ppermute | solution.py:452
  86.9 13.5 %collective-permute-start.17 = (bf16[528,384]{1,0:T(8,128)(2,1)S(1)}, bf16[528,384]{1,0:T(8,128)(2,1)S(1)}, u32[]{:S(2)}, u32[]{:S(2)}) collective-permute-start(bf16[528,384]{1,0:T(8,128)(2,1)S(1)} %get-tuple-element.79), channel_id=1, source_target_pairs={{0,24},{1,33},{2,26},{3,35},{4,28},{5,37},{6,30},{7,39},{8,16},{9,... | collective-permute-start | bytes 1216520 | tf_op jit(solution)/shard_map/ppermute | solution.py:452
  88.3 12.1 %copy-start = (bf16[384,3072]{1,0:T(8,128)(2,1)S(1)}, bf16[384,3072]{1,0:T(8,128)(2,1)}, u32[]{:S(2)}) copy-start(bf16[384,3072]{1,0:T(8,128)(2,1)} %refs_2_.3) | copy-start | bytes 7077892
  88.3 12.1 %collective-permute-start.18 = (bf16[528,384]{1,0:T(8,128)(2,1)S(1)}, bf16[528,384]{1,0:T(8,128)(2,1)S(1)}, u32[]{:S(2)}, u32[]{:S(2)}) collective-permute-start(bf16[528,384]{1,0:T(8,128)(2,1)S(1)} %get-tuple-element.80), channel_id=1, source_target_pairs={{0,16},{1,65},{2,18},{3,67},{4,20},{5,69},{6,22},{7,71},{8,24},{9,... | collective-permute-start | bytes 1216520 | tf_op jit(solution)/shard_map/ppermute | solution.py:452
  102.9 1.8 %collective-permute-start.19 = (bf16[512,384]{1,0:T(8,128)(2,1)S(1)}, bf16[512,384]{1,0:T(8,128)(2,1)S(1)}, u32[]{:S(2)}, u32[]{:S(2)}) collective-permute-start(bf16[512,384]{1,0:T(8,128)(2,1)S(1)} %get-tuple-element.84), channel_id=1, source_target_pairs={{0,1},{1,0},{2,3},{3,2},{4,5},{5,4},{6,7},{7,6},{8,9},{9,8},{10,11... | collective-permute-start | bytes 1179656 | tf_op jit(solution)/shard_map/ppermute | solution.py:466
  103.0 4.7 %collective-permute-start.24 = (bf16[512,384]{1,0:T(8,128)(2,1)S(1)}, bf16[512,384]{1,0:T(8,128)(2,1)S(1)}, u32[]{:S(2)}, u32[]{:S(2)}) collective-permute-start(bf16[512,384]{1,0:T(8,128)(2,1)S(1)} %get-tuple-element.94), channel_id=1, source_target_pairs={{0,1},{1,0},{2,3},{3,2},{4,5},{5,4},{6,7},{7,6},{8,9},{9,8},{10,11... | collective-permute-start | bytes 1179656 | tf_op jit(solution)/shard_map/ppermute | solution.py:466
  104.8 11.1 %collective-permute-start.20 = (bf16[512,384]{1,0:T(8,128)(2,1)S(1)}, bf16[512,384]{1,0:T(8,128)(2,1)S(1)}, u32[]{:S(2)}, u32[]{:S(2)}) collective-permute-start(bf16[512,384]{1,0:T(8,128)(2,1)S(1)} %add_convert_fusion.2), channel_id=1, source_target_pairs={{0,2},{1,7},{2,4},{3,1},{4,6},{5,3},{6,0},{7,5},{8,10},{9,15},{10,... | collective-permute-start | bytes 1179656 | tf_op jit(solution)/shard_map/ppermute | solution.py:456
  106.1 11.2 %collective-permute-start.22 = (bf16[512,384]{1,0:T(8,128)(2,1)S(1)}, bf16[512,384]{1,0:T(8,128)(2,1)S(1)}, u32[]{:S(2)}, u32[]{:S(2)}) collective-permute-start(bf16[512,384]{1,0:T(8,128)(2,1)S(1)} %get-tuple-element.91), channel_id=1, source_target_pairs={{0,1},{1,0},{2,3},{3,2},{4,5},{5,4},{6,7},{7,6},{8,9},{9,8},{10,11... | collective-permute-start | bytes 1179656 | tf_op jit(solution)/shard_map/ppermute | solution.py:466
  107.8 11.2 %collective-permute-start.25 = (bf16[512,384]{1,0:T(8,128)(2,1)S(1)}, bf16[512,384]{1,0:T(8,128)(2,1)S(1)}, u32[]{:S(2)}, u32[]{:S(2)}) collective-permute-start(bf16[512,384]{1,0:T(8,128)(2,1)S(1)} %add_convert_fusion), channel_id=1, source_target_pairs={{0,6},{1,3},{2,0},{3,5},{4,2},{5,7},{6,4},{7,1},{8,14},{9,11},{10,... | collective-permute-start | bytes 1179656 | tf_op jit(solution)/shard_map/ppermute | solution.py:456
  117.2 1.8 %collective-permute-start.21 = (bf16[512,384]{1,0:T(8,128)(2,1)S(1)}, bf16[512,384]{1,0:T(8,128)(2,1)S(1)}, u32[]{:S(2)}, u32[]{:S(2)}) collective-permute-start(bf16[512,384]{1,0:T(8,128)(2,1)S(1)} %get-tuple-element.89), channel_id=1, source_target_pairs={{0,1},{1,0},{2,3},{3,2},{4,5},{5,4},{6,7},{7,6},{8,9},{9,8},{10,11... | collective-permute-start | bytes 1179656 | tf_op jit(solution)/shard_map/ppermute | solution.py:466
  117.5 9.1 %collective-permute-start.23 = (bf16[512,384]{1,0:T(8,128)(2,1)S(1)}, bf16[512,384]{1,0:T(8,128)(2,1)S(1)}, u32[]{:S(2)}, u32[]{:S(2)}) collective-permute-start(bf16[512,384]{1,0:T(8,128)(2,1)S(1)} %add_convert_fusion.1), channel_id=1, source_target_pairs={{0,2},{1,7},{2,4},{3,1},{4,6},{5,3},{6,0},{7,5},{8,10},{9,15},{10,... | collective-permute-start | bytes 1179656 | tf_op jit(solution)/shard_map/ppermute | solution.py:456
